TPU v7x, 256 devices: a whole 4x4x8 slice. The times are simulated.
256 devices in a mesh: dp: 4 (over x_hi, core), ctx: 16 (over z, x_lo), tensor: 4 (over y).
Axes of the slice: x: 4 (x_hi: 2, x_lo: 2; x = x_hi * 2 + x_lo), y: 4, z: 8, core: 2. Of those that a mesh axis runs over, the one named last changes fastest.
Arguments:
- query_latent: bfloat16 [4, 8192, 1536], P('dp', 'ctx'), may hold values from -6 to 6
- shared_latent: bfloat16 [4, 8192, 512], P('dp', 'ctx'), may hold values from -6 to 6
- rope_keys: bfloat16 [4, 8192, 64], P('dp', 'ctx'), may hold values from -6 to 6
- block_order: int32 [4, 16], replicated, may hold values from 0 to 15, each once within a row
- query_weight: bfloat16 [1536, 12288], P(('dp', 'ctx'), 'tensor'), as said below
- key_weight: bfloat16 [512, 8192], P(('dp', 'ctx'), 'tensor'), may hold values from -0.25 to 0.25
- value_weight: bfloat16 [512, 8192], P(('dp', 'ctx'), 'tensor'), may hold values from -0.25 to 0.25
Outputs:
- attended: bfloat16 [4, 8192, 8192], P('dp', 'ctx', 'tensor')
- logit_max: float32 [64], P('tensor')
- clipped_query_weight: bfloat16 [1536, 12288], P(('dp', 'ctx'), 'tensor')
- clipped_key_weight: bfloat16 [512, 8192], P(('dp', 'ctx'), 'tensor')
Inputs may be any that keep to these rules, and one draw needn't show every extreme that they name: `block_order`: each row is a permutation: every block of a sequence is held by exactly one ctx index. `query_weight`: entries of each head's columns have a head-dependent spread.
All inputs are finite; a program needn't handle non-finite values.
Results may differ from a plain program's by a relative error of at most 0.012.
The roundings to bfloat16 on the way count: a program that leaves them out, or rounds other values in their place, can miss the bound.
Values may be sent and summed in bfloat16 or wider, within the bound.
No kernel may reach another device: no remote copies, remote signals or barrier semaphores. Data moves between devices by JAX's collectives and lax.ppermute only.
A program may use at most 128 MiB of HBM per device.

v0:
```python
import math

import jax
import jax.numpy as jnp
from jax import lax
from jax.sharding import PartitionSpec as P

QK_NOPE = 128
QK_ROPE = 64
V_DIM = 128
TAU = 100


def passed_along(block, axis, distance):
    devices = range(lax.axis_size(axis))
    route = [((i - distance) % len(devices), i) for i in devices]
    return lax.ppermute(block, axis, route)


def head_attend(query_head, key_head, rope_block, value_head, allowed):
    logit_scale = 1.0 / math.sqrt(QK_NOPE + QK_ROPE)
    plain = jnp.dot(query_head[:, :QK_NOPE], key_head.T, preferred_element_type=jnp.float32)
    rotated = jnp.dot(query_head[:, QK_NOPE:], rope_block.T, preferred_element_type=jnp.float32)
    logits = (plain + rotated) * logit_scale
    masked = jnp.where(allowed, logits, -jnp.inf)
    head_peak = jnp.max(masked)
    row_peak = jnp.max(masked, axis=1, keepdims=True)
    expos = jnp.exp(masked - row_peak)
    probabilities = (expos / jnp.sum(expos, axis=1, keepdims=True)).astype(jnp.bfloat16)
    result = jnp.dot(probabilities, value_head, preferred_element_type=jnp.float32).astype(
        jnp.bfloat16
    )
    return (result, head_peak)


def local(
    query_latent, shared_latent, rope_keys, block_order, query_weight, key_weight, value_weight
):
    head_width = QK_NOPE + QK_ROPE
    tokens_here = query_latent.shape[1]
    heads_here = key_weight.shape[1] // QK_NOPE
    query_rows = query_latent[0]
    query = jnp.dot(
        query_rows,
        lax.all_gather(query_weight, ("dp", "ctx"), axis=0, tiled=True),
        preferred_element_type=jnp.float32,
    ).astype(jnp.bfloat16)
    full_key, full_value = (
        lax.all_gather(key_weight, ("dp", "ctx"), axis=0, tiled=True),
        lax.all_gather(value_weight, ("dp", "ctx"), axis=0, tiled=True),
    )
    latent_own = shared_latent[0]
    rope_own = rope_keys[0]
    key_own = jnp.dot(latent_own, full_key, preferred_element_type=jnp.float32).astype(jnp.bfloat16)
    value_own = jnp.dot(latent_own, full_value, preferred_element_type=jnp.float32).astype(
        jnp.bfloat16
    )
    key_prev, value_prev, rope_prev = passed_along((key_own, value_own, rope_own), "ctx", 1)
    position = lax.axis_index("ctx")
    cycle_size = lax.axis_size("ctx")
    before = (position - 1 + cycle_size) % cycle_size
    order_row = block_order[lax.axis_index("dp")]
    offsets = jnp.arange(tokens_here, dtype=jnp.int32)
    query_place = order_row[position] * tokens_here + offsets
    key_place = jnp.concatenate([query_place, order_row[before] * tokens_here + offsets])
    allowed = key_place[None, :] <= query_place[:, None]
    keys = jnp.concatenate([key_own, key_prev], axis=0)
    values = jnp.concatenate([value_own, value_prev], axis=0)
    rope_block = jnp.concatenate([rope_own, rope_prev], axis=0)

    def per_head(head):
        query_head = lax.dynamic_slice_in_dim(query, head * head_width, head_width, 1)
        key_head = lax.dynamic_slice_in_dim(keys, head * QK_NOPE, QK_NOPE, 1)
        value_head = lax.dynamic_slice_in_dim(values, head * V_DIM, V_DIM, 1)
        return head_attend(query_head, key_head, rope_block, value_head, allowed)

    results, head_peaks = lax.map(per_head, jnp.arange(heads_here, dtype=jnp.int32))
    attended = jnp.transpose(results, (1, 0, 2)).reshape(tokens_here, heads_here * V_DIM)
    logit_max = lax.pmax(head_peaks, ("dp", "ctx"))
    clip_factor = TAU / jnp.maximum(logit_max, TAU)
    root_factor = jnp.sqrt(clip_factor)
    column_factor = jnp.concatenate(
        [
            jnp.broadcast_to(root_factor[:, None], (heads_here, QK_NOPE)),
            jnp.broadcast_to(clip_factor[:, None], (heads_here, QK_ROPE)),
        ],
        axis=1,
    )
    query_rows_here = query_weight.shape[0]
    key_rows_here = key_weight.shape[0]
    clipped_query_weight = (
        (
            query_weight.astype(jnp.float32).reshape(query_rows_here, heads_here, head_width)
            * column_factor[None]
        )
        .reshape(query_rows_here, heads_here * head_width)
        .astype(jnp.bfloat16)
    )
    clipped_key_weight = (
        (
            key_weight.astype(jnp.float32).reshape(key_rows_here, heads_here, QK_NOPE)
            * root_factor[None, :, None]
        )
        .reshape(key_rows_here, heads_here * QK_NOPE)
        .astype(jnp.bfloat16)
    )
    return (attended[None], logit_max, clipped_query_weight, clipped_key_weight)


def solution(mesh):
    return jax.shard_map(
        local,
        mesh=mesh,
        in_specs=(
            P("dp", "ctx", None),
            P("dp", "ctx", None),
            P("dp", "ctx", None),
            P(),
            P(("dp", "ctx"), "tensor"),
            P(("dp", "ctx"), "tensor"),
            P(("dp", "ctx"), "tensor"),
        ),
        out_specs=(
            P("dp", "ctx", "tensor"),
            P("tensor"),
            P(("dp", "ctx"), "tensor"),
            P(("dp", "ctx"), "tensor"),
        ),
        check_vma=False,
    )
```

profile of v0, /device:TPU:1, one launch (start us, length us, event | category | flops | bytes accessed | tf_op | source)
XLA Modules:
  0.0 945.1 jit_solution(2174399467706417599)
XLA Ops:
  9.4 186.4 %all-gather.6.cloned.1.call-done = bf16[512,2048]{1,0:T(8,128)(2,1)} async-done(((bf16[8,2048]{1,0:T(8,128)(2,1)}), bf16[512,2048]{1,0:T(8,128)(2,1)}) %all-gather.6.cloned.1.call-update) | async-done | bytes 2097168 | tf_op jit(solution)/shard_map/all_gather | solution.py:49
  195.8 4.3 convolution_convert_fusion.3
  201.2 209.8 %all-gather.8.cloned.1.call-done = bf16[512,2048]{1,0:T(8,128)(2,1)} async-done(((bf16[8,2048]{1,0:T(8,128)(2,1)}), bf16[512,2048]{1,0:T(8,128)(2,1)}) %all-gather.8.cloned.1.call-update) | async-done | bytes 2097168 | tf_op jit(solution)/shard_map/all_gather | solution.py:50
  411.0 4.2 convolution_convert_fusion.2
  415.4 3.4 collective-permute-start.1
  420.7 47.3 %collective-permute-done.1 = bf16[512,64]{1,0:T(8,128)(2,1)S(1)} collective-permute-done((bf16[512,64]{1,0:T(8,128)(2,1)S(1)}, bf16[512,64]{1,0:T(8,128)(2,1)S(1)}, u32[]{:S(2)}, u32[]{:S(2)}) %collective-permute-start.1) | collective-permute-done | bytes 65568 | tf_op jit(solution)/shard_map/ppermute | solution.py:17
  468.1 5.0 pad_maximum_fusion
  473.1 4.8 pad_maximum_fusion.1
  477.9 161.6 %all-gather.4.cloned.1.call-done = bf16[1536,3072]{1,0:T(8,128)(2,1)} async-done(((bf16[24,3072]{1,0:T(8,128)(2,1)}), bf16[1536,3072]{1,0:T(8,128)(2,1)}) %all-gather.4.cloned.1.call-update) | async-done | bytes 9437200 | tf_op jit(solution)/shard_map/all_gather | solution.py:45
  639.5 10.1 %convolution_convert_fusion.1 = bf16[512,3072]{1,0:T(8,128)(2,1)} fusion(bf16[1536,3072]{1,0:T(8,128)(2,1)} %all-gather.4.cloned.1.call-done, bf16[1,512,1536]{2,1,0:T(8,128)(2,1)S(1)} %copy-done), kind=kOutput, calls=%fused_computation.17 | convolution fusion | flops 4833411072 | bytes 14155776 | tf_op jit(solution)/shard_map/dot_general | solution.py:43
  649.6 145.7 %while.13 = (s32[]{:T(128)}, bf16[16,512,128]{2,1,0:T(8,128)(2,1)}, f32[16]{0:T(128)S(1)}, s32[16]{0:T(128)S(1)}, bf16[512,3072]{1,0:T(8,128)(2,1)}, /*index=5*/...) while((s32[]{:T(128)}, bf16[16,512,128]{2,1,0:T(8,128)(2,1)}, ...), condition=%wide.region_4.5_spmd.clone, body=%wide.region_0.4_spmd.clone.sunk | while | flops 341376000 | bytes 11551037 | solution.py:77
  664.9 2.2 fusion.40
  683.1 2.2 fusion.40
  692.2 2.2 fusion.40
  710.4 2.2 fusion.40
  719.5 2.2 fusion.40
  737.8 2.2 fusion.40
  746.9 2.2 fusion.40
  765.1 2.2 fusion.40
  774.2 2.2 fusion.40
  792.4 2.2 fusion.40
  795.3 133.2 %pmax.7 = f32[16]{0:T(128)S(1)} all-reduce(f32[16]{0:T(128)S(1)} %get-tuple-element.53), channel_id=1, replica_groups=mesh['dp'=4,'ctx'=16,'tensor'=4] {'dp','ctx'}, use_global_device_ids=true, to_apply=%region_5.6 | all-reduce | flops 16 | bytes 128 | tf_op jit(solution)/shard_map/pmax | solution.py:79
  928.5 4.3 copy.12
  932.8 4.2 broadcast_in_dim_reshape.3
  (126 shorter events, 108.9 us)
Async XLA Ops:
  7.2 632.4 %copy-start = (bf16[1,512,1536]{2,1,0:T(8,128)(2,1)S(1)}, bf16[1,512,1536]{2,1,0:T(8,128)(2,1)}, u32[]{:S(2)}) copy-start(bf16[1,512,1536]{2,1,0:T(8,128)(2,1)} %param.9) | copy-start | bytes 4718596
  7.2 188.6 %all-gather.6.cloned.1.call-start = ((), (), s32[]{:S(2)}) async-start(), calls=%async_computation.1 | async-start | bytes 2129920 | tf_op jit(solution)/shard_map/all_gather | solution.py:49
  7.9 403.1 %all-gather.8.cloned.1.call-start = ((), (), s32[]{:S(2)}) async-start(), calls=%async_computation.2 | async-start | bytes 2129920 | tf_op jit(solution)/shard_map/all_gather | solution.py:50
  8.7 630.9 %all-gather.4.cloned.1.call-start = ((), (), s32[]{:S(2)}) async-start(), calls=%async_computation | async-start | bytes 9584640 | tf_op jit(solution)/shard_map/all_gather | solution.py:45
  9.4 401.7 %copy-start.5 = (bf16[1,512,512]{2,1,0:T(8,128)(2,1)S(1)}, bf16[1,512,512]{2,1,0:T(8,128)(2,1)}, u32[]{:S(2)}) copy-start(bf16[1,512,512]{2,1,0:T(8,128)(2,1)} %param.10) | copy-start | bytes 1572868
  200.1 215.1 %copy-start.3 = (bf16[1,512,64]{1,2,0:T(8,128)(2,1)S(1)}, bf16[1,512,64]{1,2,0:T(8,128)(2,1)}, u32[]{:S(2)}) copy-start(bf16[1,512,64]{1,2,0:T(8,128)(2,1)} %param.11) | copy-start | bytes 196612
  200.1 218.7 %copy-start.4 = (s32[4,16]{1,0:T(4,128)S(1)}, s32[4,16]{1,0:T(4,128)}, u32[]{:S(2)}) copy-start(s32[4,16]{1,0:T(4,128)} %param.12) | copy-start | bytes 772
  200.1 268.0 %collective-permute-start = (bf16[512,2048]{1,0:T(8,128)(2,1)}, bf16[512,2048]{1,0:T(8,128)(2,1)}, u32[]{:S(2)}, u32[]{:S(2)}) collective-permute-start(bf16[512,2048]{1,0:T(8,128)(2,1)} %convolution_convert_fusion.3), channel_id=1, source_target_pairs={{60,0},{0,4},{4,8},{8,12},{12,16},{16,20},{20,24},{24,28},{28,32},... | collective-permute-start | bytes 6291464 | tf_op jit(solution)/shard_map/ppermute | solution.py:17
  415.2 57.9 %collective-permute-start.2 = (bf16[512,2048]{1,0:T(8,128)(2,1)}, bf16[512,2048]{1,0:T(8,128)(2,1)}, u32[]{:S(2)}, u32[]{:S(2)}) collective-permute-start(bf16[512,2048]{1,0:T(8,128)(2,1)} %convolution_convert_fusion.2), channel_id=1, source_target_pairs={{60,0},{0,4},{4,8},{8,12},{12,16},{16,20},{20,24},{24,28},{28,32},... | collective-permute-start | bytes 6291464 | tf_op jit(solution)/shard_map/ppermute | solution.py:17
  415.4 52.7 %collective-permute-start.1 = (bf16[512,64]{1,0:T(8,128)(2,1)S(1)}, bf16[512,64]{1,0:T(8,128)(2,1)S(1)}, u32[]{:S(2)}, u32[]{:S(2)}) collective-permute-start(bf16[512,64]{1,0:T(8,128)(2,1)S(1)} %bitcast.35), channel_id=1, source_target_pairs={{60,0},{0,4},{4,8},{8,12},{12,16},{16,20},{20,24},{24,28},{28,32},... | collective-permute-start | bytes 196616 | tf_op jit(solution)/shard_map/ppermute | solution.py:17
  928.5 8.5 copy-start.6
  932.8 4.5 copy-start.2
  932.8 5.1 copy-start.1
Sparse Core Ops, SparseCore 0:
  9.8 185.8 all-gather.5
  197.6 213.4 all-gather.7
  412.9 226.6 all-gather.3
where the time goes:
time: 950 us; the launch traced here: 945 us
  waiting for transfers between devices  607 us (64%)
  blocking collectives  133 us (14%)
  matrix products  103 us (11%)
  local copies, waits for them, and re-layouts  30.9 us (3%)
  other arithmetic  30.3 us (3%)
  loops' own time  21 us (2%)
  between operations  15.1 us (2%)
    all_gather x1, waiting for transfers between devices, local(): lax.all_gather(value_weight, ('dp', 'ctx'), axis=0, tiled=True)  210 us
    all_gather x1, waiting for transfers between devices, local(): lax.all_gather(key_weight, ('dp', 'ctx'), axis=0, tiled=True)  186 us
    all_gather x1, waiting for transfers between devices, local(): lax.all_gather(query_weight, ('dp', 'ctx'), axis=0, tiled=True)  162 us
    pmax x1, blocking collectives, local(): logit_max = lax.pmax(head_peaks, ('dp', 'ctx'))  133 us
    ppermute x3, waiting for transfers between devices, passed_along(): return lax.ppermute(block, axis, route)  47.3 us
    dot_general x16, matrix products, head_attend(): jnp.dot(probabilities, value_head, preferred_element_type=jnp.float32)  34.4 us
    dot_general x16, matrix products, head_attend(): jnp.dot(query_head[:, QK_NOPE:], rope_block.T, preferred_element_type=jnp...  25.5 us
    dot_general x16, matrix products, head_attend(): jnp.dot(query_head[:, :QK_NOPE], key_head.T, preferred_element_type=jnp.f...  24.3 us
  transfers between devices with their start and end apart: 6, of which 4 were waited for; matrix products, arithmetic and copies ran while one was open for 2% of the time, Pallas kernels for 0%

commit v1 on v0

v1 whole, which is shorter than its diff:
```python
import functools
import math

import jax
import jax.numpy as jnp
from jax import lax
from jax.experimental import pallas as pl
from jax.experimental.pallas import tpu as pltpu
from jax.sharding import Mesh
from jax.sharding import PartitionSpec as P

QK_NOPE = 128
QK_ROPE = 64
V_DIM = 128
TAU = 100
HEAD = QK_NOPE + QK_ROPE
SCALE = 1.0 / math.sqrt(HEAD)
SCALE2 = SCALE * math.log2(math.e)
FAR = 1e30

GROUP = ("xh", "core", "z", "xl")
GATHER = ("z", "xh", "xl", "core")
TOK = 512
PAIR = 2


def dot_f32(a, b):
    return jnp.dot(a, b, preferred_element_type=jnp.float32)


def dot_t(a, b):
    return lax.dot_general(a, b, (((1,), (1,)), ((), ())), preferred_element_type=jnp.float32)


def attend_kernel(seen_ref, x_ref, lat_ref, rope_ref, q0_ref, q1_ref, q2_ref, k_ref, v_ref, out_ref, peak_ref):
    half = TOK // 2
    query = dot_f32(x_ref[0], q0_ref[...]) + dot_f32(x_ref[1], q1_ref[...]) + dot_f32(x_ref[2], q2_ref[...])
    query = query.astype(jnp.bfloat16)
    keys = dot_f32(lat_ref[...], k_ref[...]).astype(jnp.bfloat16)
    values = dot_f32(lat_ref[...], v_ref[...]).astype(jnp.bfloat16)
    rope = rope_ref[...]
    seen = seen_ref[0] > 0
    row = lax.broadcasted_iota(jnp.int32, (half, half), 0)
    col = lax.broadcasted_iota(jnp.int32, (half, half), 1)
    diagonal = col <= row
    for head in range(PAIR):
        q_head = query[:, head * HEAD : (head + 1) * HEAD]
        key_head = jnp.concatenate([keys[:, head * QK_NOPE : (head + 1) * QK_NOPE], rope], axis=1)
        value_head = values[:, head * V_DIM : (head + 1) * V_DIM]
        head_peak = None
        for part in range(2):
            q_part = q_head[part * half : (part + 1) * half]
            spans = []
            if part == 1:
                spans.append((0, half, "all"))
            spans.append((part * half, half, "diag"))
            spans.append((TOK, TOK, "prev"))
            logits = []
            for start, size, kind in spans:
                s = dot_t(q_part, key_head[start : start + size])
                if kind == "diag":
                    s = jnp.where(diagonal, s, -jnp.inf)
                logits.append(s)
            peak = functools.reduce(jnp.maximum, [jnp.max(s, axis=1, keepdims=True) for s in logits[:-1]])
            prev_peak = jnp.max(logits[-1], axis=1, keepdims=True)
            peak = jnp.where(seen, jnp.maximum(peak, prev_peak), peak)
            here = jnp.max(peak)
            head_peak = here if head_peak is None else jnp.maximum(head_peak, here)
            shift = peak * SCALE2
            shift_prev = jnp.where(seen, shift, FAR)
            expos = [
                jnp.exp2(s * SCALE2 - (shift_prev if kind == "prev" else shift))
                for s, (_, _, kind) in zip(logits, spans)
            ]
            total = functools.reduce(jnp.add, [jnp.sum(e, axis=1, keepdims=True) for e in expos])
            inverse = 1.0 / total
            result = None
            for e, (start, size, _) in zip(expos, spans):
                term = dot_f32((e * inverse).astype(jnp.bfloat16), value_head[start : start + size])
                result = term if result is None else result + term
            out_ref[part * half : (part + 1) * half, head * V_DIM : (head + 1) * V_DIM] = result.astype(jnp.bfloat16)
        peak_ref[0, head : head + 1, :] = jnp.broadcast_to(head_peak * SCALE, (1, 128))


def attend(seen, x, latents, rope, gathered, heads):
    pairs = heads // PAIR
    q_cols = heads * HEAD
    wide_q, wide_k = PAIR * HEAD, PAIR * QK_NOPE
    rows = gathered.shape[0]

    def weight(offset, width):
        return pl.BlockSpec((rows, width), lambda p: (0, offset // width + p))

    whole = lambda a: pl.BlockSpec(a.shape, lambda p: (0,) * a.ndim)
    k_at, v_at = 3 * q_cols, 3 * q_cols + heads * QK_NOPE
    return pl.pallas_call(
        attend_kernel,
        grid=(pairs,),
        in_specs=[
            pl.BlockSpec(memory_space=pltpu.SMEM),
            whole(x),
            whole(latents),
            whole(rope),
            weight(0, wide_q),
            weight(q_cols, wide_q),
            weight(2 * q_cols, wide_q),
            weight(k_at, wide_k),
            weight(v_at, wide_k),
        ],
        out_specs=[
            pl.BlockSpec((TOK, PAIR * V_DIM), lambda p: (0, p)),
            pl.BlockSpec((1, 8, 128), lambda p: (p, 0, 0)),
        ],
        out_shape=[
            jax.ShapeDtypeStruct((TOK, heads * V_DIM), jnp.bfloat16),
            jax.ShapeDtypeStruct((pairs, 8, 128), jnp.float32),
        ],
        compiler_params=pltpu.CompilerParams(vmem_limit_bytes=48 * 1024 * 1024),
        cost_estimate=pl.CostEstimate(flops=14_000_000_000, bytes_accessed=20_000_000, transcendentals=8_000_000),
    )(seen, x, latents, rope, gathered, gathered, gathered, gathered, gathered)


def local(query_latent, shared_latent, rope_keys, block_order, query_weight, key_weight, value_weight):
    heads = key_weight.shape[1] // QK_NOPE
    packed = jnp.concatenate(
        [query_weight[0:8], query_weight[8:16], query_weight[16:24], key_weight, value_weight], axis=1
    )
    gathered = lax.all_gather(packed, GATHER, axis=0, tiled=True)

    cycle = lax.axis_size("z") * lax.axis_size("xl")
    route = [(i, (i + 1) % cycle) for i in range(cycle)]
    lat_prev = lax.ppermute(shared_latent[0], ("z", "xl"), route)
    rope_prev = lax.ppermute(rope_keys[0], ("z", "xl"), route)
    latents = jnp.concatenate([shared_latent[0], lat_prev], axis=0)
    latents = latents.reshape(2 * TOK, 2, 2, 8, 2, 8).transpose(0, 3, 1, 4, 2, 5).reshape(2 * TOK, 512)
    rope = jnp.concatenate([rope_keys[0], rope_prev], axis=0)
    x = query_latent[0].reshape(TOK, 2, 2, 8, 2, 3, 8).transpose(5, 0, 3, 1, 4, 2, 6).reshape(3, TOK, 512)

    position = lax.axis_index(("z", "xl"))
    order_row = block_order[lax.axis_index(("xh", "core"))]
    seen = (order_row[(position - 1 + cycle) % cycle] < order_row[position]).astype(jnp.int32).reshape(1)

    attended, peaks = attend(seen, x, latents, rope, gathered, heads)
    peaks = peaks[:, :PAIR, 0].reshape(1, heads)
    everyone = math.prod(lax.axis_size(a) for a in GROUP)
    shared = lax.all_to_all(jnp.broadcast_to(peaks[None], (everyone, 1, heads)), GATHER, 0, 0)
    logit_max = jnp.max(shared, axis=(0, 1))
    clip = TAU / jnp.maximum(logit_max, TAU)
    root = jnp.sqrt(clip)
    factors = jnp.concatenate(
        [jnp.broadcast_to(root[:, None], (heads, QK_NOPE)), jnp.broadcast_to(clip[:, None], (heads, QK_ROPE))], axis=1
    ).reshape(1, heads * HEAD)
    clipped_q = (query_weight.astype(jnp.float32) * factors).astype(jnp.bfloat16)
    clipped_k = (key_weight.astype(jnp.float32) * jnp.repeat(root, QK_NOPE)[None]).astype(jnp.bfloat16)
    return (attended[None], logit_max, clipped_q, clipped_k)


def solution(mesh):
    fine = Mesh(mesh.devices.reshape(2, 2, 8, 2, 4), ("xh", "core", "z", "xl", "tensor"))
    dp, ctx = ("xh", "core"), ("z", "xl")
    return jax.shard_map(
        local,
        mesh=fine,
        in_specs=(
            P(dp, ctx, None),
            P(dp, ctx, None),
            P(dp, ctx, None),
            P(),
            P(GROUP, "tensor"),
            P(GROUP, "tensor"),
            P(GROUP, "tensor"),
        ),
        out_specs=(
            P(dp, ctx, "tensor"),
            P("tensor"),
            P(GROUP, "tensor"),
            P(GROUP, "tensor"),
        ),
        check_vma=False,
    )
```

time: 950 us -> 169 us (0.18)
  waiting for transfers between devices: 607 us -> 81.8 us
  blocking collectives: 133 us -> 15.4 us
  matrix products: 103 us -> 0 us
  Pallas kernels: 0 us -> 35.4 us
  other arithmetic: 30.3 us -> 2.79 us
  loops' own time: 21 us -> 0 us
  local copies, waits for them, and re-layouts: 30.9 us -> 13.8 us
    all_gather x3 -> x1, waiting for transfers between devices: 558 us -> 67.6 us  [local(): gathered = lax.all_gather(packed, GATHER, axis=0, tiled=True)]
    pmax x1 -> x0, blocking collectives: 133 us -> none  [local(): logit_max = lax.pmax(head_peaks, ('dp', 'ctx'))]
    dot_general x51 -> x0, matrix products: 103 us -> none  [the longest x16 34.4 us: head_attend(): jnp.dot(probabilities, value_head, preferred_element_type=jnp.float32)]
    pallas_call x0 -> x1, Pallas kernels: none -> 35.4 us  [attend(): pl.pallas_call(attend_kernel, grid=(pairs,), in_specs=[pl.BlockSpec(memor...]
    ppermute x3 -> x2, waiting for transfers between devices: 47.3 us -> 14.2 us  [the longest x1 14.2 us: local(): rope_prev = lax.ppermute(rope_keys[0], ('z', 'xl'), route)]
    another operation x1 -> x0, loops' own time: 21 us -> none  [local(): lax.map(per_head, jnp.arange(heads_here, dtype=jnp.int32))]
    reduce_max x16 -> x1, other arithmetic: 19.1 us -> 0.08 us  [local(): logit_max = jnp.max(shared, axis=(0, 1))]
    all_to_all x0 -> x1, blocking collectives: none -> 15.4 us  [local(): lax.all_to_all(jnp.broadcast_to(peaks[None], (everyone, 1, heads)), GATHE...]
  transfers between devices with their start and end apart: 6 -> 3, of which waited for: 4 -> 2; matrix products, arithmetic and copies ran while one was open for 2% -> 6% of each run, Pallas kernels for 0% -> 0%
where the time goes in v1:
time: 169 us; the launch traced here: 168 us
  waiting for transfers between devices  81.8 us (48%)
  Pallas kernels  35.4 us (21%)
  blocking collectives  15.4 us (9%)
  between operations  15.4 us (9%)
  local copies, waits for them, and re-layouts  13.8 us (8%)
  starting transfers between devices  3.76 us (2%)
  other arithmetic  2.79 us (2%)
    all_gather x1, waiting for transfers between devices, local(): gathered = lax.all_gather(packed, GATHER, axis=0, tiled=True)  67.6 us
    pallas_call x1, Pallas kernels, attend(): pl.pallas_call(attend_kernel, grid=(pairs,), in_specs=[pl.BlockSpec(memor...  35.4 us
    all_to_all x1, blocking collectives, local(): lax.all_to_all(jnp.broadcast_to(peaks[None], (everyone, 1, heads)), GATHE...  15.4 us
    ppermute x1, waiting for transfers between devices, local(): rope_prev = lax.ppermute(rope_keys[0], ('z', 'xl'), route)  14.2 us
    unnamed x17, local copies, waits for them, and re-layouts  7.68 us
  transfers between devices with their start and end apart: 3, of which 2 were waited for; matrix products, arithmetic and copies ran while one was open for 6% of the time, Pallas kernels for 0%

profile of v1, /device:TPU:1, one launch (start us, length us, event | category | flops | bytes accessed | tf_op | source)
XLA Modules:
  0.0 168.3 jit_solution(8640942860170068246)
XLA Ops:
  7.2 0.9 slice_dynamic-update-slice_fusion.2
  8.1 0.8 slice_dynamic-update-slice_fusion.1
  8.9 0.8 slice_dynamic-update-slice_fusion
  9.7 0.8 constant_dynamic-update-slice_fusion.1
  10.5 0.8 constant_dynamic-update-slice_fusion
  11.3 0.7 copy-done.2
  12.0 2.0 %copy.33 = bf16[1,512,512]{1,2,0:T(8,128)(2,1)} copy(bf16[1,512,512]{2,1,0:T(8,128)(2,1)} %param.8) | data formatting | bytes 1048576 | tf_op args[1]
  14.0 2.0 %collective-permute-start = (bf16[512,512]{0,1:T(8,128)(2,1)}, bf16[512,512]{0,1:T(8,128)(2,1)}, u32[]{:S(2)}, u32[]{:S(2)}) collective-permute-start(bf16[512,512]{0,1:T(8,128)(2,1)} %bitcast.5), channel_id=1, source_target_pairs={{0,4},{4,8},{8,12},{12,16},{16,20},{20,24},{24,28},{28,32},{32,36}... | collective-permute-start | bytes 1572872 | tf_op jit(solution)/shard_map/ppermute | solution.py:132
  16.1 1.0 copy.36
  17.0 1.7 %collective-permute-start.1 = (bf16[512,64]{1,0:T(8,128)(2,1)S(1)}, bf16[512,64]{1,0:T(8,128)(2,1)S(1)}, u32[]{:S(2)}, u32[]{:S(2)}) collective-permute-start(bf16[512,64]{1,0:T(8,128)(2,1)S(1)} %bitcast.18), channel_id=1, source_target_pairs={{0,4},{4,8},{8,12},{12,16},{16,20},{20,24},{24,28},{28,32},{32,36}... | collective-permute-start | bytes 196616 | tf_op jit(solution)/shard_map/ppermute | solution.py:133
  18.7 1.3 fusion.1
  21.4 0.7 copy.31
  22.1 0.2 copy.32
  22.3 0.7 copy.37.x_ref
  23.0 14.2 %collective-permute-done.1 = bf16[512,64]{1,0:T(8,128)(2,1)S(1)} collective-permute-done((bf16[512,64]{1,0:T(8,128)(2,1)S(1)}, bf16[512,64]{1,0:T(8,128)(2,1)S(1)}, u32[]{:S(2)}, u32[]{:S(2)}) %collective-permute-start.1) | collective-permute-done | bytes 65568 | tf_op jit(solution)/shard_map/ppermute | solution.py:133
  37.2 1.3 maximum_bitcast_fusion
  38.6 1.1 copy.35
  39.6 1.5 copy.38.lat_ref
  41.1 67.6 %all-gather.2.cloned.1.call-done.q0_ref.q1_ref.q2_ref.k_ref.v_ref = bf16[512,13312]{1,0:T(8,128)(2,1)} async-done(((bf16[8,13312]{1,0:T(8,128)(2,1)}), bf16[512,13312]{1,0:T(8,128)(2,1)}) %all-gather.2.cloned.1.call-update) | async-done | bytes 13631504 | tf_op jit(solution)/shard_map/all_gather | solution.py:128
  108.8 35.4 %shard_map.102 = (bf16[512,2048]{1,0:T(8,128)(2,1)}, f32[8,8,128]{2,1,0:T(8,128)S(1)}) custom-call(s32[1]{0:T(128)} %bitcast.seen_ref, bf16[3,512,512]{2,1,0:T(8,128)(2,1)S(1)} %copy.37.x_ref, bf16[1024,512]{1,0:T(8,128)(2,1)S(1)} %copy.38.lat_ref, bf16[1024,64]{1,0:T(8,128)(2,1)S(1)} %pad_maximum_fusion.rope_ref, ...), custom_call_target="tpu_custom_call" | custom-call | flops 14000000000 | bytes 20000000 | tf_op jit(solution)/shard_map/pallas_call | solution.py:96
  144.4 15.4 %all_to_all.5 = f32[64,1,16]{2,1,0:T(1,128)S(1)} all-to-all(f32[64,1,16]{2,1,0:T(1,128)S(1)} %broadcast_in_dim.12), channel_id=1, replica_groups=mesh['xh'=2,'core'=2,'z'=8,'xl'=2,'tensor'=4] {'z','xh','xl','core'}, dimensions={0} | all-to-all | bytes 8192 | tf_op jit(solution)/shard_map/all_to_all | solution.py:146
  159.7 0.1 reduce_max.9
  160.1 0.6 multiply_convert_fusion.1
  160.8 0.7 multiply_convert_fusion
  (22 shorter events, 0.6 us)
Async XLA Ops:
  7.2 14.2 %copy-start = (bf16[1,512,1536]{2,1,0:T(8,128)(2,1)S(1)}, bf16[1,512,1536]{2,1,0:T(8,128)(2,1)}, u32[]{:S(2)}) copy-start(bf16[1,512,1536]{2,1,0:T(8,128)(2,1)} %param.7) | copy-start | bytes 4718596
  7.2 101.6 %all-gather.2.cloned.1.call-start = ((), (), s32[]{:S(2)}) async-start(), calls=%async_computation.1 | async-start | bytes 13844480 | tf_op jit(solution)/shard_map/all_gather | solution.py:128
  11.3 0.7 copy-start.2
  14.0 23.2 %collective-permute-start = (bf16[512,512]{0,1:T(8,128)(2,1)}, bf16[512,512]{0,1:T(8,128)(2,1)}, u32[]{:S(2)}, u32[]{:S(2)}) collective-permute-start(bf16[512,512]{0,1:T(8,128)(2,1)} %bitcast.5), channel_id=1, source_target_pairs={{0,4},{4,8},{8,12},{12,16},{16,20},{20,24},{24,28},{28,32},{32,36}... | collective-permute-start | bytes 1572872 | tf_op jit(solution)/shard_map/ppermute | solution.py:132
  17.0 20.2 %collective-permute-start.1 = (bf16[512,64]{1,0:T(8,128)(2,1)S(1)}, bf16[512,64]{1,0:T(8,128)(2,1)S(1)}, u32[]{:S(2)}, u32[]{:S(2)}) collective-permute-start(bf16[512,64]{1,0:T(8,128)(2,1)S(1)} %bitcast.18), channel_id=1, source_target_pairs={{0,4},{4,8},{8,12},{12,16},{16,20},{20,24},{24,28},{28,32},{32,36}... | collective-permute-start | bytes 196616 | tf_op jit(solution)/shard_map/ppermute | solution.py:133
  108.8 51.4 %copy-start.3 = (bf16[8,2048]{1,0:T(8,128)(2,1)S(1)}, bf16[8,2048]{1,0:T(8,128)(2,1)}, u32[]{:S(2)}) copy-start(bf16[8,2048]{1,0:T(8,128)(2,1)} %param.12) | copy-start | bytes 98308
  108.8 52.0 %copy-start.1 = (bf16[24,3072]{1,0:T(8,128)(2,1)S(1)}, bf16[24,3072]{1,0:T(8,128)(2,1)}, u32[]{:S(2)}) copy-start(bf16[24,3072]{1,0:T(8,128)(2,1)} %param.11) | copy-start | bytes 442372
  159.8 1.6 copy-start.4
Sparse Core Ops, SparseCore 0:
  12.1 96.6 all-gather.1

commit v2 on v1

v2 whole, which is shorter than its diff:
```python
import functools
import math

import jax
import jax.numpy as jnp
from jax import lax
from jax.experimental import pallas as pl
from jax.experimental.pallas import tpu as pltpu
from jax.sharding import Mesh
from jax.sharding import PartitionSpec as P

QK_NOPE = 128
QK_ROPE = 64
V_DIM = 128
TAU = 100
HEAD = QK_NOPE + QK_ROPE
SCALE = 1.0 / math.sqrt(HEAD)
SCALE2 = SCALE * math.log2(math.e)
FAR = 1e30

GROUP = ("xh", "core", "z", "xl")
X = ("xh", "xl")
TOK = 512
HALF = TOK // 2
PAIR = 2
Q_WIDE = PAIR * HEAD
K_WIDE = PAIR * QK_NOPE
WIDE = 3 * Q_WIDE + 2 * K_WIDE
PAIRS = 8
PAIRS_A = 5
PAIRS_B = PAIRS - PAIRS_A
MIB = 1024 * 1024
VMEM = pl.BlockSpec(memory_space=pltpu.VMEM)
SMEM = pl.BlockSpec(memory_space=pltpu.SMEM)
ANY = pl.BlockSpec(memory_space=pl.ANY)


def dot_f32(a, b):
    return jnp.dot(a, b, preferred_element_type=jnp.float32)


def dot_t(a, b):
    return lax.dot_general(a, b, (((1,), (1,)), ((), ())), preferred_element_type=jnp.float32)


def attend_pair(seen, x_ref, lat_ref, rope_ref, weight, out_ref, peak_ref):
    query = functools.reduce(jnp.add, [dot_f32(x_ref[j], weight(j * Q_WIDE, Q_WIDE)) for j in range(3)])
    query = query.astype(jnp.bfloat16)
    keys = dot_f32(lat_ref[...], weight(3 * Q_WIDE, K_WIDE)).astype(jnp.bfloat16)
    values = dot_f32(lat_ref[...], weight(3 * Q_WIDE + K_WIDE, K_WIDE)).astype(jnp.bfloat16)
    rope = rope_ref[...]
    row = lax.broadcasted_iota(jnp.int32, (HALF, HALF), 0)
    col = lax.broadcasted_iota(jnp.int32, (HALF, HALF), 1)
    diagonal = col <= row
    ones = (lax.broadcasted_iota(jnp.int32, (2 * TOK, V_DIM), 1) == 0).astype(jnp.bfloat16)

    def logits_of(head, part):
        q_part = query[part * HALF : (part + 1) * HALF, head * HEAD : (head + 1) * HEAD]
        key_head = jnp.concatenate([keys[:, head * QK_NOPE : (head + 1) * QK_NOPE], rope], axis=1)
        spans = [(0, HALF, "all")] if part == 1 else []
        spans += [(part * HALF, HALF, "diag"), (TOK, TOK, "prev")]
        logits = []
        for start, size, kind in spans:
            s = dot_t(q_part, key_head[start : start + size])
            logits.append(jnp.where(diagonal, s, -jnp.inf) if kind == "diag" else s)
        return spans, logits

    def finish(head, part, spans, logits):
        value_head = jnp.concatenate([values[:, head * V_DIM : (head + 1) * V_DIM], ones], axis=1)
        peak = functools.reduce(jnp.maximum, [jnp.max(s, axis=1, keepdims=True) for s in logits[:-1]])
        prev_peak = jnp.max(logits[-1], axis=1, keepdims=True)
        peak = jnp.where(seen, jnp.maximum(peak, prev_peak), peak)
        shift = peak * SCALE2
        shift_prev = jnp.where(seen, shift, FAR)
        result = None
        for s, (start, size, kind) in zip(logits, spans):
            expo = jnp.exp2(s * SCALE2 - (shift_prev if kind == "prev" else shift))
            term = dot_f32(expo.astype(jnp.bfloat16), value_head[start : start + size])
            result = term if result is None else result + term
        result = result[:, :V_DIM] * (1.0 / result[:, V_DIM : V_DIM + 1])
        out_ref[part * HALF : (part + 1) * HALF, head * V_DIM : (head + 1) * V_DIM] = result.astype(jnp.bfloat16)
        return jnp.max(peak)

    order = [(head, part) for head in range(PAIR) for part in range(2)]
    peaks = []
    current = logits_of(*order[0])
    for i, (head, part) in enumerate(order):
        following = logits_of(*order[i + 1]) if i + 1 < len(order) else None
        peaks.append(finish(head, part, *current))
        current = following
    for head in range(PAIR):
        top = jnp.maximum(peaks[2 * head], peaks[2 * head + 1]) * SCALE
        peak_ref[0, head : head + 1, :] = jnp.broadcast_to(top, (1, 128))


def late_kernel(place_ref, x_ref, lat_ref, rope_ref, w_ref, _out, _peaks, out_ref, peak_ref):
    attend_pair(
        place_ref[0] > 0, x_ref, lat_ref, rope_ref, lambda start, width: w_ref[:, start : start + width], out_ref, peak_ref
    )


def early_kernel(place_ref, x_ref, lat_ref, rope_ref, *rest):
    pieces, (out_ref, peak_ref, w_ref, sems) = rest[:10], rest[10:]
    pair = pl.program_id(0)

    @pl.when(pair == 0)
    def _():
        me, core = place_ref[1], place_ref[2]
        copies = []
        for side in range(2):
            owner = core if side == 0 else 1 - core
            own, before, after, far_low, far_high = pieces[5 * side : 5 * side + 5]
            for piece, step, first in ((own, 0, 0), (before, 3, 0), (after, 1, 0), (far_low, 2, 0), (far_high, 2, 32)):
                block = lax.rem(me + step, 4) * 2 + owner
                rows = pl.ds(pl.multiple_of(block * 64 + first, 32), piece.shape[0])
                copies.append(pltpu.make_async_copy(piece, w_ref.at[rows, :], sems.at[len(copies)]))
        for copy in copies:
            copy.start()
        for copy in copies:
            copy.wait()

    def weight(start, width):
        return w_ref[:, pl.ds(pl.multiple_of(pair * WIDE + start, 128), width)]

    attend_pair(place_ref[0] > 0, x_ref, lat_ref, rope_ref, weight, out_ref, peak_ref)


def whole(array):
    return pl.BlockSpec(array.shape, lambda p: (0,) * array.ndim)


def cost(pairs):
    return pl.CostEstimate(flops=1_800_000_000 * pairs, bytes_accessed=2_000_000 * pairs, transcendentals=1_000_000 * pairs)


def outputs(first):
    specs = [
        pl.BlockSpec((TOK, PAIR * V_DIM), lambda p: (0, first + p)),
        pl.BlockSpec((1, 8, 128), lambda p: (first + p, 0, 0)),
    ]
    shapes = [
        jax.ShapeDtypeStruct((TOK, PAIRS * PAIR * V_DIM), jnp.bfloat16),
        jax.ShapeDtypeStruct((PAIRS, 8, 128), jnp.float32),
    ]
    return specs, shapes


def attend_early(place, x, latents, rope, pieces):
    specs, shapes = outputs(PAIRS_A)
    return pl.pallas_call(
        early_kernel,
        grid=(PAIRS_B,),
        in_specs=[SMEM, whole(x), whole(latents), whole(rope)] + [ANY] * len(pieces),
        out_specs=specs,
        out_shape=shapes,
        scratch_shapes=[
            pltpu.VMEM((TOK, PAIRS_B * WIDE), jnp.bfloat16),
            pltpu.SemaphoreType.DMA((len(pieces),)),
        ],
        compiler_params=pltpu.CompilerParams(vmem_limit_bytes=36 * MIB),
        cost_estimate=cost(PAIRS_B),
        name="early",
    )(place, x, latents, rope, *pieces)


def attend_late(place, x, latents, rope, gathered, out, peaks):
    specs, shapes = outputs(0)
    return pl.pallas_call(
        late_kernel,
        grid=(PAIRS_A,),
        in_specs=[SMEM, whole(x), whole(latents), whole(rope)]
        + [pl.BlockSpec((TOK, WIDE), lambda p: (0, p)), ANY, ANY],
        out_specs=specs,
        out_shape=shapes,
        input_output_aliases={5: 0, 6: 1},
        compiler_params=pltpu.CompilerParams(vmem_limit_bytes=56 * MIB),
        cost_estimate=cost(PAIRS_A),
        name="late",
    )(place, x, latents, rope, gathered, out, peaks)


def pack_kernel(q_ref, k_ref, v_ref, a_ref, b_ref):
    for pair in range(PAIRS):
        ref, at = (a_ref, pair) if pair < PAIRS_A else (b_ref, pair - PAIRS_A)
        at = at * WIDE
        for j in range(3):
            ref[:, at + j * Q_WIDE : at + (j + 1) * Q_WIDE] = q_ref[8 * j : 8 * j + 8, pair * Q_WIDE : (pair + 1) * Q_WIDE]
        at += 3 * Q_WIDE
        ref[:, at : at + K_WIDE] = k_ref[:, pair * K_WIDE : (pair + 1) * K_WIDE]
        ref[:, at + K_WIDE : at + 2 * K_WIDE] = v_ref[:, pair * K_WIDE : (pair + 1) * K_WIDE]


def pack(query_weight, key_weight, value_weight):
    return pl.pallas_call(
        pack_kernel,
        in_specs=[VMEM] * 3,
        out_specs=[VMEM] * 2,
        out_shape=[
            jax.ShapeDtypeStruct((8, PAIRS_A * WIDE), jnp.bfloat16),
            jax.ShapeDtypeStruct((8, PAIRS_B * WIDE), jnp.bfloat16),
        ],
        name="pack",
    )(query_weight, key_weight, value_weight)


def order_kernel(offsets, me_ref, *refs):
    pieces, out_ref, stack = refs[:-2], refs[-2], refs[-1]
    count = len(pieces)
    for offset, piece in zip(offsets, pieces):
        stack[offset % count] = piece[...]
    me = me_ref[0]
    for slot in range(0, count, 2):
        two = [stack[lax.rem(slot + i + count - me, count)] for i in range(2)]
        out_ref[8 * slot : 8 * slot + 16, :] = jnp.concatenate(two, axis=0)


def in_order(me, offsets, pieces):
    rows, columns = pieces[0].shape
    count = len(pieces)
    return pl.pallas_call(
        functools.partial(order_kernel, offsets),
        in_specs=[SMEM] + [VMEM] * count,
        out_specs=VMEM,
        out_shape=jax.ShapeDtypeStruct((rows * count, columns), jnp.bfloat16),
        scratch_shapes=[pltpu.VMEM((count, rows, columns), jnp.bfloat16)],
        name="in_order",
    )(me.reshape(1), *pieces)


def moved(block, axes, distance):
    count = lax.axis_size(axes)
    return lax.ppermute(block, axes, [(i, (i + distance) % count) for i in range(count)])


def local(query_latent, shared_latent, rope_keys, block_order, query_weight, key_weight, value_weight):
    heads = key_weight.shape[1] // QK_NOPE
    me_x = lax.axis_index(X).astype(jnp.int32)
    me_z = lax.axis_index("z").astype(jnp.int32)
    me_core = lax.axis_index("core").astype(jnp.int32)
    cycle = lax.axis_size(("z", "xl"))
    position = lax.axis_index(("z", "xl"))
    order_row = block_order[lax.axis_index(("xh", "core"))]
    seen = (order_row[(position - 1 + cycle) % cycle] < order_row[position]).astype(jnp.int32)
    place = jnp.stack([seen, me_x, me_core])

    packed_a, packed_b = pack(query_weight, key_weight, value_weight)

    along_x = [packed_a, moved(packed_a, X, 1), moved(packed_a, X, -1), moved(packed_a, X, 2)]
    shard_a = in_order(me_x, (0, -1, 1, 2), along_x)
    gathered_a = lax.all_gather(shard_a, ("z", "core"), axis=0, tiled=True)

    along_z, offsets = [packed_b], [0]
    up = down = packed_b
    for step in range(1, 5):
        up = moved(up, "z", 1)
        along_z.append(up)
        offsets.append(-step)
        if step < 4:
            down = moved(down, "z", -1)
            along_z.append(down)
            offsets.append(step)
    own = in_order(me_z, tuple(offsets), along_z)
    before, after = moved(own, X, 1), moved(own, X, -1)
    far_low, far_high = moved(before[:32], X, 1), moved(after[32:], X, -1)
    mine = [own, before, after, far_low, far_high]
    pieces = mine + [moved(piece, "core", 1) for piece in mine]

    lat_prev = moved(shared_latent[0], ("z", "xl"), 1)
    rope_prev = moved(rope_keys[0], ("z", "xl"), 1)
    latents = jnp.concatenate([shared_latent[0], lat_prev], axis=0).reshape(2 * TOK, 2, 2, 8, 2, 8)
    rope = jnp.concatenate([rope_keys[0], rope_prev], axis=0)
    x = query_latent[0].reshape(TOK, 2, 2, 8, 2, 3, 8)
    lat_a = latents.transpose(0, 3, 2, 1, 4, 5).reshape(2 * TOK, 512)
    lat_b = latents.transpose(0, 1, 4, 2, 3, 5).reshape(2 * TOK, 512)
    x_a = x.transpose(5, 0, 3, 2, 1, 4, 6).reshape(3, TOK, 512)
    x_b = x.transpose(5, 0, 1, 4, 2, 3, 6).reshape(3, TOK, 512)

    attended, peaks = attend_early(place, x_b, lat_b, rope, pieces)
    attended, peaks = attend_late(place, x_a, lat_a, rope, gathered_a, attended, peaks)

    peaks = peaks[:, :PAIR, 0].reshape(1, heads)
    everyone = lax.axis_size(GROUP)
    shared = lax.all_to_all(jnp.broadcast_to(peaks[None], (everyone, 1, heads)), GROUP, 0, 0)
    logit_max = jnp.max(shared, axis=(0, 1))
    clip = TAU / jnp.maximum(logit_max, TAU)
    root = jnp.sqrt(clip)
    factors = jnp.concatenate(
        [jnp.broadcast_to(root[:, None], (heads, QK_NOPE)), jnp.broadcast_to(clip[:, None], (heads, QK_ROPE))], axis=1
    ).reshape(1, heads * HEAD)
    clipped_q = (query_weight.astype(jnp.float32) * factors).astype(jnp.bfloat16)
    clipped_k = (key_weight.astype(jnp.float32) * jnp.repeat(root, QK_NOPE)[None]).astype(jnp.bfloat16)
    return (attended[None], logit_max, clipped_q, clipped_k)


def solution(mesh):
    fine = Mesh(mesh.devices.reshape(2, 2, 8, 2, 4), ("xh", "core", "z", "xl", "tensor"))
    dp, ctx = ("xh", "core"), ("z", "xl")
    return jax.shard_map(
        local,
        mesh=fine,
        in_specs=(
            P(dp, ctx, None),
            P(dp, ctx, None),
            P(dp, ctx, None),
            P(),
            P(GROUP, "tensor"),
            P(GROUP, "tensor"),
            P(GROUP, "tensor"),
        ),
        out_specs=(
            P(dp, ctx, "tensor"),
            P("tensor"),
            P(GROUP, "tensor"),
            P(GROUP, "tensor"),
        ),
        check_vma=False,
    )
```

time: 169 us -> 177 us (1.047)
  waiting for transfers between devices: 81.8 us -> 25.7 us
  starting transfers between devices: 3.76 us -> 51.6 us
  local copies, waits for them, and re-layouts: 13.8 us -> 23.7 us
  blocking collectives: 15.4 us -> 18.4 us
  Pallas kernels: 35.4 us -> 37.2 us
    all_gather x1, waiting for transfers between devices: 67.6 us -> 0.01 us  [local(): gathered_a = lax.all_gather(shard_a, ('z', 'core'), axis=0, tiled=True)]
    ppermute x2 -> x21, starting transfers between devices: 3.73 us -> 51.6 us  [moved(): lax.ppermute(block, axes, [(i, (i + distance) % count) for i in range(cou...]
    ppermute x2 -> x21, waiting for transfers between devices: 14.2 us -> 25.6 us  [moved(): lax.ppermute(block, axes, [(i, (i + distance) % count) for i in range(cou...]
    transpose x2 -> x4, local copies, waits for them, and re-layouts: 1.29 us -> 7.63 us  [the longest x1 2.74 us: local(): x_a = x.transpose(5, 0, 3, 2, 1, 4, 6).reshape(3, TOK, 512)]
    reshape x2 -> x4, local copies, waits for them, and re-layouts: 2.2 us -> 8.08 us  [the longest x1 2.6 us: local(): x_a = x.transpose(5, 0, 3, 2, 1, 4, 6).reshape(3, TOK, 512)]
    unnamed x17 -> x47, local copies, waits for them, and re-layouts: 7.68 us -> 4.14 us
    all_to_all x1, blocking collectives: 15.4 us -> 18.4 us  [local(): lax.all_to_all(jnp.broadcast_to(peaks[None], (everyone, 1, heads)), GROUP...]
    slice x0 -> x2, local copies, waits for them, and re-layouts: none -> 1.99 us  [local(): far_low, far_high = (moved(before[:32], X, 1), moved(after[32:], X, -1))]
  transfers between devices with their start and end apart: 3 -> 22, of which waited for: 2 -> 9; matrix products, arithmetic and copies ran while one was open for 6% -> 13% of each run, Pallas kernels for 0% -> 9%
where the time goes in v2:
time: 177 us; the launch traced here: 176 us
  starting transfers between devices  51.6 us (29%)
  Pallas kernels  37.2 us (21%)
  waiting for transfers between devices  25.7 us (15%)
  local copies, waits for them, and re-layouts  23.7 us (13%)
  blocking collectives  18.4 us (10%)
  between operations  15.6 us (9%)
  other arithmetic  3.81 us (2%)
    ppermute x21, starting transfers between devices, moved(): lax.ppermute(block, axes, [(i, (i + distance) % count) for i in range(cou...  51.6 us
    ppermute x21, waiting for transfers between devices, moved(): lax.ppermute(block, axes, [(i, (i + distance) % count) for i in range(cou...  25.6 us
    all_to_all x1, blocking collectives, local(): lax.all_to_all(jnp.broadcast_to(peaks[None], (everyone, 1, heads)), GROUP...  18.4 us
    pallas_call x1, Pallas kernels, attend_late(): pl.pallas_call(late_kernel, grid=(PAIRS_A,), in_specs=[SMEM, whole(x), wh...  18.3 us
    pallas_call x1, Pallas kernels, attend_early(): pl.pallas_call(early_kernel, grid=(PAIRS_B,), in_specs=[SMEM, whole(x), w...  13 us
    pallas_call x2, Pallas kernels, in_order(): pl.pallas_call(functools.partial(order_kernel, offsets), in_specs=[SMEM]...  4.21 us
    unnamed x47, local copies, waits for them, and re-layouts  4.14 us
  transfers between devices with their start and end apart: 22, of which 9 were waited for; matrix products, arithmetic and copies ran while one was open for 13% of the time, Pallas kernels for 9%

profile of v2, /device:TPU:1, one launch (start us, length us, event | category | flops | bytes accessed | tf_op | source)
XLA Modules:
  0.0 176.0 jit_solution(17736162679480672113)
XLA Ops:
  8.9 2.0 %collective-permute-start.2 = (bf16[8,8320]{1,0:T(8,128)(2,1)}, bf16[8,8320]{1,0:T(8,128)(2,1)S(1)}, u32[]{:S(2)}, u32[]{:S(2)}) collective-permute-start(bf16[8,8320]{1,0:T(8,128)(2,1)} %get-tuple-element.10.refs_0_), channel_id=1, source_target_pairs={{0,4},{4,128},{128,132},{132,0},{1,5},{5,129},{129,133},{133,1},{2... | collective-permute-start | bytes 399368 | tf_op jit(solution)/shard_map/ppermute | solution.py:232
  12.2 1.7 collective-permute-start.4
  15.0 3.9 %collective-permute-done.4.refs_3_ = bf16[8,8320]{1,0:T(8,128)(2,1)S(1)} collective-permute-done((bf16[8,8320]{1,0:T(8,128)(2,1)}, bf16[8,8320]{1,0:T(8,128)(2,1)S(1)}, u32[]{:S(2)}, u32[]{:S(2)}) %collective-permute-start.4) | collective-permute-done | bytes 133152 | tf_op jit(solution)/shard_map/ppermute | solution.py:232
  19.6 2.1 %in_order.2 = bf16[32,8320]{1,0:T(8,128)(2,1)} custom-call(s32[1]{0:T(128)} %bitcast.1.me_ref, bf16[8,8320]{1,0:T(8,128)(2,1)} %get-tuple-element.10.refs_0_, bf16[8,8320]{1,0:T(8,128)(2,1)} %copy-done.8, bf16[8,8320]{1,0:T(8,128)(2,1)} %copy-done.9, bf16[8,8320]{1,0:T(8,128)(2,1)} %copy-done.10), custom_call_target="tpu_custom_call" | custom-call | tf_op jit(solution)/shard_map/in_order/pallas_call | solution.py:220
  21.7 2.4 %collective-permute-start.5 = (bf16[8,4992]{1,0:T(8,128)(2,1)}, bf16[8,4992]{1,0:T(8,128)(2,1)S(1)}, u32[]{:S(2)}, u32[]{:S(2)}) collective-permute-start(bf16[8,4992]{1,0:T(8,128)(2,1)} %get-tuple-element.11.refs_0_), channel_id=1, source_target_pairs={{0,8},{8,16},{16,24},{24,32},{32,40},{40,48},{48,56},{56,0},{1,9},... | collective-permute-start | bytes 239624 | tf_op jit(solution)/shard_map/ppermute | solution.py:232
  24.1 4.0 %collective-permute-start.6 = (bf16[8,4992]{1,0:T(8,128)(2,1)}, bf16[8,4992]{1,0:T(8,128)(2,1)S(1)}, u32[]{:S(2)}, u32[]{:S(2)}) collective-permute-start(bf16[8,4992]{1,0:T(8,128)(2,1)} %get-tuple-element.11.refs_0_), channel_id=1, source_target_pairs={{0,56},{8,0},{16,8},{24,16},{32,24},{40,32},{48,40},{56,48},{1,57}... | collective-permute-start | bytes 239624 | tf_op jit(solution)/shard_map/ppermute | solution.py:232
  28.1 1.9 %collective-permute-done.5.refs_1_ = bf16[8,4992]{1,0:T(8,128)(2,1)S(1)} collective-permute-done((bf16[8,4992]{1,0:T(8,128)(2,1)}, bf16[8,4992]{1,0:T(8,128)(2,1)S(1)}, u32[]{:S(2)}, u32[]{:S(2)}) %collective-permute-start.5) | collective-permute-done | bytes 79904 | tf_op jit(solution)/shard_map/ppermute | solution.py:232
  30.1 2.7 %collective-permute-start.8 = (bf16[8,4992]{1,0:T(8,128)(2,1)S(1)}, bf16[8,4992]{1,0:T(8,128)(2,1)S(1)}, u32[]{:S(2)}, u32[]{:S(2)}) collective-permute-start(bf16[8,4992]{1,0:T(8,128)(2,1)S(1)} %collective-permute-done.6.refs_2_), channel_id=1, source_target_pairs={{0,56},{8,0},{16,8},{24,16},{32,24},{40,32},{48,40},{56,48},{1,57}... | collective-permute-start | bytes 239624 | tf_op jit(solution)/shard_map/ppermute | solution.py:232
  34.6 2.7 %collective-permute-start.10 = (bf16[8,4992]{1,0:T(8,128)(2,1)S(1)}, bf16[8,4992]{1,0:T(8,128)(2,1)S(1)}, u32[]{:S(2)}, u32[]{:S(2)}) collective-permute-start(bf16[8,4992]{1,0:T(8,128)(2,1)S(1)} %collective-permute-done.8.refs_4_), channel_id=1, source_target_pairs={{0,56},{8,0},{16,8},{24,16},{32,24},{40,32},{48,40},{56,48},{1,57}... | collective-permute-start | bytes 239624 | tf_op jit(solution)/shard_map/ppermute | solution.py:232
  40.3 5.9 %collective-permute-done.11.refs_7_ = bf16[8,4992]{1,0:T(8,128)(2,1)S(1)} collective-permute-done((bf16[8,4992]{1,0:T(8,128)(2,1)S(1)}, bf16[8,4992]{1,0:T(8,128)(2,1)S(1)}, u32[]{:S(2)}, u32[]{:S(2)}) %collective-permute-start.11) | collective-permute-done | bytes 79904 | tf_op jit(solution)/shard_map/ppermute | solution.py:232
  46.8 2.2 %in_order.3.rest_0_ = bf16[64,4992]{1,0:T(8,128)(2,1)} custom-call(s32[1]{0:T(128)} %bitcast.16.me_ref, bf16[8,4992]{1,0:T(8,128)(2,1)} %get-tuple-element.11.refs_0_, bf16[8,4992]{1,0:T(8,128)(2,1)} %copy-done.12, bf16[8,4992]{1,0:T(8,128)(2,1)} %copy-done.13, bf16[8,4992]{1,0:T(8,128)(2,1)} %copy-done.14, bf16[8,4992]{1,0:T(8,128)(2,1)} %copy-done.15, ...), custom_call_target="tpu_custom_call" | custom-call | tf_op jit(solution)/shard_map/in_order/pallas_call | solution.py:220
  49.0 2.7 %collective-permute-start.13 = (bf16[64,4992]{1,0:T(8,128)(2,1)}, bf16[64,4992]{1,0:T(8,128)(2,1)}, u32[]{:S(2)}, u32[]{:S(2)}) collective-permute-start(bf16[64,4992]{1,0:T(8,128)(2,1)} %in_order.3.rest_0_), channel_id=1, source_target_pairs={{0,132},{4,0},{128,4},{132,128},{1,133},{5,1},{129,5},{133,129},{2... | collective-permute-start | bytes 1916936 | tf_op jit(solution)/shard_map/ppermute | solution.py:232
  52.0 8.1 %collective-permute-done.12.rest_1_ = bf16[64,4992]{1,0:T(8,128)(2,1)} collective-permute-done((bf16[64,4992]{1,0:T(8,128)(2,1)}, bf16[64,4992]{1,0:T(8,128)(2,1)}, u32[]{:S(2)}, u32[]{:S(2)}) %collective-permute-start.12) | collective-permute-done | bytes 639008 | tf_op jit(solution)/shard_map/ppermute | solution.py:232
  62.2 2.9 %collective-permute-start.15 = (bf16[32,4992]{1,0:T(8,128)(2,1)S(1)}, bf16[32,4992]{1,0:T(8,128)(2,1)}, u32[]{:S(2)}, u32[]{:S(2)}) collective-permute-start(bf16[32,4992]{1,0:T(8,128)(2,1)S(1)} %slice.13), channel_id=1, source_target_pairs={{0,132},{4,0},{128,4},{132,128},{1,133},{5,1},{129,5},{133,129},{2... | collective-permute-start | bytes 958472 | tf_op jit(solution)/shard_map/ppermute | solution.py:232
  65.3 18.3 %collective-permute-start.16 = (bf16[64,4992]{1,0:T(8,128)(2,1)S(1)}, bf16[64,4992]{1,0:T(8,128)(2,1)}, u32[]{:S(2)}, u32[]{:S(2)}) collective-permute-start(bf16[64,4992]{1,0:T(8,128)(2,1)S(1)} %copy-done), channel_id=1, source_target_pairs={{0,64},{64,0},{1,65},{65,1},{2,66},{66,2},{3,67},{67,3},{4,68},{68... | collective-permute-start | bytes 1916936 | tf_op jit(solution)/shard_map/ppermute | solution.py:232
  83.6 9.7 %collective-permute-start.17 = (bf16[64,4992]{1,0:T(8,128)(2,1)}, bf16[64,4992]{1,0:T(8,128)(2,1)}, u32[]{:S(2)}, u32[]{:S(2)}) collective-permute-start(bf16[64,4992]{1,0:T(8,128)(2,1)} %collective-permute-done.12.rest_1_), channel_id=1, source_target_pairs={{0,64},{64,0},{1,65},{65,1},{2,66},{66,2},{3,67},{67,3},{4,68},{68... | collective-permute-start | bytes 1916936 | tf_op jit(solution)/shard_map/ppermute | solution.py:232
  101.2 2.7 %copy.44 = bf16[3,512,8,2,2,2,8]{1,6,5,4,3,2,0:T(8,128)(2,1)} copy(bf16[3,512,8,2,2,2,8]{1,6,0,5,2,3,4:T(8,128)(2,1)} %bitcast.25) | data formatting | bytes 3145728 | tf_op jit(solution)/shard_map/transpose | solution.py:275
  103.9 2.6 %copy.53.x_ref = bf16[3,512,512]{2,1,0:T(8,128)(2,1)} copy(bf16[3,512,512]{1,2,0:T(8,128)(2,1)} %bitcast.26) | data formatting | bytes 3145728 | tf_op jit(solution)/shard_map/reshape | solution.py:275
  106.6 2.3 %fusion = (bf16[1024,2,2,2,8,8]{0,5,2,4,3,1:T(8,128)(2,1)S(1)}, bf16[1024,8,2,2,2,8]{0,5,4,1,2,3:T(8,128)(2,1)}) fusion(bf16[512,2,2,8,2,8]{0,5,4,3,2,1:T(8,128)(2,1)} %bitcast.34, bf16[512,2,2,8,2,8]{0,5,4,3,2,1:T(8,128)(2,1)S(1)} %bitcast.31), kind=kLoop, calls=%fused_computation.1 | loop fusion | flops 2097152 | bytes 3145728 | tf_op jit(solution)/shard_map/transpose | solution.py:274
  111.4 2.3 %copy.47 = bf16[1024,8,2,2,2,8]{0,5,4,3,2,1:T(8,128)(2,1)} copy(bf16[1024,8,2,2,2,8]{0,5,4,1,2,3:T(8,128)(2,1)} %get-tuple-element.19) | data formatting | bytes 2097152 | tf_op jit(solution)/shard_map/transpose | solution.py:273
  113.8 2.3 %copy.54.lat_ref = bf16[1024,512]{1,0:T(8,128)(2,1)} copy(bf16[1024,512]{0,1:T(8,128)(2,1)} %bitcast.29) | data formatting | bytes 2097152 | tf_op jit(solution)/shard_map/reshape | solution.py:273
  116.1 13.0 %early.1 = (bf16[512,2048]{1,0:T(8,128)(2,1)}, f32[8,8,128]{2,1,0:T(8,128)S(1)}) custom-call(s32[3]{0:T(128)S(1)} %pad_add_fusion.place_ref, bf16[3,512,512]{2,1,0:T(8,128)(2,1)S(1)} %copy.51.x_ref, bf16[1024,512]{1,0:T(8,128)(2,1)S(1)} %copy.52.lat_ref, bf16[1024,64]{1,0:T(8,128)(2,1)S(1)} %pad_maximum_fusion.1.rope_ref, bf16[64,4992]{1,0:T(8,128)(2,1)S(1)} %copy-done, ...), custom_call_target="tpu_custom_call" | custom-call | flops 5400000000 | bytes 6000000 | tf_op jit(solution)/shard_map/early/pallas_call | solution.py:150
  129.7 18.3 %late.1 = (bf16[512,2048]{1,0:T(8,128)(2,1)}, f32[8,8,128]{2,1,0:T(8,128)}) custom-call(s32[3]{0:T(128)} %copy-done.3, bf16[3,512,512]{2,1,0:T(8,128)(2,1)} %copy.53.x_ref, bf16[1024,512]{1,0:T(8,128)(2,1)} %copy.54.lat_ref, bf16[1024,64]{1,0:T(8,128)(2,1)} %copy-done.1, ...), custom_call_target="tpu_custom_call", output_to_operand_aliasing={{0}: (5, {}), {1}: (6, {})} | custom-call | flops 8999999488 | bytes 10000000 | tf_op jit(solution)/shard_map/late/pallas_call | solution.py:168
  149.0 18.4 %all_to_all.5 = f32[64,1,16]{2,1,0:T(1,128)S(1)} all-to-all(f32[64,1,16]{2,1,0:T(1,128)S(1)} %broadcast_in_dim.12), channel_id=1, replica_groups=mesh['xh'=2,'core'=2,'z'=8,'xl'=2,'tensor'=4] {'xh','core','z','xl'}, dimensions={0} | all-to-all | bytes 8192 | tf_op jit(solution)/shard_map/all_to_all | solution.py:283
  (100 shorter events, 25.0 us)
Async XLA Ops:
  7.2 44.5 %copy-start.6 = (bf16[1,512,512]{2,1,0:T(8,128)(2,1)S(1)}, bf16[1,512,512]{2,1,0:T(8,128)(2,1)}, u32[]{:S(2)}) copy-start(bf16[1,512,512]{2,1,0:T(8,128)(2,1)} %param.8) | copy-start | bytes 1572868
  7.2 122.6 %all-gather.2.cloned.1.call-start = ((), (), s32[]{:S(2)}) async-start(), calls=%async_computation.1 | async-start | bytes 9052160 | tf_op jit(solution)/shard_map/all_gather | solution.py:250
  8.9 5.9 %collective-permute-start.2 = (bf16[8,8320]{1,0:T(8,128)(2,1)}, bf16[8,8320]{1,0:T(8,128)(2,1)S(1)}, u32[]{:S(2)}, u32[]{:S(2)}) collective-permute-start(bf16[8,8320]{1,0:T(8,128)(2,1)} %get-tuple-element.10.refs_0_), channel_id=1, source_target_pairs={{0,4},{4,128},{128,132},{132,0},{1,5},{5,129},{129,133},{133,1},{2... | collective-permute-start | bytes 399368 | tf_op jit(solution)/shard_map/ppermute | solution.py:232
  10.9 4.1 %collective-permute-start.3 = (bf16[8,8320]{1,0:T(8,128)(2,1)}, bf16[8,8320]{1,0:T(8,128)(2,1)S(1)}, u32[]{:S(2)}, u32[]{:S(2)}) collective-permute-start(bf16[8,8320]{1,0:T(8,128)(2,1)} %get-tuple-element.10.refs_0_), channel_id=1, source_target_pairs={{0,132},{4,0},{128,4},{132,128},{1,133},{5,1},{129,5},{133,129},{2... | collective-permute-start | bytes 399368 | tf_op jit(solution)/shard_map/ppermute | solution.py:232
  12.2 6.7 %collective-permute-start.4 = (bf16[8,8320]{1,0:T(8,128)(2,1)}, bf16[8,8320]{1,0:T(8,128)(2,1)S(1)}, u32[]{:S(2)}, u32[]{:S(2)}) collective-permute-start(bf16[8,8320]{1,0:T(8,128)(2,1)} %get-tuple-element.10.refs_0_), channel_id=1, source_target_pairs={{0,128},{4,132},{128,0},{132,4},{1,129},{5,133},{129,1},{133,5},{2... | collective-permute-start | bytes 399368 | tf_op jit(solution)/shard_map/ppermute | solution.py:232
  21.7 71.8 %copy-start.21 = (s32[4,16]{1,0:T(4,128)S(1)}, s32[4,16]{1,0:T(4,128)}, u32[]{:S(2)}) copy-start(s32[4,16]{1,0:T(4,128)} %param.10) | copy-start | bytes 772
  21.7 8.4 %collective-permute-start.5 = (bf16[8,4992]{1,0:T(8,128)(2,1)}, bf16[8,4992]{1,0:T(8,128)(2,1)S(1)}, u32[]{:S(2)}, u32[]{:S(2)}) collective-permute-start(bf16[8,4992]{1,0:T(8,128)(2,1)} %get-tuple-element.11.refs_0_), channel_id=1, source_target_pairs={{0,8},{8,16},{16,24},{24,32},{32,40},{40,48},{48,56},{56,0},{1,9},... | collective-permute-start | bytes 239624 | tf_op jit(solution)/shard_map/ppermute | solution.py:232
  24.1 6.0 %collective-permute-start.6 = (bf16[8,4992]{1,0:T(8,128)(2,1)}, bf16[8,4992]{1,0:T(8,128)(2,1)S(1)}, u32[]{:S(2)}, u32[]{:S(2)}) collective-permute-start(bf16[8,4992]{1,0:T(8,128)(2,1)} %get-tuple-element.11.refs_0_), channel_id=1, source_target_pairs={{0,56},{8,0},{16,8},{24,16},{32,24},{40,32},{48,40},{56,48},{1,57}... | collective-permute-start | bytes 239624 | tf_op jit(solution)/shard_map/ppermute | solution.py:232
  30.1 4.5 %collective-permute-start.7 = (bf16[8,4992]{1,0:T(8,128)(2,1)S(1)}, bf16[8,4992]{1,0:T(8,128)(2,1)S(1)}, u32[]{:S(2)}, u32[]{:S(2)}) collective-permute-start(bf16[8,4992]{1,0:T(8,128)(2,1)S(1)} %collective-permute-done.5.refs_1_), channel_id=1, source_target_pairs={{0,8},{8,16},{16,24},{24,32},{32,40},{40,48},{48,56},{56,0},{1,9},... | collective-permute-start | bytes 239624 | tf_op jit(solution)/shard_map/ppermute | solution.py:232
  30.1 4.5 %collective-permute-start.8 = (bf16[8,4992]{1,0:T(8,128)(2,1)S(1)}, bf16[8,4992]{1,0:T(8,128)(2,1)S(1)}, u32[]{:S(2)}, u32[]{:S(2)}) collective-permute-start(bf16[8,4992]{1,0:T(8,128)(2,1)S(1)} %collective-permute-done.6.refs_2_), channel_id=1, source_target_pairs={{0,56},{8,0},{16,8},{24,16},{32,24},{40,32},{48,40},{56,48},{1,57}... | collective-permute-start | bytes 239624 | tf_op jit(solution)/shard_map/ppermute | solution.py:232
  34.6 4.5 %collective-permute-start.9 = (bf16[8,4992]{1,0:T(8,128)(2,1)S(1)}, bf16[8,4992]{1,0:T(8,128)(2,1)S(1)}, u32[]{:S(2)}, u32[]{:S(2)}) collective-permute-start(bf16[8,4992]{1,0:T(8,128)(2,1)S(1)} %collective-permute-done.7.refs_3_), channel_id=1, source_target_pairs={{0,8},{8,16},{16,24},{24,32},{32,40},{40,48},{48,56},{56,0},{1,9},... | collective-permute-start | bytes 239624 | tf_op jit(solution)/shard_map/ppermute | solution.py:232
  34.6 5.7 %collective-permute-start.10 = (bf16[8,4992]{1,0:T(8,128)(2,1)S(1)}, bf16[8,4992]{1,0:T(8,128)(2,1)S(1)}, u32[]{:S(2)}, u32[]{:S(2)}) collective-permute-start(bf16[8,4992]{1,0:T(8,128)(2,1)S(1)} %collective-permute-done.8.refs_4_), channel_id=1, source_target_pairs={{0,56},{8,0},{16,8},{24,16},{32,24},{40,32},{48,40},{56,48},{1,57}... | collective-permute-start | bytes 239624 | tf_op jit(solution)/shard_map/ppermute | solution.py:232
  39.0 7.2 %collective-permute-start.11 = (bf16[8,4992]{1,0:T(8,128)(2,1)S(1)}, bf16[8,4992]{1,0:T(8,128)(2,1)S(1)}, u32[]{:S(2)}, u32[]{:S(2)}) collective-permute-start(bf16[8,4992]{1,0:T(8,128)(2,1)S(1)} %collective-permute-done.9.refs_5_), channel_id=1, source_target_pairs={{0,8},{8,16},{16,24},{24,32},{32,40},{40,48},{48,56},{56,0},{1,9},... | collective-permute-start | bytes 239624 | tf_op jit(solution)/shard_map/ppermute | solution.py:232
  49.0 11.1 %collective-permute-start.12 = (bf16[64,4992]{1,0:T(8,128)(2,1)}, bf16[64,4992]{1,0:T(8,128)(2,1)}, u32[]{:S(2)}, u32[]{:S(2)}) collective-permute-start(bf16[64,4992]{1,0:T(8,128)(2,1)} %in_order.3.rest_0_), channel_id=1, source_target_pairs={{0,4},{4,128},{128,132},{132,0},{1,5},{5,129},{129,133},{133,1},{2... | collective-permute-start | bytes 1916936 | tf_op jit(solution)/shard_map/ppermute | solution.py:232
  49.0 12.2 %collective-permute-start.13 = (bf16[64,4992]{1,0:T(8,128)(2,1)}, bf16[64,4992]{1,0:T(8,128)(2,1)}, u32[]{:S(2)}, u32[]{:S(2)}) collective-permute-start(bf16[64,4992]{1,0:T(8,128)(2,1)} %in_order.3.rest_0_), channel_id=1, source_target_pairs={{0,132},{4,0},{128,4},{132,128},{1,133},{5,1},{129,5},{133,129},{2... | collective-permute-start | bytes 1916936 | tf_op jit(solution)/shard_map/ppermute | solution.py:232
  51.9 41.5 %collective-permute-start = (bf16[512,512]{0,1:T(8,128)(2,1)S(1)}, bf16[512,512]{0,1:T(8,128)(2,1)S(1)}, u32[]{:S(2)}, u32[]{:S(2)}) collective-permute-start(bf16[512,512]{0,1:T(8,128)(2,1)S(1)} %bitcast.30), channel_id=1, source_target_pairs={{0,4},{4,8},{8,12},{12,16},{16,20},{20,24},{24,28},{28,32},{32,36}... | collective-permute-start | bytes 1572872 | tf_op jit(solution)/shard_map/ppermute | solution.py:232
  61.1 34.3 %collective-permute-start.14 = (bf16[32,4992]{1,0:T(8,128)(2,1)S(1)}, bf16[32,4992]{1,0:T(8,128)(2,1)}, u32[]{:S(2)}, u32[]{:S(2)}) collective-permute-start(bf16[32,4992]{1,0:T(8,128)(2,1)S(1)} %slice.12), channel_id=1, source_target_pairs={{0,4},{4,128},{128,132},{132,0},{1,5},{5,129},{129,133},{133,1},{2... | collective-permute-start | bytes 958472 | tf_op jit(solution)/shard_map/ppermute | solution.py:232
  62.2 33.7 %collective-permute-start.15 = (bf16[32,4992]{1,0:T(8,128)(2,1)S(1)}, bf16[32,4992]{1,0:T(8,128)(2,1)}, u32[]{:S(2)}, u32[]{:S(2)}) collective-permute-start(bf16[32,4992]{1,0:T(8,128)(2,1)S(1)} %slice.13), channel_id=1, source_target_pairs={{0,132},{4,0},{128,4},{132,128},{1,133},{5,1},{129,5},{133,129},{2... | collective-permute-start | bytes 958472 | tf_op jit(solution)/shard_map/ppermute | solution.py:232
  65.2 18.4 %collective-permute-start.1 = (bf16[512,64]{1,0:T(8,128)(2,1)S(1)}, bf16[512,64]{1,0:T(8,128)(2,1)S(1)}, u32[]{:S(2)}, u32[]{:S(2)}) collective-permute-start(bf16[512,64]{1,0:T(8,128)(2,1)S(1)} %bitcast.32), channel_id=1, source_target_pairs={{0,4},{4,8},{8,12},{12,16},{16,20},{20,24},{24,28},{28,32},{32,36}... | collective-permute-start | bytes 196616 | tf_op jit(solution)/shard_map/ppermute | solution.py:232
  65.3 50.7 %collective-permute-start.16 = (bf16[64,4992]{1,0:T(8,128)(2,1)S(1)}, bf16[64,4992]{1,0:T(8,128)(2,1)}, u32[]{:S(2)}, u32[]{:S(2)}) collective-permute-start(bf16[64,4992]{1,0:T(8,128)(2,1)S(1)} %copy-done), channel_id=1, source_target_pairs={{0,64},{64,0},{1,65},{65,1},{2,66},{66,2},{3,67},{67,3},{4,68},{68... | collective-permute-start | bytes 1916936 | tf_op jit(solution)/shard_map/ppermute | solution.py:232
  83.6 32.4 %collective-permute-start.17 = (bf16[64,4992]{1,0:T(8,128)(2,1)}, bf16[64,4992]{1,0:T(8,128)(2,1)}, u32[]{:S(2)}, u32[]{:S(2)}) collective-permute-start(bf16[64,4992]{1,0:T(8,128)(2,1)} %collective-permute-done.12.rest_1_), channel_id=1, source_target_pairs={{0,64},{64,0},{1,65},{65,1},{2,66},{66,2},{3,67},{67,3},{4,68},{68... | collective-permute-start | bytes 1916936 | tf_op jit(solution)/shard_map/ppermute | solution.py:232
  93.4 22.7 %collective-permute-start.18 = (bf16[64,4992]{1,0:T(8,128)(2,1)}, bf16[64,4992]{1,0:T(8,128)(2,1)}, u32[]{:S(2)}, u32[]{:S(2)}) collective-permute-start(bf16[64,4992]{1,0:T(8,128)(2,1)} %collective-permute-done.13.rest_2_), channel_id=1, source_target_pairs={{0,64},{64,0},{1,65},{65,1},{2,66},{66,2},{3,67},{67,3},{4,68},{68... | collective-permute-start | bytes 1916936 | tf_op jit(solution)/shard_map/ppermute | solution.py:232
  95.4 20.7 %collective-permute-start.19 = (bf16[32,4992]{1,0:T(8,128)(2,1)}, bf16[32,4992]{1,0:T(8,128)(2,1)}, u32[]{:S(2)}, u32[]{:S(2)}) collective-permute-start(bf16[32,4992]{1,0:T(8,128)(2,1)} %collective-permute-done.14.rest_3_), channel_id=1, source_target_pairs={{0,64},{64,0},{1,65},{65,1},{2,66},{66,2},{3,67},{67,3},{4,68},{68... | collective-permute-start | bytes 958472 | tf_op jit(solution)/shard_map/ppermute | solution.py:232
  95.9 20.2 %collective-permute-start.20 = (bf16[32,4992]{1,0:T(8,128)(2,1)}, bf16[32,4992]{1,0:T(8,128)(2,1)}, u32[]{:S(2)}, u32[]{:S(2)}) collective-permute-start(bf16[32,4992]{1,0:T(8,128)(2,1)} %collective-permute-done.15.rest_4_), channel_id=1, source_target_pairs={{0,64},{64,0},{1,65},{65,1},{2,66},{66,2},{3,67},{67,3},{4,68},{68... | collective-permute-start | bytes 958472 | tf_op jit(solution)/shard_map/ppermute | solution.py:232
  (20 other events, 250.7 us)
Sparse Core Ops, SparseCore 0:
  21.8 62.9 all-gather.1

commit v3 on v2

--- a/solution.py
+++ b/solution.py
@@ -204,14 +204,10 @@
 
 
 def order_kernel(offsets, me_ref, *refs):
-    pieces, out_ref, stack = refs[:-2], refs[-2], refs[-1]
+    pieces, out_ref = refs[:-1], refs[-1]
     count = len(pieces)
     for offset, piece in zip(offsets, pieces):
-        stack[offset % count] = piece[...]
-    me = me_ref[0]
-    for slot in range(0, count, 2):
-        two = [stack[lax.rem(slot + i + count - me, count)] for i in range(2)]
-        out_ref[8 * slot : 8 * slot + 16, :] = jnp.concatenate(two, axis=0)
+        out_ref[lax.rem(me_ref[0] + offset % count, count)] = piece[...]
 
 
 def in_order(me, offsets, pieces):
@@ -221,10 +217,89 @@
         functools.partial(order_kernel, offsets),
         in_specs=[SMEM] + [VMEM] * count,
         out_specs=VMEM,
-        out_shape=jax.ShapeDtypeStruct((rows * count, columns), jnp.bfloat16),
-        scratch_shapes=[pltpu.VMEM((count, rows, columns), jnp.bfloat16)],
+        out_shape=jax.ShapeDtypeStruct((count, rows, columns), jnp.bfloat16),
         name="in_order",
-    )(me.reshape(1), *pieces)
+    )(me.reshape(1), *pieces).reshape(count * rows, columns)
+
+
+def one_hot(source, first):
+    at = lax.broadcasted_iota(jnp.int32, (128, source.shape[1]), 0) + first
+    return jnp.where(at == source, 1.0, 0.0).astype(jnp.bfloat16)
+
+
+def picked(rows, tiles, source):
+    left = jnp.concatenate([rows(tile) for tile in tiles], axis=1)
+    right = jnp.concatenate([one_hot(source, tile * 128) for tile in tiles], axis=0)
+    return dot_f32(left, right).astype(jnp.bfloat16)
+
+
+def late_source(c, tile, strip):
+    z, core, xh, xl, r = 2 * tile + ((c >> 6) & 1), (c >> 5) & 1, (c >> 4) & 1, (c >> 3) & 1, c & 7
+    return ((xh * 2 + core) * 16 + z * 2 + xl) * strip + r
+
+
+def early_source(c, tile, strip):
+    core, z, r = (c >> 6) & 1, (c >> 3) & 7, c & 7
+    return ((tile // 2 * 2 + core) * 16 + z * 2 + tile % 2) * strip + r
+
+
+def order_query_kernel(x_ref, late_ref, early_ref):
+    column = lax.broadcasted_iota(jnp.int32, (1, 384), 1)
+    c, j = column & 127, column >> 7
+    rows = lambda tile: x_ref[:, tile * 128 : (tile + 1) * 128]
+    for tile in range(4):
+        low, high = 96 * tile // 128, (96 * tile + 95) // 128
+        near = [3 * block + part for block in range(4) for part in range(low, high + 1)]
+        late = picked(rows, near, late_source(c, tile, 24) + 8 * j)
+        near = [3 * (tile // 2 * 2 + core) + part for core in range(2) for part in range(3)]
+        early = picked(rows, near, early_source(c, tile, 24) + 8 * j)
+        for strip in range(3):
+            late_ref[strip, :, tile * 128 : (tile + 1) * 128] = late[:, strip * 128 : (strip + 1) * 128]
+            early_ref[strip, :, tile * 128 : (tile + 1) * 128] = early[:, strip * 128 : (strip + 1) * 128]
+
+
+def order_query(x):
+    shape = jax.ShapeDtypeStruct((3, TOK, 512), jnp.bfloat16)
+    return pl.pallas_call(
+        order_query_kernel,
+        in_specs=[VMEM],
+        out_specs=[VMEM] * 2,
+        out_shape=[shape, shape],
+        compiler_params=pltpu.CompilerParams(vmem_limit_bytes=24 * MIB),
+        cost_estimate=pl.CostEstimate(flops=2_500_000_000, bytes_accessed=6_000_000, transcendentals=0),
+        name="order_query",
+    )(x)
+
+
+def order_latent_kernel(me_ref, own_ref, own_rope_ref, *refs):
+    pieces, (late_ref, early_ref, rope_ref, prev_ref) = refs[:4], refs[4:]
+    for offset, piece in zip((0, -1, 1, 2), pieces):
+        slot = lax.rem(me_ref[0] + offset % 4, 4)
+        prev_ref[pl.ds(pl.multiple_of(slot * 128, 128), 128), :] = piece[...]
+    rope_ref[:TOK] = own_rope_ref[...]
+    rope_ref[TOK:] = prev_ref[:, 512:]
+    c = lax.broadcasted_iota(jnp.int32, (1, 128), 1)
+    for part, ref in ((0, own_ref), (1, prev_ref)):
+        rows = lambda tile: ref[:, tile * 128 : (tile + 1) * 128]
+        for tile in range(4):
+            at = slice(tile * 128, (tile + 1) * 128)
+            late_ref[part * TOK : (part + 1) * TOK, at] = picked(rows, range(4), late_source(c, tile, 8))
+            near = [tile // 2 * 2, tile // 2 * 2 + 1]
+            early_ref[part * TOK : (part + 1) * TOK, at] = picked(rows, near, early_source(c, tile, 8))
+
+
+def order_latent(me, own, own_rope, pieces):
+    shape = jax.ShapeDtypeStruct((2 * TOK, 512), jnp.bfloat16)
+    return pl.pallas_call(
+        order_latent_kernel,
+        in_specs=[SMEM] + [VMEM] * 6,
+        out_specs=[VMEM] * 3,
+        out_shape=[shape, shape, jax.ShapeDtypeStruct((2 * TOK, QK_ROPE), jnp.bfloat16)],
+        scratch_shapes=[pltpu.VMEM((TOK, 512 + QK_ROPE), jnp.bfloat16)],
+        compiler_params=pltpu.CompilerParams(vmem_limit_bytes=24 * MIB),
+        cost_estimate=pl.CostEstimate(flops=1_000_000_000, bytes_accessed=4_000_000, transcendentals=0),
+        name="order_latent",
+    )(me.reshape(1), own, own_rope, *pieces)
 
 
 def moved(block, axes, distance):
@@ -245,35 +320,35 @@
 
     packed_a, packed_b = pack(query_weight, key_weight, value_weight)
 
+    barrier = lax.optimization_barrier
+    me_t = lax.axis_index("tensor").astype(jnp.int32)
+    quarter = TOK // lax.axis_size("tensor")
+    latent, rope_own = shared_latent[0], rope_keys[0]
+
     along_x = [packed_a, moved(packed_a, X, 1), moved(packed_a, X, -1), moved(packed_a, X, 2)]
     shard_a = in_order(me_x, (0, -1, 1, 2), along_x)
+    mine = jnp.concatenate(
+        [lax.dynamic_slice_in_dim(a, me_t * quarter, quarter, 0) for a in (latent, rope_own)], axis=1
+    )
+    shard_a, mine, packed_b = barrier((shard_a, mine, packed_b))
     gathered_a = lax.all_gather(shard_a, ("z", "core"), axis=0, tiled=True)
 
-    along_z, offsets = [packed_b], [0]
-    up = down = packed_b
-    for step in range(1, 5):
-        up = moved(up, "z", 1)
-        along_z.append(up)
-        offsets.append(-step)
-        if step < 4:
-            down = moved(down, "z", -1)
-            along_z.append(down)
-            offsets.append(step)
-    own = in_order(me_z, tuple(offsets), along_z)
+    up, down = moved(packed_b, "z", 1), moved(packed_b, "z", -1)
+    up2, down2 = moved(packed_b, "z", 2), moved(packed_b, "z", -2)
+    up3, down3, up4 = moved(up, "z", 2), moved(down, "z", -2), moved(up2, "z", 2)
+    own = in_order(me_z, (0, -1, 1, -2, 2, -3, 3, -4), [packed_b, up, down, up2, down2, up3, down3, up4])
+    theirs = moved(mine, ("z", "xl"), 1)
+    own, theirs = barrier((own, theirs))
+
     before, after = moved(own, X, 1), moved(own, X, -1)
+    prev = [theirs, moved(theirs, "tensor", 1), moved(theirs, "tensor", -1), moved(theirs, "tensor", 2)]
+    x_a, x_b = order_query(query_latent[0])
+    before, after, x_a, x_b = barrier((before, after, x_a, x_b))
     far_low, far_high = moved(before[:32], X, 1), moved(after[32:], X, -1)
+    lat_a, lat_b, rope = order_latent(me_t, latent, rope_own, prev)
+    far_low, far_high, lat_a, lat_b, rope = barrier((far_low, far_high, lat_a, lat_b, rope))
     mine = [own, before, after, far_low, far_high]
     pieces = mine + [moved(piece, "core", 1) for piece in mine]
-
-    lat_prev = moved(shared_latent[0], ("z", "xl"), 1)
-    rope_prev = moved(rope_keys[0], ("z", "xl"), 1)
-    latents = jnp.concatenate([shared_latent[0], lat_prev], axis=0).reshape(2 * TOK, 2, 2, 8, 2, 8)
-    rope = jnp.concatenate([rope_keys[0], rope_prev], axis=0)
-    x = query_latent[0].reshape(TOK, 2, 2, 8, 2, 3, 8)
-    lat_a = latents.transpose(0, 3, 2, 1, 4, 5).reshape(2 * TOK, 512)
-    lat_b = latents.transpose(0, 1, 4, 2, 3, 5).reshape(2 * TOK, 512)
-    x_a = x.transpose(5, 0, 3, 2, 1, 4, 6).reshape(3, TOK, 512)
-    x_b = x.transpose(5, 0, 1, 4, 2, 3, 6).reshape(3, TOK, 512)
 
     attended, peaks = attend_early(place, x_b, lat_b, rope, pieces)
     attended, peaks = attend_late(place, x_a, lat_a, rope, gathered_a, attended, peaks)

time: 177 us -> 149 us (0.84)
  waiting for transfers between devices: 25.7 us -> 11.1 us
  starting transfers between devices: 51.6 us -> 38 us
  Pallas kernels: 37.2 us -> 42.8 us
  other arithmetic: 3.81 us -> 1.52 us
  blocking collectives: 18.4 us -> 16.2 us
    ppermute x21 -> x23, waiting for transfers between devices: 25.6 us -> 11.1 us  [moved(): lax.ppermute(block, axes, [(i, (i + distance) % count) for i in range(cou...]
    ppermute x21 -> x23, starting transfers between devices: 51.6 us -> 37.9 us  [moved(): lax.ppermute(block, axes, [(i, (i + distance) % count) for i in range(cou...]
    unnamed x47 -> x69, local copies, waits for them, and re-layouts: 4.14 us -> 17.6 us
    reshape x4 -> x0, local copies, waits for them, and re-layouts: 8.08 us -> none  [the longest x1 2.6 us: local(): x_a = x.transpose(5, 0, 3, 2, 1, 4, 6).reshape(3, TOK, 512)]
    transpose x4 -> x0, local copies, waits for them, and re-layouts: 7.63 us -> none  [the longest x1 2.74 us: local(): x_a = x.transpose(5, 0, 3, 2, 1, 4, 6).reshape(3, TOK, 512)]
    pallas_call x0 -> x2, Pallas kernels: none -> 6.28 us  [the longest x1 3.45 us: order_query(): pl.pallas_call(order_query_kernel, in_specs=[VMEM], out_specs=[VMEM] * 2,...]
    transpose x1 -> x0, other arithmetic: 2.25 us -> none  [local(): lat_b = latents.transpose(0, 1, 4, 2, 3, 5).reshape(2 * TOK, 512)]
    all_to_all x1, blocking collectives: 18.4 us -> 16.2 us  [local(): lax.all_to_all(jnp.broadcast_to(peaks[None], (everyone, 1, heads)), GROUP...]
  transfers between devices with their start and end apart: 22 -> 24, of which waited for: 9 -> 4; matrix products, arithmetic and copies ran while one was open for 13% -> 3% of each run, Pallas kernels for 9% -> 14%
where the time goes in v3:
time: 149 us; the launch traced here: 148 us
  Pallas kernels  42.8 us (29%)
  starting transfers between devices  38 us (26%)
  local copies, waits for them, and re-layouts  22.7 us (15%)
  blocking collectives  16.2 us (11%)
  between operations  15.6 us (10%)
  waiting for transfers between devices  11.1 us (7%)
  other arithmetic  1.52 us (1%)
    ppermute x23, starting transfers between devices, moved(): lax.ppermute(block, axes, [(i, (i + distance) % count) for i in range(cou...  37.9 us
    pallas_call x1, Pallas kernels, attend_late(): pl.pallas_call(late_kernel, grid=(PAIRS_A,), in_specs=[SMEM, whole(x), wh...  18.3 us
    unnamed x69, local copies, waits for them, and re-layouts  17.6 us
    all_to_all x1, blocking collectives, local(): lax.all_to_all(jnp.broadcast_to(peaks[None], (everyone, 1, heads)), GROUP...  16.2 us
    pallas_call x1, Pallas kernels, attend_early(): pl.pallas_call(early_kernel, grid=(PAIRS_B,), in_specs=[SMEM, whole(x), w...  12.7 us
    ppermute x23, waiting for transfers between devices, moved(): lax.ppermute(block, axes, [(i, (i + distance) % count) for i in range(cou...  11.1 us
    pallas_call x2, Pallas kernels, in_order(): pl.pallas_call(functools.partial(order_kernel, offsets), in_specs=[SMEM]...  3.99 us
    pallas_call x1, Pallas kernels, order_query(): pl.pallas_call(order_query_kernel, in_specs=[VMEM], out_specs=[VMEM] * 2,...  3.45 us
  transfers between devices with their start and end apart: 24, of which 4 were waited for; matrix products, arithmetic and copies ran while one was open for 3% of the time, Pallas kernels for 14%

profile of v3, /device:TPU:1, one launch (start us, length us, event | category | flops | bytes accessed | tf_op | source)
XLA Modules:
  0.0 148.0 jit_solution(4431934268551519968)
XLA Ops:
  7.2 1.6 %pack.1 = (bf16[8,8320]{1,0:T(8,128)(2,1)}, bf16[8,4992]{1,0:T(8,128)(2,1)}) custom-call(bf16[24,3072]{1,0:T(8,128)(2,1)} %q_ref.1, bf16[8,2048]{1,0:T(8,128)(2,1)} %k_ref.1, bf16[8,2048]{1,0:T(8,128)(2,1)} %v_ref.1), custom_call_target="tpu_custom_call" | custom-call | tf_op jit(solution)/shard_map/pack/pallas_call | solution.py:194
  8.8 2.0 %collective-permute-start = (bf16[8,8320]{1,0:T(8,128)(2,1)}, bf16[8,8320]{1,0:T(8,128)(2,1)S(1)}, u32[]{:S(2)}, u32[]{:S(2)}) collective-permute-start(bf16[8,8320]{1,0:T(8,128)(2,1)} %get-tuple-element.29.refs_0_), channel_id=1, source_target_pairs={{0,4},{4,128},{128,132},{132,0},{1,5},{5,129},{129,133},{133,1},{2... | collective-permute-start | bytes 399368 | tf_op jit(solution)/shard_map/ppermute | solution.py:307
  12.2 1.7 %collective-permute-start.2 = (bf16[8,8320]{1,0:T(8,128)(2,1)}, bf16[8,8320]{1,0:T(8,128)(2,1)S(1)}, u32[]{:S(2)}, u32[]{:S(2)}) collective-permute-start(bf16[8,8320]{1,0:T(8,128)(2,1)} %get-tuple-element.29.refs_0_), channel_id=1, source_target_pairs={{0,128},{4,132},{128,0},{132,4},{1,129},{5,133},{129,1},{133,5},{2... | collective-permute-start | bytes 399368 | tf_op jit(solution)/shard_map/ppermute | solution.py:307
  15.7 3.1 %collective-permute-done.2.refs_3_ = bf16[8,8320]{1,0:T(8,128)(2,1)S(1)} collective-permute-done((bf16[8,8320]{1,0:T(8,128)(2,1)}, bf16[8,8320]{1,0:T(8,128)(2,1)S(1)}, u32[]{:S(2)}, u32[]{:S(2)}) %collective-permute-start.2) | collective-permute-done | bytes 133152 | tf_op jit(solution)/shard_map/ppermute | solution.py:307
  19.5 1.9 %in_order.2 = bf16[4,8,8320]{2,1,0:T(8,128)(2,1)} custom-call(s32[1]{0:T(128)} %bitcast.1.me_ref, bf16[8,8320]{1,0:T(8,128)(2,1)} %get-tuple-element.29.refs_0_, bf16[8,8320]{1,0:T(8,128)(2,1)} %copy-done.20, bf16[8,8320]{1,0:T(8,128)(2,1)} %copy-done.21, bf16[8,8320]{1,0:T(8,128)(2,1)} %copy-done.22), custom_call_target="tpu_custom_call" | custom-call | tf_op jit(solution)/shard_map/in_order/pallas_call | solution.py:216
  21.4 2.5 %collective-permute-start.3 = (bf16[8,4992]{1,0:T(8,128)(2,1)S(1)}, bf16[8,4992]{1,0:T(8,128)(2,1)S(1)}, u32[]{:S(2)}, u32[]{:S(2)}) collective-permute-start(bf16[8,4992]{1,0:T(8,128)(2,1)S(1)} %copy-done.24), channel_id=1, source_target_pairs={{0,8},{8,16},{16,24},{24,32},{32,40},{40,48},{48,56},{56,0},{1,9},... | collective-permute-start | bytes 239624 | tf_op jit(solution)/shard_map/ppermute | solution.py:307
  24.0 4.0 %collective-permute-start.4 = (bf16[8,4992]{1,0:T(8,128)(2,1)S(1)}, bf16[8,4992]{1,0:T(8,128)(2,1)S(1)}, u32[]{:S(2)}, u32[]{:S(2)}) collective-permute-start(bf16[8,4992]{1,0:T(8,128)(2,1)S(1)} %copy-done.24), channel_id=1, source_target_pairs={{0,56},{8,0},{16,8},{24,16},{32,24},{40,32},{48,40},{56,48},{1,57}... | collective-permute-start | bytes 239624 | tf_op jit(solution)/shard_map/ppermute | solution.py:307
  28.0 3.6 %collective-permute-start.6 = (bf16[8,4992]{1,0:T(8,128)(2,1)S(1)}, bf16[8,4992]{1,0:T(8,128)(2,1)S(1)}, u32[]{:S(2)}, u32[]{:S(2)}) collective-permute-start(bf16[8,4992]{1,0:T(8,128)(2,1)S(1)} %copy-done.24), channel_id=1, source_target_pairs={{0,48},{8,56},{16,0},{24,8},{32,16},{40,24},{48,32},{56,40},{1,49}... | collective-permute-start | bytes 239624 | tf_op jit(solution)/shard_map/ppermute | solution.py:307
  32.3 2.9 %collective-permute-start.8 = (bf16[8,4992]{1,0:T(8,128)(2,1)S(1)}, bf16[8,4992]{1,0:T(8,128)(2,1)S(1)}, u32[]{:S(2)}, u32[]{:S(2)}) collective-permute-start(bf16[8,4992]{1,0:T(8,128)(2,1)S(1)} %collective-permute-done.4.refs_2_), channel_id=1, source_target_pairs={{0,48},{8,56},{16,0},{24,8},{32,16},{40,24},{48,32},{56,40},{1,49}... | collective-permute-start | bytes 239624 | tf_op jit(solution)/shard_map/ppermute | solution.py:307
  35.9 2.7 %collective-permute-done.7.refs_5_ = bf16[8,4992]{1,0:T(8,128)(2,1)S(1)} collective-permute-done((bf16[8,4992]{1,0:T(8,128)(2,1)S(1)}, bf16[8,4992]{1,0:T(8,128)(2,1)S(1)}, u32[]{:S(2)}, u32[]{:S(2)}) %collective-permute-start.7) | collective-permute-done | bytes 79904 | tf_op jit(solution)/shard_map/ppermute | solution.py:307
  38.6 1.5 %collective-permute-done.8.refs_6_ = bf16[8,4992]{1,0:T(8,128)(2,1)S(1)} collective-permute-done((bf16[8,4992]{1,0:T(8,128)(2,1)S(1)}, bf16[8,4992]{1,0:T(8,128)(2,1)S(1)}, u32[]{:S(2)}, u32[]{:S(2)}) %collective-permute-start.8) | collective-permute-done | bytes 79904 | tf_op jit(solution)/shard_map/ppermute | solution.py:307
  40.1 3.7 %collective-permute-done.9.refs_7_ = bf16[8,4992]{1,0:T(8,128)(2,1)S(1)} collective-permute-done((bf16[8,4992]{1,0:T(8,128)(2,1)S(1)}, bf16[8,4992]{1,0:T(8,128)(2,1)S(1)}, u32[]{:S(2)}, u32[]{:S(2)}) %collective-permute-start.9) | collective-permute-done | bytes 79904 | tf_op jit(solution)/shard_map/ppermute | solution.py:307
  44.4 2.0 %in_order.3 = bf16[8,8,4992]{2,1,0:T(8,128)(2,1)} custom-call(s32[1]{0:T(128)} %bitcast.3.me_ref, bf16[8,4992]{1,0:T(8,128)(2,1)} %get-tuple-element.31.refs_0_, bf16[8,4992]{1,0:T(8,128)(2,1)} %copy-done.25, bf16[8,4992]{1,0:T(8,128)(2,1)} %copy-done.26, bf16[8,4992]{1,0:T(8,128)(2,1)} %copy-done.27, bf16[8,4992]{1,0:T(8,128)(2,1)} %copy-done.28, ...), custom_call_target="tpu_custom_call" | custom-call | tf_op jit(solution)/shard_map/in_order/pallas_call | solution.py:216
  46.5 1.7 %collective-permute-start.11 = (bf16[64,4992]{1,0:T(8,128)(2,1)}, bf16[64,4992]{1,0:T(8,128)(2,1)S(1)}, u32[]{:S(2)}, u32[]{:S(2)}) collective-permute-start(bf16[64,4992]{1,0:T(8,128)(2,1)} %bitcast.16), channel_id=1, source_target_pairs={{0,4},{4,128},{128,132},{132,0},{1,5},{5,129},{129,133},{133,1},{2... | collective-permute-start | bytes 1916936 | tf_op jit(solution)/shard_map/ppermute | solution.py:307
  48.2 1.6 %collective-permute-start.12 = (bf16[64,4992]{1,0:T(8,128)(2,1)}, bf16[64,4992]{1,0:T(8,128)(2,1)S(1)}, u32[]{:S(2)}, u32[]{:S(2)}) collective-permute-start(bf16[64,4992]{1,0:T(8,128)(2,1)} %bitcast.17), channel_id=1, source_target_pairs={{0,132},{4,0},{128,4},{132,128},{1,133},{5,1},{129,5},{133,129},{2... | collective-permute-start | bytes 1916936 | tf_op jit(solution)/shard_map/ppermute | solution.py:307
  51.1 1.6 %collective-permute-start.16 = (bf16[128,576]{1,0:T(8,128)(2,1)}, bf16[128,576]{1,0:T(8,128)(2,1)S(1)}, u32[]{:S(2)}, u32[]{:S(2)}) collective-permute-start(bf16[128,576]{1,0:T(8,128)(2,1)} %collective-permute-done.10.refs_0_), channel_id=1, source_target_pairs={{0,3},{1,0},{2,1},{3,2},{4,7},{5,4},{6,5},{7,6},{8,11},{9,8},{10,9... | collective-permute-start | bytes 442376 | tf_op jit(solution)/shard_map/ppermute | solution.py:307
  52.8 1.5 %collective-permute-start.17 = (bf16[128,576]{1,0:T(8,128)(2,1)}, bf16[128,576]{1,0:T(8,128)(2,1)S(1)}, u32[]{:S(2)}, u32[]{:S(2)}) collective-permute-start(bf16[128,576]{1,0:T(8,128)(2,1)} %collective-permute-done.10.refs_0_), channel_id=1, source_target_pairs={{0,2},{1,3},{2,0},{3,1},{4,6},{5,7},{6,4},{7,5},{8,10},{9,11},{10,... | collective-permute-start | bytes 442376 | tf_op jit(solution)/shard_map/ppermute | solution.py:307
  55.7 3.4 %order_query.1 = (bf16[3,512,512]{2,1,0:T(8,128)(2,1)S(1)}, bf16[3,512,512]{2,1,0:T(8,128)(2,1)S(1)}) custom-call(bf16[512,1536]{1,0:T(8,128)(2,1)S(1)} %bitcast.22), custom_call_target="tpu_custom_call" | custom-call | flops 2500000000 | bytes 6000000 | tf_op jit(solution)/shard_map/order_query/pallas_call | solution.py:263
  63.0 2.7 %collective-permute-start.14 = (bf16[32,4992]{1,0:T(8,128)(2,1)}, bf16[32,4992]{1,0:T(8,128)(2,1)}, u32[]{:S(2)}, u32[]{:S(2)}) collective-permute-start(bf16[32,4992]{1,0:T(8,128)(2,1)} %slice.10), channel_id=1, source_target_pairs={{0,132},{4,0},{128,4},{132,128},{1,133},{5,1},{129,5},{133,129},{2... | collective-permute-start | bytes 958472 | tf_op jit(solution)/shard_map/ppermute | solution.py:307
  66.4 7.0 %collective-permute-start.18 = (bf16[64,4992]{1,0:T(8,128)(2,1)S(1)}, bf16[64,4992]{1,0:T(8,128)(2,1)S(1)}, u32[]{:S(2)}, u32[]{:S(2)}) collective-permute-start(bf16[64,4992]{1,0:T(8,128)(2,1)S(1)} %bitcast.18), channel_id=1, source_target_pairs={{0,64},{64,0},{1,65},{65,1},{2,66},{66,2},{3,67},{67,3},{4,68},{68... | collective-permute-start | bytes 1916936 | tf_op jit(solution)/shard_map/ppermute | solution.py:307
  79.0 2.8 %order_latent.1 = (bf16[1024,512]{1,0:T(8,128)(2,1)S(1)}, bf16[1024,512]{1,0:T(8,128)(2,1)S(1)}, bf16[1024,64]{1,0:T(8,128)(2,1)S(1)}) custom-call(s32[1]{0:T(128)} %bitcast.9.me_ref, bf16[512,512]{1,0:T(8,128)(2,1)S(1)} %bitcast.21, bf16[512,64]{1,0:T(8,128)(2,1)S(1)} %bitcast.20, bf16[128,576]{1,0:T(8,128)(2,1)} %collective-permute-done.10.refs_0_, ...), custom_call_target="tpu_custom_call" | custom-call | flops 1000000000 | bytes 4000000 | tf_op jit(solution)/shard_map/order_latent/pallas_call | solution.py:293
  90.7 12.7 %early.1 = (bf16[512,2048]{1,0:T(8,128)(2,1)}, f32[8,8,128]{2,1,0:T(8,128)S(1)}) custom-call(s32[3]{0:T(128)S(1)} %pad_add_fusion.place_ref, bf16[3,512,512]{2,1,0:T(8,128)(2,1)S(1)} %copy-done.18, bf16[1024,512]{1,0:T(8,128)(2,1)S(1)} %copy-done.13, bf16[1024,64]{1,0:T(8,128)(2,1)S(1)} %copy-done.15, bf16[64,4992]{1,0:T(8,128)(2,1)S(1)} %bitcast.19, ...), custom_call_target="tpu_custom_call" | custom-call | flops 5400000000 | bytes 6000000 | tf_op jit(solution)/shard_map/early/pallas_call | solution.py:150
  104.0 18.3 %late.1 = (bf16[512,2048]{1,0:T(8,128)(2,1)}, f32[8,8,128]{2,1,0:T(8,128)}) custom-call(s32[3]{0:T(128)} %copy-done.3, bf16[3,512,512]{2,1,0:T(8,128)(2,1)} %copy-done.16, bf16[1024,512]{1,0:T(8,128)(2,1)} %copy-done.11, bf16[1024,64]{1,0:T(8,128)(2,1)} %copy-done.14, ...), custom_call_target="tpu_custom_call", output_to_operand_aliasing={{0}: (5, {}), {1}: (6, {})} | custom-call | flops 8999999488 | bytes 10000000 | tf_op jit(solution)/shard_map/late/pallas_call | solution.py:168
  123.2 16.2 %all_to_all.5 = f32[64,1,16]{2,1,0:T(1,128)S(1)} all-to-all(f32[64,1,16]{2,1,0:T(1,128)S(1)} %broadcast_in_dim.12), channel_id=1, replica_groups=mesh['xh'=2,'core'=2,'z'=8,'xl'=2,'tensor'=4] {'xh','core','z','xl'}, dimensions={0} | all-to-all | bytes 8192 | tf_op jit(solution)/shard_map/all_to_all | solution.py:358
  (122 shorter events, 29.5 us)
Async XLA Ops:
  7.2 96.8 %all-gather.2.cloned.1.call-start = ((), (), s32[]{:S(2)}) async-start(), calls=%async_computation.1 | async-start | bytes 9052160 | tf_op jit(solution)/shard_map/all_gather | solution.py:334
  8.8 6.8 %collective-permute-start = (bf16[8,8320]{1,0:T(8,128)(2,1)}, bf16[8,8320]{1,0:T(8,128)(2,1)S(1)}, u32[]{:S(2)}, u32[]{:S(2)}) collective-permute-start(bf16[8,8320]{1,0:T(8,128)(2,1)} %get-tuple-element.29.refs_0_), channel_id=1, source_target_pairs={{0,4},{4,128},{128,132},{132,0},{1,5},{5,129},{129,133},{133,1},{2... | collective-permute-start | bytes 399368 | tf_op jit(solution)/shard_map/ppermute | solution.py:307
  10.9 4.8 %collective-permute-start.1 = (bf16[8,8320]{1,0:T(8,128)(2,1)}, bf16[8,8320]{1,0:T(8,128)(2,1)S(1)}, u32[]{:S(2)}, u32[]{:S(2)}) collective-permute-start(bf16[8,8320]{1,0:T(8,128)(2,1)} %get-tuple-element.29.refs_0_), channel_id=1, source_target_pairs={{0,132},{4,0},{128,4},{132,128},{1,133},{5,1},{129,5},{133,129},{2... | collective-permute-start | bytes 399368 | tf_op jit(solution)/shard_map/ppermute | solution.py:307
  12.2 6.6 %collective-permute-start.2 = (bf16[8,8320]{1,0:T(8,128)(2,1)}, bf16[8,8320]{1,0:T(8,128)(2,1)S(1)}, u32[]{:S(2)}, u32[]{:S(2)}) collective-permute-start(bf16[8,8320]{1,0:T(8,128)(2,1)} %get-tuple-element.29.refs_0_), channel_id=1, source_target_pairs={{0,128},{4,132},{128,0},{132,4},{1,129},{5,133},{129,1},{133,5},{2... | collective-permute-start | bytes 399368 | tf_op jit(solution)/shard_map/ppermute | solution.py:307
  21.4 10.1 %collective-permute-start.3 = (bf16[8,4992]{1,0:T(8,128)(2,1)S(1)}, bf16[8,4992]{1,0:T(8,128)(2,1)S(1)}, u32[]{:S(2)}, u32[]{:S(2)}) collective-permute-start(bf16[8,4992]{1,0:T(8,128)(2,1)S(1)} %copy-done.24), channel_id=1, source_target_pairs={{0,8},{8,16},{16,24},{24,32},{32,40},{40,48},{48,56},{56,0},{1,9},... | collective-permute-start | bytes 239624 | tf_op jit(solution)/shard_map/ppermute | solution.py:307
  24.0 8.3 %collective-permute-start.4 = (bf16[8,4992]{1,0:T(8,128)(2,1)S(1)}, bf16[8,4992]{1,0:T(8,128)(2,1)S(1)}, u32[]{:S(2)}, u32[]{:S(2)}) collective-permute-start(bf16[8,4992]{1,0:T(8,128)(2,1)S(1)} %copy-done.24), channel_id=1, source_target_pairs={{0,56},{8,0},{16,8},{24,16},{32,24},{40,32},{48,40},{56,48},{1,57}... | collective-permute-start | bytes 239624 | tf_op jit(solution)/shard_map/ppermute | solution.py:307
  28.0 7.2 %collective-permute-start.5 = (bf16[8,4992]{1,0:T(8,128)(2,1)S(1)}, bf16[8,4992]{1,0:T(8,128)(2,1)S(1)}, u32[]{:S(2)}, u32[]{:S(2)}) collective-permute-start(bf16[8,4992]{1,0:T(8,128)(2,1)S(1)} %copy-done.24), channel_id=1, source_target_pairs={{0,16},{8,24},{16,32},{24,40},{32,48},{40,56},{48,0},{56,8},{1,17}... | collective-permute-start | bytes 239624 | tf_op jit(solution)/shard_map/ppermute | solution.py:307
  28.0 18.5 %collective-permute-start.10 = (bf16[128,576]{1,0:T(8,128)(2,1)S(1)}, bf16[128,576]{1,0:T(8,128)(2,1)}, u32[]{:S(2)}, u32[]{:S(2)}) collective-permute-start(bf16[128,576]{1,0:T(8,128)(2,1)S(1)} %pad_maximum_fusion), channel_id=1, source_target_pairs={{0,4},{4,8},{8,12},{12,16},{16,20},{20,24},{24,28},{28,32},{32,36}... | collective-permute-start | bytes 442376 | tf_op jit(solution)/shard_map/ppermute | solution.py:307
  28.0 7.9 %collective-permute-start.6 = (bf16[8,4992]{1,0:T(8,128)(2,1)S(1)}, bf16[8,4992]{1,0:T(8,128)(2,1)S(1)}, u32[]{:S(2)}, u32[]{:S(2)}) collective-permute-start(bf16[8,4992]{1,0:T(8,128)(2,1)S(1)} %copy-done.24), channel_id=1, source_target_pairs={{0,48},{8,56},{16,0},{24,8},{32,16},{40,24},{48,32},{56,40},{1,49}... | collective-permute-start | bytes 239624 | tf_op jit(solution)/shard_map/ppermute | solution.py:307
  31.6 7.0 %collective-permute-start.7 = (bf16[8,4992]{1,0:T(8,128)(2,1)S(1)}, bf16[8,4992]{1,0:T(8,128)(2,1)S(1)}, u32[]{:S(2)}, u32[]{:S(2)}) collective-permute-start(bf16[8,4992]{1,0:T(8,128)(2,1)S(1)} %collective-permute-done.3.refs_1_), channel_id=1, source_target_pairs={{0,16},{8,24},{16,32},{24,40},{32,48},{40,56},{48,0},{56,8},{1,17}... | collective-permute-start | bytes 239624 | tf_op jit(solution)/shard_map/ppermute | solution.py:307
  32.3 7.8 %collective-permute-start.8 = (bf16[8,4992]{1,0:T(8,128)(2,1)S(1)}, bf16[8,4992]{1,0:T(8,128)(2,1)S(1)}, u32[]{:S(2)}, u32[]{:S(2)}) collective-permute-start(bf16[8,4992]{1,0:T(8,128)(2,1)S(1)} %collective-permute-done.4.refs_2_), channel_id=1, source_target_pairs={{0,48},{8,56},{16,0},{24,8},{32,16},{40,24},{48,32},{56,40},{1,49}... | collective-permute-start | bytes 239624 | tf_op jit(solution)/shard_map/ppermute | solution.py:307
  35.2 8.7 %collective-permute-start.9 = (bf16[8,4992]{1,0:T(8,128)(2,1)S(1)}, bf16[8,4992]{1,0:T(8,128)(2,1)S(1)}, u32[]{:S(2)}, u32[]{:S(2)}) collective-permute-start(bf16[8,4992]{1,0:T(8,128)(2,1)S(1)} %collective-permute-done.5.refs_3_), channel_id=1, source_target_pairs={{0,16},{8,24},{16,32},{24,40},{32,48},{40,56},{48,0},{56,8},{1,17}... | collective-permute-start | bytes 239624 | tf_op jit(solution)/shard_map/ppermute | solution.py:307
  46.5 15.0 %collective-permute-start.11 = (bf16[64,4992]{1,0:T(8,128)(2,1)}, bf16[64,4992]{1,0:T(8,128)(2,1)S(1)}, u32[]{:S(2)}, u32[]{:S(2)}) collective-permute-start(bf16[64,4992]{1,0:T(8,128)(2,1)} %bitcast.16), channel_id=1, source_target_pairs={{0,4},{4,128},{128,132},{132,0},{1,5},{5,129},{129,133},{133,1},{2... | collective-permute-start | bytes 1916936 | tf_op jit(solution)/shard_map/ppermute | solution.py:307
  48.2 13.3 %collective-permute-start.12 = (bf16[64,4992]{1,0:T(8,128)(2,1)}, bf16[64,4992]{1,0:T(8,128)(2,1)S(1)}, u32[]{:S(2)}, u32[]{:S(2)}) collective-permute-start(bf16[64,4992]{1,0:T(8,128)(2,1)} %bitcast.17), channel_id=1, source_target_pairs={{0,132},{4,0},{128,4},{132,128},{1,133},{5,1},{129,5},{133,129},{2... | collective-permute-start | bytes 1916936 | tf_op jit(solution)/shard_map/ppermute | solution.py:307
  49.8 15.9 %collective-permute-start.15 = (bf16[128,576]{1,0:T(8,128)(2,1)}, bf16[128,576]{1,0:T(8,128)(2,1)S(1)}, u32[]{:S(2)}, u32[]{:S(2)}) collective-permute-start(bf16[128,576]{1,0:T(8,128)(2,1)} %collective-permute-done.10.refs_0_), channel_id=1, source_target_pairs={{0,1},{1,2},{2,3},{3,0},{4,5},{5,6},{6,7},{7,4},{8,9},{9,10},{10,1... | collective-permute-start | bytes 442376 | tf_op jit(solution)/shard_map/ppermute | solution.py:307
  51.1 22.2 %collective-permute-start.16 = (bf16[128,576]{1,0:T(8,128)(2,1)}, bf16[128,576]{1,0:T(8,128)(2,1)S(1)}, u32[]{:S(2)}, u32[]{:S(2)}) collective-permute-start(bf16[128,576]{1,0:T(8,128)(2,1)} %collective-permute-done.10.refs_0_), channel_id=1, source_target_pairs={{0,3},{1,0},{2,1},{3,2},{4,7},{5,4},{6,5},{7,6},{8,11},{9,8},{10,9... | collective-permute-start | bytes 442376 | tf_op jit(solution)/shard_map/ppermute | solution.py:307
  52.8 21.3 %collective-permute-start.17 = (bf16[128,576]{1,0:T(8,128)(2,1)}, bf16[128,576]{1,0:T(8,128)(2,1)S(1)}, u32[]{:S(2)}, u32[]{:S(2)}) collective-permute-start(bf16[128,576]{1,0:T(8,128)(2,1)} %collective-permute-done.10.refs_0_), channel_id=1, source_target_pairs={{0,2},{1,3},{2,0},{3,1},{4,6},{5,7},{6,4},{7,5},{8,10},{9,11},{10,... | collective-permute-start | bytes 442376 | tf_op jit(solution)/shard_map/ppermute | solution.py:307
  62.3 22.3 %collective-permute-start.13 = (bf16[32,4992]{1,0:T(8,128)(2,1)}, bf16[32,4992]{1,0:T(8,128)(2,1)S(1)}, u32[]{:S(2)}, u32[]{:S(2)}) collective-permute-start(bf16[32,4992]{1,0:T(8,128)(2,1)} %slice.9), channel_id=1, source_target_pairs={{0,4},{4,128},{128,132},{132,0},{1,5},{5,129},{129,133},{133,1},{2... | collective-permute-start | bytes 958472 | tf_op jit(solution)/shard_map/ppermute | solution.py:307
  63.0 21.5 %collective-permute-start.14 = (bf16[32,4992]{1,0:T(8,128)(2,1)}, bf16[32,4992]{1,0:T(8,128)(2,1)}, u32[]{:S(2)}, u32[]{:S(2)}) collective-permute-start(bf16[32,4992]{1,0:T(8,128)(2,1)} %slice.10), channel_id=1, source_target_pairs={{0,132},{4,0},{128,4},{132,128},{1,133},{5,1},{129,5},{133,129},{2... | collective-permute-start | bytes 958472 | tf_op jit(solution)/shard_map/ppermute | solution.py:307
  66.4 20.6 %collective-permute-start.18 = (bf16[64,4992]{1,0:T(8,128)(2,1)S(1)}, bf16[64,4992]{1,0:T(8,128)(2,1)S(1)}, u32[]{:S(2)}, u32[]{:S(2)}) collective-permute-start(bf16[64,4992]{1,0:T(8,128)(2,1)S(1)} %bitcast.18), channel_id=1, source_target_pairs={{0,64},{64,0},{1,65},{65,1},{2,66},{66,2},{3,67},{67,3},{4,68},{68... | collective-permute-start | bytes 1916936 | tf_op jit(solution)/shard_map/ppermute | solution.py:307
  74.0 13.0 %collective-permute-start.19 = (bf16[64,4992]{1,0:T(8,128)(2,1)S(1)}, bf16[64,4992]{1,0:T(8,128)(2,1)}, u32[]{:S(2)}, u32[]{:S(2)}) collective-permute-start(bf16[64,4992]{1,0:T(8,128)(2,1)S(1)} %collective-permute-done.11.rest_1_), channel_id=1, source_target_pairs={{0,64},{64,0},{1,65},{65,1},{2,66},{66,2},{3,67},{67,3},{4,68},{68... | collective-permute-start | bytes 1916936 | tf_op jit(solution)/shard_map/ppermute | solution.py:307
  74.7 12.3 %collective-permute-start.20 = (bf16[64,4992]{1,0:T(8,128)(2,1)S(1)}, bf16[64,4992]{1,0:T(8,128)(2,1)}, u32[]{:S(2)}, u32[]{:S(2)}) collective-permute-start(bf16[64,4992]{1,0:T(8,128)(2,1)S(1)} %collective-permute-done.12.rest_2_), channel_id=1, source_target_pairs={{0,64},{64,0},{1,65},{65,1},{2,66},{66,2},{3,67},{67,3},{4,68},{68... | collective-permute-start | bytes 1916936 | tf_op jit(solution)/shard_map/ppermute | solution.py:307
  84.5 2.5 %collective-permute-start.21 = (bf16[32,4992]{1,0:T(8,128)(2,1)S(1)}, bf16[32,4992]{1,0:T(8,128)(2,1)S(1)}, u32[]{:S(2)}, u32[]{:S(2)}) collective-permute-start(bf16[32,4992]{1,0:T(8,128)(2,1)S(1)} %collective-permute-done.13.rest_3_), channel_id=1, source_target_pairs={{0,64},{64,0},{1,65},{65,1},{2,66},{66,2},{3,67},{67,3},{4,68},{68... | collective-permute-start | bytes 958472 | tf_op jit(solution)/shard_map/ppermute | solution.py:307
  84.5 2.5 %collective-permute-start.22 = (bf16[32,4992]{1,0:T(8,128)(2,1)}, bf16[32,4992]{1,0:T(8,128)(2,1)S(1)}, u32[]{:S(2)}, u32[]{:S(2)}) collective-permute-start(bf16[32,4992]{1,0:T(8,128)(2,1)} %collective-permute-done.14.rest_4_), channel_id=1, source_target_pairs={{0,64},{64,0},{1,65},{65,1},{2,66},{66,2},{3,67},{67,3},{4,68},{68... | collective-permute-start | bytes 958472 | tf_op jit(solution)/shard_map/ppermute | solution.py:307
  (34 other events, 228.5 us)
Sparse Core Ops, SparseCore 0:
  21.6 63.7 all-gather.1

commit v4 on v3

--- a/solution.py
+++ b/solution.py
@@ -33,6 +33,9 @@
 VMEM = pl.BlockSpec(memory_space=pltpu.VMEM)
 SMEM = pl.BlockSpec(memory_space=pltpu.SMEM)
 ANY = pl.BlockSpec(memory_space=pl.ANY)
+HBM = pl.BlockSpec(memory_space=pltpu.HBM)
+EARLY_MIB = 24
+LATE_MIB = 48
 
 
 def dot_f32(a, b):
@@ -93,90 +96,81 @@
         peak_ref[0, head : head + 1, :] = jnp.broadcast_to(top, (1, 128))
 
 
-def late_kernel(place_ref, x_ref, lat_ref, rope_ref, w_ref, _out, _peaks, out_ref, peak_ref):
-    attend_pair(
-        place_ref[0] > 0, x_ref, lat_ref, rope_ref, lambda start, width: w_ref[:, start : start + width], out_ref, peak_ref
-    )
-
-
-def early_kernel(place_ref, x_ref, lat_ref, rope_ref, *rest):
-    pieces, (out_ref, peak_ref, w_ref, sems) = rest[:10], rest[10:]
+def in_slots(pairs, copies, w_ref, sems):
     pair = pl.program_id(0)
+    slot = lax.rem(pair, 2)
 
     @pl.when(pair == 0)
     def _():
-        me, core = place_ref[1], place_ref[2]
-        copies = []
+        for copy in copies(0, 0):
+            copy.start()
+
+    @pl.when(pair + 1 < pairs)
+    def _():
+        for copy in copies(pair + 1, 1 - slot):
+            copy.start()
+
+    for copy in copies(pair, slot):
+        copy.wait()
+    return lambda start, width: w_ref[slot, :, start : start + width]
+
+
+def late_kernel(place_ref, x_ref, lat_ref, rope_ref, all_ref, *rest):
+    out_ref, peak_ref, w_ref, sems = rest[-4:]
+
+    def copies(pair, slot):
+        columns = pl.ds(pl.multiple_of(pair * WIDE, 128), WIDE)
+        return [pltpu.make_async_copy(all_ref.at[:, columns], w_ref.at[slot], sems.at[slot, 0])]
+
+    weight = in_slots(PAIRS_A, copies, w_ref, sems)
+    attend_pair(place_ref[0] > 0, x_ref, lat_ref, rope_ref, weight, out_ref, peak_ref)
+
+
+def early_kernel(place_ref, x_ref, lat_ref, rope_ref, *rest):
+    pieces, (out_ref, peak_ref, w_ref, sems) = rest[:10], rest[-4:]
+    me, core = place_ref[1], place_ref[2]
+
+    def copies(pair, slot):
+        columns = pl.ds(pl.multiple_of(pair * WIDE, 128), WIDE)
+        made = []
         for side in range(2):
             owner = core if side == 0 else 1 - core
-            own, before, after, far_low, far_high = pieces[5 * side : 5 * side + 5]
-            for piece, step, first in ((own, 0, 0), (before, 3, 0), (after, 1, 0), (far_low, 2, 0), (far_high, 2, 32)):
+            for piece, step, first in zip(pieces[5 * side : 5 * side + 5], (0, 3, 1, 2, 2), (0, 0, 0, 0, 32)):
                 block = lax.rem(me + step, 4) * 2 + owner
                 rows = pl.ds(pl.multiple_of(block * 64 + first, 32), piece.shape[0])
-                copies.append(pltpu.make_async_copy(piece, w_ref.at[rows, :], sems.at[len(copies)]))
-        for copy in copies:
-            copy.start()
-        for copy in copies:
-            copy.wait()
-
-    def weight(start, width):
-        return w_ref[:, pl.ds(pl.multiple_of(pair * WIDE + start, 128), width)]
-
+                made.append(
+                    pltpu.make_async_copy(piece.at[:, columns], w_ref.at[slot, rows, :], sems.at[slot, len(made)])
+                )
+        return made
+
+    weight = in_slots(PAIRS_B, copies, w_ref, sems)
     attend_pair(place_ref[0] > 0, x_ref, lat_ref, rope_ref, weight, out_ref, peak_ref)
 
 
-def whole(array):
-    return pl.BlockSpec(array.shape, lambda p: (0,) * array.ndim)
-
-
-def cost(pairs):
-    return pl.CostEstimate(flops=1_800_000_000 * pairs, bytes_accessed=2_000_000 * pairs, transcendentals=1_000_000 * pairs)
-
-
-def outputs(first):
-    specs = [
-        pl.BlockSpec((TOK, PAIR * V_DIM), lambda p: (0, first + p)),
-        pl.BlockSpec((1, 8, 128), lambda p: (first + p, 0, 0)),
-    ]
-    shapes = [
-        jax.ShapeDtypeStruct((TOK, PAIRS * PAIR * V_DIM), jnp.bfloat16),
-        jax.ShapeDtypeStruct((PAIRS, 8, 128), jnp.float32),
-    ]
-    return specs, shapes
-
-
-def attend_early(place, x, latents, rope, pieces):
-    specs, shapes = outputs(PAIRS_A)
-    return pl.pallas_call(
-        early_kernel,
-        grid=(PAIRS_B,),
-        in_specs=[SMEM, whole(x), whole(latents), whole(rope)] + [ANY] * len(pieces),
-        out_specs=specs,
-        out_shape=shapes,
+def attend(kernel, name, first, pairs, copies, place, x, latents, rope, weights, before=()):
+    return pl.pallas_call(
+        kernel,
+        grid=(pairs,),
+        in_specs=[SMEM, VMEM, VMEM, VMEM] + [HBM if len(weights) == 1 else ANY] * len(weights) + [ANY] * len(before),
+        out_specs=[
+            pl.BlockSpec((TOK, PAIR * V_DIM), lambda p: (0, first + p)),
+            pl.BlockSpec((1, 8, 128), lambda p: (first + p, 0, 0)),
+        ],
+        out_shape=[
+            jax.ShapeDtypeStruct((TOK, PAIRS * PAIR * V_DIM), jnp.bfloat16),
+            jax.ShapeDtypeStruct((PAIRS, 8, 128), jnp.float32),
+        ],
+        input_output_aliases={4 + len(weights) + i: i for i in range(len(before))},
         scratch_shapes=[
-            pltpu.VMEM((TOK, PAIRS_B * WIDE), jnp.bfloat16),
-            pltpu.SemaphoreType.DMA((len(pieces),)),
+            pltpu.VMEM((2, TOK, WIDE), jnp.bfloat16),
+            pltpu.SemaphoreType.DMA((2, copies)),
         ],
-        compiler_params=pltpu.CompilerParams(vmem_limit_bytes=36 * MIB),
-        cost_estimate=cost(PAIRS_B),
-        name="early",
-    )(place, x, latents, rope, *pieces)
-
-
-def attend_late(place, x, latents, rope, gathered, out, peaks):
-    specs, shapes = outputs(0)
-    return pl.pallas_call(
-        late_kernel,
-        grid=(PAIRS_A,),
-        in_specs=[SMEM, whole(x), whole(latents), whole(rope)]
-        + [pl.BlockSpec((TOK, WIDE), lambda p: (0, p)), ANY, ANY],
-        out_specs=specs,
-        out_shape=shapes,
-        input_output_aliases={5: 0, 6: 1},
-        compiler_params=pltpu.CompilerParams(vmem_limit_bytes=56 * MIB),
-        cost_estimate=cost(PAIRS_A),
-        name="late",
-    )(place, x, latents, rope, gathered, out, peaks)
+        compiler_params=pltpu.CompilerParams(vmem_limit_bytes=(LATE_MIB if before else EARLY_MIB) * MIB),
+        cost_estimate=pl.CostEstimate(
+            flops=1_800_000_000 * pairs, bytes_accessed=2_000_000 * pairs, transcendentals=1_000_000 * pairs
+        ),
+        name=name,
+    )(place, x, latents, rope, *weights, *before)
 
 
 def pack_kernel(q_ref, k_ref, v_ref, a_ref, b_ref):
@@ -350,8 +344,8 @@
     mine = [own, before, after, far_low, far_high]
     pieces = mine + [moved(piece, "core", 1) for piece in mine]
 
-    attended, peaks = attend_early(place, x_b, lat_b, rope, pieces)
-    attended, peaks = attend_late(place, x_a, lat_a, rope, gathered_a, attended, peaks)
+    done = attend(early_kernel, "early", PAIRS_A, PAIRS_B, 10, place, x_b, lat_b, rope, pieces)
+    attended, peaks = attend(late_kernel, "late", 0, PAIRS_A, 1, place, x_a, lat_a, rope, [gathered_a], done)
 
     peaks = peaks[:, :PAIR, 0].reshape(1, heads)
     everyone = lax.axis_size(GROUP)

time: 149 us -> 149 us (level)
    unnamed x69, local copies, waits for them, and re-layouts: 17.6 us -> 19.7 us
where the time goes in v4:
time: 149 us
  Pallas kernels  42.2 us (28%)
  starting transfers between devices  38 us (26%)
  local copies, waits for them, and re-layouts  24 us (16%)
  blocking collectives  16.2 us (11%)
  between operations  15.6 us (10%)
  waiting for transfers between devices  11.1 us (7%)
  other arithmetic  1.52 us (1%)
    ppermute x23, starting transfers between devices, moved(): lax.ppermute(block, axes, [(i, (i + distance) % count) for i in range(cou...  37.9 us
    pallas_call x2, Pallas kernels, attend(): pl.pallas_call(kernel, grid=(pairs,), in_specs=[SMEM, VMEM, VMEM, VMEM] +...  30.3 us
    unnamed x69, local copies, waits for them, and re-layouts  19.7 us
    all_to_all x1, blocking collectives, local(): lax.all_to_all(jnp.broadcast_to(peaks[None], (everyone, 1, heads)), GROUP...  16.2 us
    ppermute x23, waiting for transfers between devices, moved(): lax.ppermute(block, axes, [(i, (i + distance) % count) for i in range(cou...  11.1 us
    pallas_call x2, Pallas kernels, in_order(): pl.pallas_call(functools.partial(order_kernel, offsets), in_specs=[SMEM]...  3.99 us
    pallas_call x1, Pallas kernels, order_query(): pl.pallas_call(order_query_kernel, in_specs=[VMEM], out_specs=[VMEM] * 2,...  3.45 us
  transfers between devices with their start and end apart: 24, of which 4 were waited for; matrix products, arithmetic and copies ran while one was open for 3% of the time, Pallas kernels for 14%

profile of v4, /device:TPU:1, one launch (start us, length us, event | category | flops | bytes accessed | tf_op | source)
XLA Modules:
  0.0 148.6 jit_solution(7976516742934055321)
XLA Ops:
  7.2 1.6 %pack.1 = (bf16[8,8320]{1,0:T(8,128)(2,1)}, bf16[8,4992]{1,0:T(8,128)(2,1)}) custom-call(bf16[24,3072]{1,0:T(8,128)(2,1)} %q_ref.1, bf16[8,2048]{1,0:T(8,128)(2,1)} %k_ref.1, bf16[8,2048]{1,0:T(8,128)(2,1)} %v_ref.1), custom_call_target="tpu_custom_call" | custom-call | tf_op jit(solution)/shard_map/pack/pallas_call | solution.py:188
  8.8 2.0 %collective-permute-start = (bf16[8,8320]{1,0:T(8,128)(2,1)}, bf16[8,8320]{1,0:T(8,128)(2,1)S(1)}, u32[]{:S(2)}, u32[]{:S(2)}) collective-permute-start(bf16[8,8320]{1,0:T(8,128)(2,1)} %get-tuple-element.29.refs_0_), channel_id=1, source_target_pairs={{0,4},{4,128},{128,132},{132,0},{1,5},{5,129},{129,133},{133,1},{2... | collective-permute-start | bytes 399368 | tf_op jit(solution)/shard_map/ppermute | solution.py:301
  12.2 1.7 %collective-permute-start.2 = (bf16[8,8320]{1,0:T(8,128)(2,1)}, bf16[8,8320]{1,0:T(8,128)(2,1)S(1)}, u32[]{:S(2)}, u32[]{:S(2)}) collective-permute-start(bf16[8,8320]{1,0:T(8,128)(2,1)} %get-tuple-element.29.refs_0_), channel_id=1, source_target_pairs={{0,128},{4,132},{128,0},{132,4},{1,129},{5,133},{129,1},{133,5},{2... | collective-permute-start | bytes 399368 | tf_op jit(solution)/shard_map/ppermute | solution.py:301
  15.7 3.1 %collective-permute-done.2.refs_3_ = bf16[8,8320]{1,0:T(8,128)(2,1)S(1)} collective-permute-done((bf16[8,8320]{1,0:T(8,128)(2,1)}, bf16[8,8320]{1,0:T(8,128)(2,1)S(1)}, u32[]{:S(2)}, u32[]{:S(2)}) %collective-permute-start.2) | collective-permute-done | bytes 133152 | tf_op jit(solution)/shard_map/ppermute | solution.py:301
  19.5 1.9 %in_order.2 = bf16[4,8,8320]{2,1,0:T(8,128)(2,1)} custom-call(s32[1]{0:T(128)} %bitcast.1.me_ref, bf16[8,8320]{1,0:T(8,128)(2,1)} %get-tuple-element.29.refs_0_, bf16[8,8320]{1,0:T(8,128)(2,1)} %copy-done.20, bf16[8,8320]{1,0:T(8,128)(2,1)} %copy-done.21, bf16[8,8320]{1,0:T(8,128)(2,1)} %copy-done.22), custom_call_target="tpu_custom_call" | custom-call | tf_op jit(solution)/shard_map/in_order/pallas_call | solution.py:210
  21.4 2.5 %collective-permute-start.3 = (bf16[8,4992]{1,0:T(8,128)(2,1)S(1)}, bf16[8,4992]{1,0:T(8,128)(2,1)S(1)}, u32[]{:S(2)}, u32[]{:S(2)}) collective-permute-start(bf16[8,4992]{1,0:T(8,128)(2,1)S(1)} %copy-done.24), channel_id=1, source_target_pairs={{0,8},{8,16},{16,24},{24,32},{32,40},{40,48},{48,56},{56,0},{1,9},... | collective-permute-start | bytes 239624 | tf_op jit(solution)/shard_map/ppermute | solution.py:301
  24.0 4.0 %collective-permute-start.4 = (bf16[8,4992]{1,0:T(8,128)(2,1)S(1)}, bf16[8,4992]{1,0:T(8,128)(2,1)S(1)}, u32[]{:S(2)}, u32[]{:S(2)}) collective-permute-start(bf16[8,4992]{1,0:T(8,128)(2,1)S(1)} %copy-done.24), channel_id=1, source_target_pairs={{0,56},{8,0},{16,8},{24,16},{32,24},{40,32},{48,40},{56,48},{1,57}... | collective-permute-start | bytes 239624 | tf_op jit(solution)/shard_map/ppermute | solution.py:301
  28.0 3.6 %collective-permute-start.6 = (bf16[8,4992]{1,0:T(8,128)(2,1)S(1)}, bf16[8,4992]{1,0:T(8,128)(2,1)S(1)}, u32[]{:S(2)}, u32[]{:S(2)}) collective-permute-start(bf16[8,4992]{1,0:T(8,128)(2,1)S(1)} %copy-done.24), channel_id=1, source_target_pairs={{0,48},{8,56},{16,0},{24,8},{32,16},{40,24},{48,32},{56,40},{1,49}... | collective-permute-start | bytes 239624 | tf_op jit(solution)/shard_map/ppermute | solution.py:301
  32.3 2.9 %collective-permute-start.8 = (bf16[8,4992]{1,0:T(8,128)(2,1)S(1)}, bf16[8,4992]{1,0:T(8,128)(2,1)S(1)}, u32[]{:S(2)}, u32[]{:S(2)}) collective-permute-start(bf16[8,4992]{1,0:T(8,128)(2,1)S(1)} %collective-permute-done.4.refs_2_), channel_id=1, source_target_pairs={{0,48},{8,56},{16,0},{24,8},{32,16},{40,24},{48,32},{56,40},{1,49}... | collective-permute-start | bytes 239624 | tf_op jit(solution)/shard_map/ppermute | solution.py:301
  35.9 2.7 %collective-permute-done.7.refs_5_ = bf16[8,4992]{1,0:T(8,128)(2,1)S(1)} collective-permute-done((bf16[8,4992]{1,0:T(8,128)(2,1)S(1)}, bf16[8,4992]{1,0:T(8,128)(2,1)S(1)}, u32[]{:S(2)}, u32[]{:S(2)}) %collective-permute-start.7) | collective-permute-done | bytes 79904 | tf_op jit(solution)/shard_map/ppermute | solution.py:301
  38.6 1.5 %collective-permute-done.8.refs_6_ = bf16[8,4992]{1,0:T(8,128)(2,1)S(1)} collective-permute-done((bf16[8,4992]{1,0:T(8,128)(2,1)S(1)}, bf16[8,4992]{1,0:T(8,128)(2,1)S(1)}, u32[]{:S(2)}, u32[]{:S(2)}) %collective-permute-start.8) | collective-permute-done | bytes 79904 | tf_op jit(solution)/shard_map/ppermute | solution.py:301
  40.1 3.7 %collective-permute-done.9.refs_7_ = bf16[8,4992]{1,0:T(8,128)(2,1)S(1)} collective-permute-done((bf16[8,4992]{1,0:T(8,128)(2,1)S(1)}, bf16[8,4992]{1,0:T(8,128)(2,1)S(1)}, u32[]{:S(2)}, u32[]{:S(2)}) %collective-permute-start.9) | collective-permute-done | bytes 79904 | tf_op jit(solution)/shard_map/ppermute | solution.py:301
  44.4 2.0 %in_order.3 = bf16[8,8,4992]{2,1,0:T(8,128)(2,1)} custom-call(s32[1]{0:T(128)} %bitcast.3.me_ref, bf16[8,4992]{1,0:T(8,128)(2,1)} %get-tuple-element.31.refs_0_, bf16[8,4992]{1,0:T(8,128)(2,1)} %copy-done.25, bf16[8,4992]{1,0:T(8,128)(2,1)} %copy-done.26, bf16[8,4992]{1,0:T(8,128)(2,1)} %copy-done.27, bf16[8,4992]{1,0:T(8,128)(2,1)} %copy-done.28, ...), custom_call_target="tpu_custom_call" | custom-call | tf_op jit(solution)/shard_map/in_order/pallas_call | solution.py:210
  46.5 1.7 %collective-permute-start.11 = (bf16[64,4992]{1,0:T(8,128)(2,1)}, bf16[64,4992]{1,0:T(8,128)(2,1)S(1)}, u32[]{:S(2)}, u32[]{:S(2)}) collective-permute-start(bf16[64,4992]{1,0:T(8,128)(2,1)} %bitcast.16), channel_id=1, source_target_pairs={{0,4},{4,128},{128,132},{132,0},{1,5},{5,129},{129,133},{133,1},{2... | collective-permute-start | bytes 1916936 | tf_op jit(solution)/shard_map/ppermute | solution.py:301
  48.2 1.6 %collective-permute-start.12 = (bf16[64,4992]{1,0:T(8,128)(2,1)}, bf16[64,4992]{1,0:T(8,128)(2,1)S(1)}, u32[]{:S(2)}, u32[]{:S(2)}) collective-permute-start(bf16[64,4992]{1,0:T(8,128)(2,1)} %bitcast.17), channel_id=1, source_target_pairs={{0,132},{4,0},{128,4},{132,128},{1,133},{5,1},{129,5},{133,129},{2... | collective-permute-start | bytes 1916936 | tf_op jit(solution)/shard_map/ppermute | solution.py:301
  51.1 1.6 %collective-permute-start.16 = (bf16[128,576]{1,0:T(8,128)(2,1)}, bf16[128,576]{1,0:T(8,128)(2,1)S(1)}, u32[]{:S(2)}, u32[]{:S(2)}) collective-permute-start(bf16[128,576]{1,0:T(8,128)(2,1)} %collective-permute-done.10.refs_0_), channel_id=1, source_target_pairs={{0,3},{1,0},{2,1},{3,2},{4,7},{5,4},{6,5},{7,6},{8,11},{9,8},{10,9... | collective-permute-start | bytes 442376 | tf_op jit(solution)/shard_map/ppermute | solution.py:301
  52.8 1.5 %collective-permute-start.17 = (bf16[128,576]{1,0:T(8,128)(2,1)}, bf16[128,576]{1,0:T(8,128)(2,1)S(1)}, u32[]{:S(2)}, u32[]{:S(2)}) collective-permute-start(bf16[128,576]{1,0:T(8,128)(2,1)} %collective-permute-done.10.refs_0_), channel_id=1, source_target_pairs={{0,2},{1,3},{2,0},{3,1},{4,6},{5,7},{6,4},{7,5},{8,10},{9,11},{10,... | collective-permute-start | bytes 442376 | tf_op jit(solution)/shard_map/ppermute | solution.py:301
  55.7 3.4 %order_query.1 = (bf16[3,512,512]{2,1,0:T(8,128)(2,1)S(1)}, bf16[3,512,512]{2,1,0:T(8,128)(2,1)S(1)}) custom-call(bf16[512,1536]{1,0:T(8,128)(2,1)S(1)} %bitcast.22), custom_call_target="tpu_custom_call" | custom-call | flops 2500000000 | bytes 6000000 | tf_op jit(solution)/shard_map/order_query/pallas_call | solution.py:257
  63.0 2.7 %collective-permute-start.14 = (bf16[32,4992]{1,0:T(8,128)(2,1)}, bf16[32,4992]{1,0:T(8,128)(2,1)}, u32[]{:S(2)}, u32[]{:S(2)}) collective-permute-start(bf16[32,4992]{1,0:T(8,128)(2,1)} %slice.10), channel_id=1, source_target_pairs={{0,132},{4,0},{128,4},{132,128},{1,133},{5,1},{129,5},{133,129},{2... | collective-permute-start | bytes 958472 | tf_op jit(solution)/shard_map/ppermute | solution.py:301
  66.4 7.0 %collective-permute-start.18 = (bf16[64,4992]{1,0:T(8,128)(2,1)S(1)}, bf16[64,4992]{1,0:T(8,128)(2,1)S(1)}, u32[]{:S(2)}, u32[]{:S(2)}) collective-permute-start(bf16[64,4992]{1,0:T(8,128)(2,1)S(1)} %bitcast.18), channel_id=1, source_target_pairs={{0,64},{64,0},{1,65},{65,1},{2,66},{66,2},{3,67},{67,3},{4,68},{68... | collective-permute-start | bytes 1916936 | tf_op jit(solution)/shard_map/ppermute | solution.py:301
  79.0 2.8 %order_latent.1 = (bf16[1024,512]{1,0:T(8,128)(2,1)S(1)}, bf16[1024,512]{1,0:T(8,128)(2,1)S(1)}, bf16[1024,64]{1,0:T(8,128)(2,1)S(1)}) custom-call(s32[1]{0:T(128)} %bitcast.9.me_ref, bf16[512,512]{1,0:T(8,128)(2,1)S(1)} %bitcast.21, bf16[512,64]{1,0:T(8,128)(2,1)S(1)} %bitcast.20, bf16[128,576]{1,0:T(8,128)(2,1)} %collective-permute-done.10.refs_0_, ...), custom_call_target="tpu_custom_call" | custom-call | flops 1000000000 | bytes 4000000 | tf_op jit(solution)/shard_map/order_latent/pallas_call | solution.py:287
  90.6 12.2 %early.1 = (bf16[512,2048]{1,0:T(8,128)(2,1)}, f32[8,8,128]{2,1,0:T(8,128)S(1)}) custom-call(s32[3]{0:T(128)S(1)} %pad_add_fusion.place_ref, bf16[3,512,512]{2,1,0:T(8,128)(2,1)S(1)} %copy-done.18, bf16[1024,512]{1,0:T(8,128)(2,1)S(1)} %copy-done.12, bf16[1024,64]{1,0:T(8,128)(2,1)S(1)} %copy-done.14, bf16[64,4992]{1,0:T(8,128)(2,1)S(1)} %bitcast.19, ...), custom_call_target="tpu_custom_call" | custom-call | flops 5400000000 | bytes 6000000 | tf_op jit(solution)/shard_map/early/pallas_call | solution.py:151
  105.6 18.0 %late.1 = (bf16[512,2048]{1,0:T(8,128)(2,1)}, f32[8,8,128]{2,1,0:T(8,128)S(1)}) custom-call(s32[3]{0:T(128)S(1)} %pad_add_fusion.place_ref, bf16[3,512,512]{2,1,0:T(8,128)(2,1)S(1)} %copy-done.16, bf16[1024,512]{1,0:T(8,128)(2,1)S(1)} %copy-done.10, bf16[1024,64]{1,0:T(8,128)(2,1)S(1)} %copy-done.14, ...), custom_call_target="tpu_custom_call", output_to_operand_aliasing={{0}: (5, {}), {1}: (6, {})} | custom-call | flops 8999999488 | bytes 10000000 | tf_op jit(solution)/shard_map/late/pallas_call | solution.py:151
  123.8 16.2 %all_to_all.5 = f32[64,1,16]{2,1,0:T(1,128)S(1)} all-to-all(f32[64,1,16]{2,1,0:T(1,128)S(1)} %broadcast_in_dim.12), channel_id=1, replica_groups=mesh['xh'=2,'core'=2,'z'=8,'xl'=2,'tensor'=4] {'xh','core','z','xl'}, dimensions={0} | all-to-all | bytes 8192 | tf_op jit(solution)/shard_map/all_to_all | solution.py:352
  (122 shorter events, 30.8 us)
Async XLA Ops:
  7.2 95.8 %all-gather.2.cloned.1.call-start = ((), (), s32[]{:S(2)}) async-start(), calls=%async_computation.1 | async-start | bytes 9052160 | tf_op jit(solution)/shard_map/all_gather | solution.py:328
  8.8 6.8 %collective-permute-start = (bf16[8,8320]{1,0:T(8,128)(2,1)}, bf16[8,8320]{1,0:T(8,128)(2,1)S(1)}, u32[]{:S(2)}, u32[]{:S(2)}) collective-permute-start(bf16[8,8320]{1,0:T(8,128)(2,1)} %get-tuple-element.29.refs_0_), channel_id=1, source_target_pairs={{0,4},{4,128},{128,132},{132,0},{1,5},{5,129},{129,133},{133,1},{2... | collective-permute-start | bytes 399368 | tf_op jit(solution)/shard_map/ppermute | solution.py:301
  10.9 4.8 %collective-permute-start.1 = (bf16[8,8320]{1,0:T(8,128)(2,1)}, bf16[8,8320]{1,0:T(8,128)(2,1)S(1)}, u32[]{:S(2)}, u32[]{:S(2)}) collective-permute-start(bf16[8,8320]{1,0:T(8,128)(2,1)} %get-tuple-element.29.refs_0_), channel_id=1, source_target_pairs={{0,132},{4,0},{128,4},{132,128},{1,133},{5,1},{129,5},{133,129},{2... | collective-permute-start | bytes 399368 | tf_op jit(solution)/shard_map/ppermute | solution.py:301
  12.2 6.6 %collective-permute-start.2 = (bf16[8,8320]{1,0:T(8,128)(2,1)}, bf16[8,8320]{1,0:T(8,128)(2,1)S(1)}, u32[]{:S(2)}, u32[]{:S(2)}) collective-permute-start(bf16[8,8320]{1,0:T(8,128)(2,1)} %get-tuple-element.29.refs_0_), channel_id=1, source_target_pairs={{0,128},{4,132},{128,0},{132,4},{1,129},{5,133},{129,1},{133,5},{2... | collective-permute-start | bytes 399368 | tf_op jit(solution)/shard_map/ppermute | solution.py:301
  21.4 10.1 %collective-permute-start.3 = (bf16[8,4992]{1,0:T(8,128)(2,1)S(1)}, bf16[8,4992]{1,0:T(8,128)(2,1)S(1)}, u32[]{:S(2)}, u32[]{:S(2)}) collective-permute-start(bf16[8,4992]{1,0:T(8,128)(2,1)S(1)} %copy-done.24), channel_id=1, source_target_pairs={{0,8},{8,16},{16,24},{24,32},{32,40},{40,48},{48,56},{56,0},{1,9},... | collective-permute-start | bytes 239624 | tf_op jit(solution)/shard_map/ppermute | solution.py:301
  24.0 8.3 %collective-permute-start.4 = (bf16[8,4992]{1,0:T(8,128)(2,1)S(1)}, bf16[8,4992]{1,0:T(8,128)(2,1)S(1)}, u32[]{:S(2)}, u32[]{:S(2)}) collective-permute-start(bf16[8,4992]{1,0:T(8,128)(2,1)S(1)} %copy-done.24), channel_id=1, source_target_pairs={{0,56},{8,0},{16,8},{24,16},{32,24},{40,32},{48,40},{56,48},{1,57}... | collective-permute-start | bytes 239624 | tf_op jit(solution)/shard_map/ppermute | solution.py:301
  28.0 7.2 %collective-permute-start.5 = (bf16[8,4992]{1,0:T(8,128)(2,1)S(1)}, bf16[8,4992]{1,0:T(8,128)(2,1)S(1)}, u32[]{:S(2)}, u32[]{:S(2)}) collective-permute-start(bf16[8,4992]{1,0:T(8,128)(2,1)S(1)} %copy-done.24), channel_id=1, source_target_pairs={{0,16},{8,24},{16,32},{24,40},{32,48},{40,56},{48,0},{56,8},{1,17}... | collective-permute-start | bytes 239624 | tf_op jit(solution)/shard_map/ppermute | solution.py:301
  28.0 18.5 %collective-permute-start.10 = (bf16[128,576]{1,0:T(8,128)(2,1)S(1)}, bf16[128,576]{1,0:T(8,128)(2,1)}, u32[]{:S(2)}, u32[]{:S(2)}) collective-permute-start(bf16[128,576]{1,0:T(8,128)(2,1)S(1)} %pad_maximum_fusion), channel_id=1, source_target_pairs={{0,4},{4,8},{8,12},{12,16},{16,20},{20,24},{24,28},{28,32},{32,36}... | collective-permute-start | bytes 442376 | tf_op jit(solution)/shard_map/ppermute | solution.py:301
  28.0 7.9 %collective-permute-start.6 = (bf16[8,4992]{1,0:T(8,128)(2,1)S(1)}, bf16[8,4992]{1,0:T(8,128)(2,1)S(1)}, u32[]{:S(2)}, u32[]{:S(2)}) collective-permute-start(bf16[8,4992]{1,0:T(8,128)(2,1)S(1)} %copy-done.24), channel_id=1, source_target_pairs={{0,48},{8,56},{16,0},{24,8},{32,16},{40,24},{48,32},{56,40},{1,49}... | collective-permute-start | bytes 239624 | tf_op jit(solution)/shard_map/ppermute | solution.py:301
  31.6 7.0 %collective-permute-start.7 = (bf16[8,4992]{1,0:T(8,128)(2,1)S(1)}, bf16[8,4992]{1,0:T(8,128)(2,1)S(1)}, u32[]{:S(2)}, u32[]{:S(2)}) collective-permute-start(bf16[8,4992]{1,0:T(8,128)(2,1)S(1)} %collective-permute-done.3.refs_1_), channel_id=1, source_target_pairs={{0,16},{8,24},{16,32},{24,40},{32,48},{40,56},{48,0},{56,8},{1,17}... | collective-permute-start | bytes 239624 | tf_op jit(solution)/shard_map/ppermute | solution.py:301
  32.3 7.8 %collective-permute-start.8 = (bf16[8,4992]{1,0:T(8,128)(2,1)S(1)}, bf16[8,4992]{1,0:T(8,128)(2,1)S(1)}, u32[]{:S(2)}, u32[]{:S(2)}) collective-permute-start(bf16[8,4992]{1,0:T(8,128)(2,1)S(1)} %collective-permute-done.4.refs_2_), channel_id=1, source_target_pairs={{0,48},{8,56},{16,0},{24,8},{32,16},{40,24},{48,32},{56,40},{1,49}... | collective-permute-start | bytes 239624 | tf_op jit(solution)/shard_map/ppermute | solution.py:301
  35.2 8.7 %collective-permute-start.9 = (bf16[8,4992]{1,0:T(8,128)(2,1)S(1)}, bf16[8,4992]{1,0:T(8,128)(2,1)S(1)}, u32[]{:S(2)}, u32[]{:S(2)}) collective-permute-start(bf16[8,4992]{1,0:T(8,128)(2,1)S(1)} %collective-permute-done.5.refs_3_), channel_id=1, source_target_pairs={{0,16},{8,24},{16,32},{24,40},{32,48},{40,56},{48,0},{56,8},{1,17}... | collective-permute-start | bytes 239624 | tf_op jit(solution)/shard_map/ppermute | solution.py:301
  46.5 15.0 %collective-permute-start.11 = (bf16[64,4992]{1,0:T(8,128)(2,1)}, bf16[64,4992]{1,0:T(8,128)(2,1)S(1)}, u32[]{:S(2)}, u32[]{:S(2)}) collective-permute-start(bf16[64,4992]{1,0:T(8,128)(2,1)} %bitcast.16), channel_id=1, source_target_pairs={{0,4},{4,128},{128,132},{132,0},{1,5},{5,129},{129,133},{133,1},{2... | collective-permute-start | bytes 1916936 | tf_op jit(solution)/shard_map/ppermute | solution.py:301
  48.2 13.3 %collective-permute-start.12 = (bf16[64,4992]{1,0:T(8,128)(2,1)}, bf16[64,4992]{1,0:T(8,128)(2,1)S(1)}, u32[]{:S(2)}, u32[]{:S(2)}) collective-permute-start(bf16[64,4992]{1,0:T(8,128)(2,1)} %bitcast.17), channel_id=1, source_target_pairs={{0,132},{4,0},{128,4},{132,128},{1,133},{5,1},{129,5},{133,129},{2... | collective-permute-start | bytes 1916936 | tf_op jit(solution)/shard_map/ppermute | solution.py:301
  49.8 15.9 %collective-permute-start.15 = (bf16[128,576]{1,0:T(8,128)(2,1)}, bf16[128,576]{1,0:T(8,128)(2,1)S(1)}, u32[]{:S(2)}, u32[]{:S(2)}) collective-permute-start(bf16[128,576]{1,0:T(8,128)(2,1)} %collective-permute-done.10.refs_0_), channel_id=1, source_target_pairs={{0,1},{1,2},{2,3},{3,0},{4,5},{5,6},{6,7},{7,4},{8,9},{9,10},{10,1... | collective-permute-start | bytes 442376 | tf_op jit(solution)/shard_map/ppermute | solution.py:301
  51.1 22.2 %collective-permute-start.16 = (bf16[128,576]{1,0:T(8,128)(2,1)}, bf16[128,576]{1,0:T(8,128)(2,1)S(1)}, u32[]{:S(2)}, u32[]{:S(2)}) collective-permute-start(bf16[128,576]{1,0:T(8,128)(2,1)} %collective-permute-done.10.refs_0_), channel_id=1, source_target_pairs={{0,3},{1,0},{2,1},{3,2},{4,7},{5,4},{6,5},{7,6},{8,11},{9,8},{10,9... | collective-permute-start | bytes 442376 | tf_op jit(solution)/shard_map/ppermute | solution.py:301
  52.8 21.3 %collective-permute-start.17 = (bf16[128,576]{1,0:T(8,128)(2,1)}, bf16[128,576]{1,0:T(8,128)(2,1)S(1)}, u32[]{:S(2)}, u32[]{:S(2)}) collective-permute-start(bf16[128,576]{1,0:T(8,128)(2,1)} %collective-permute-done.10.refs_0_), channel_id=1, source_target_pairs={{0,2},{1,3},{2,0},{3,1},{4,6},{5,7},{6,4},{7,5},{8,10},{9,11},{10,... | collective-permute-start | bytes 442376 | tf_op jit(solution)/shard_map/ppermute | solution.py:301
  62.3 22.3 %collective-permute-start.13 = (bf16[32,4992]{1,0:T(8,128)(2,1)}, bf16[32,4992]{1,0:T(8,128)(2,1)S(1)}, u32[]{:S(2)}, u32[]{:S(2)}) collective-permute-start(bf16[32,4992]{1,0:T(8,128)(2,1)} %slice.9), channel_id=1, source_target_pairs={{0,4},{4,128},{128,132},{132,0},{1,5},{5,129},{129,133},{133,1},{2... | collective-permute-start | bytes 958472 | tf_op jit(solution)/shard_map/ppermute | solution.py:301
  63.0 21.5 %collective-permute-start.14 = (bf16[32,4992]{1,0:T(8,128)(2,1)}, bf16[32,4992]{1,0:T(8,128)(2,1)}, u32[]{:S(2)}, u32[]{:S(2)}) collective-permute-start(bf16[32,4992]{1,0:T(8,128)(2,1)} %slice.10), channel_id=1, source_target_pairs={{0,132},{4,0},{128,4},{132,128},{1,133},{5,1},{129,5},{133,129},{2... | collective-permute-start | bytes 958472 | tf_op jit(solution)/shard_map/ppermute | solution.py:301
  66.4 20.6 %collective-permute-start.18 = (bf16[64,4992]{1,0:T(8,128)(2,1)S(1)}, bf16[64,4992]{1,0:T(8,128)(2,1)S(1)}, u32[]{:S(2)}, u32[]{:S(2)}) collective-permute-start(bf16[64,4992]{1,0:T(8,128)(2,1)S(1)} %bitcast.18), channel_id=1, source_target_pairs={{0,64},{64,0},{1,65},{65,1},{2,66},{66,2},{3,67},{67,3},{4,68},{68... | collective-permute-start | bytes 1916936 | tf_op jit(solution)/shard_map/ppermute | solution.py:301
  74.0 13.0 %collective-permute-start.19 = (bf16[64,4992]{1,0:T(8,128)(2,1)S(1)}, bf16[64,4992]{1,0:T(8,128)(2,1)}, u32[]{:S(2)}, u32[]{:S(2)}) collective-permute-start(bf16[64,4992]{1,0:T(8,128)(2,1)S(1)} %collective-permute-done.11.rest_1_), channel_id=1, source_target_pairs={{0,64},{64,0},{1,65},{65,1},{2,66},{66,2},{3,67},{67,3},{4,68},{68... | collective-permute-start | bytes 1916936 | tf_op jit(solution)/shard_map/ppermute | solution.py:301
  74.7 12.3 %collective-permute-start.20 = (bf16[64,4992]{1,0:T(8,128)(2,1)S(1)}, bf16[64,4992]{1,0:T(8,128)(2,1)}, u32[]{:S(2)}, u32[]{:S(2)}) collective-permute-start(bf16[64,4992]{1,0:T(8,128)(2,1)S(1)} %collective-permute-done.12.rest_2_), channel_id=1, source_target_pairs={{0,64},{64,0},{1,65},{65,1},{2,66},{66,2},{3,67},{67,3},{4,68},{68... | collective-permute-start | bytes 1916936 | tf_op jit(solution)/shard_map/ppermute | solution.py:301
  84.5 2.5 %collective-permute-start.21 = (bf16[32,4992]{1,0:T(8,128)(2,1)S(1)}, bf16[32,4992]{1,0:T(8,128)(2,1)S(1)}, u32[]{:S(2)}, u32[]{:S(2)}) collective-permute-start(bf16[32,4992]{1,0:T(8,128)(2,1)S(1)} %collective-permute-done.13.rest_3_), channel_id=1, source_target_pairs={{0,64},{64,0},{1,65},{65,1},{2,66},{66,2},{3,67},{67,3},{4,68},{68... | collective-permute-start | bytes 958472 | tf_op jit(solution)/shard_map/ppermute | solution.py:301
  84.5 2.5 %collective-permute-start.22 = (bf16[32,4992]{1,0:T(8,128)(2,1)}, bf16[32,4992]{1,0:T(8,128)(2,1)}, u32[]{:S(2)}, u32[]{:S(2)}) collective-permute-start(bf16[32,4992]{1,0:T(8,128)(2,1)} %collective-permute-done.14.rest_4_), channel_id=1, source_target_pairs={{0,64},{64,0},{1,65},{65,1},{2,66},{66,2},{3,67},{67,3},{4,68},{68... | collective-permute-start | bytes 958472 | tf_op jit(solution)/shard_map/ppermute | solution.py:301
  (34 other events, 212.2 us)
Sparse Core Ops, SparseCore 0:
  21.6 63.7 all-gather.1

commit v5 on v4

--- a/solution.py
+++ b/solution.py
@@ -34,7 +34,13 @@
 SMEM = pl.BlockSpec(memory_space=pltpu.SMEM)
 ANY = pl.BlockSpec(memory_space=pl.ANY)
 HBM = pl.BlockSpec(memory_space=pltpu.HBM)
-EARLY_MIB = 24
+
+
+def whole(shape):
+    return pl.BlockSpec(shape, lambda p: (0,) * len(shape))
+
+
+EARLY_MIB = 20
 LATE_MIB = 48
 
 
@@ -151,7 +157,7 @@
     return pl.pallas_call(
         kernel,
         grid=(pairs,),
-        in_specs=[SMEM, VMEM, VMEM, VMEM] + [HBM if len(weights) == 1 else ANY] * len(weights) + [ANY] * len(before),
+        in_specs=[SMEM] + [whole(a.shape) for a in (x, latents, rope)] + [HBM if len(weights) == 1 else ANY] * len(weights) + [ANY] * len(before),
         out_specs=[
             pl.BlockSpec((TOK, PAIR * V_DIM), lambda p: (0, first + p)),
             pl.BlockSpec((1, 8, 128), lambda p: (first + p, 0, 0)),
@@ -193,6 +199,7 @@
             jax.ShapeDtypeStruct((8, PAIRS_A * WIDE), jnp.bfloat16),
             jax.ShapeDtypeStruct((8, PAIRS_B * WIDE), jnp.bfloat16),
         ],
+        compiler_params=pltpu.CompilerParams(vmem_limit_bytes=4 * MIB),
         name="pack",
     )(query_weight, key_weight, value_weight)
 
@@ -212,8 +219,26 @@
         in_specs=[SMEM] + [VMEM] * count,
         out_specs=VMEM,
         out_shape=jax.ShapeDtypeStruct((count, rows, columns), jnp.bfloat16),
+        compiler_params=pltpu.CompilerParams(vmem_limit_bytes=4 * MIB),
         name="in_order",
     )(me.reshape(1), *pieces).reshape(count * rows, columns)
+
+
+def halves_kernel(before_ref, after_ref, low_ref, high_ref):
+    low_ref[...] = before_ref[:32]
+    high_ref[...] = after_ref[32:]
+
+
+def halves(before, after):
+    shape = jax.ShapeDtypeStruct((32, before.shape[1]), before.dtype)
+    return pl.pallas_call(
+        halves_kernel,
+        in_specs=[VMEM] * 2,
+        out_specs=[VMEM] * 2,
+        out_shape=[shape, shape],
+        compiler_params=pltpu.CompilerParams(vmem_limit_bytes=4 * MIB),
+        name="halves",
+    )(before, after)
 
 
 def one_hot(source, first):
@@ -256,10 +281,11 @@
     shape = jax.ShapeDtypeStruct((3, TOK, 512), jnp.bfloat16)
     return pl.pallas_call(
         order_query_kernel,
-        in_specs=[VMEM],
-        out_specs=[VMEM] * 2,
+        grid=(1,),
+        in_specs=[whole(x.shape)],
+        out_specs=[whole(shape.shape)] * 2,
         out_shape=[shape, shape],
-        compiler_params=pltpu.CompilerParams(vmem_limit_bytes=24 * MIB),
+        compiler_params=pltpu.CompilerParams(vmem_limit_bytes=16 * MIB),
         cost_estimate=pl.CostEstimate(flops=2_500_000_000, bytes_accessed=6_000_000, transcendentals=0),
         name="order_query",
     )(x)
@@ -283,17 +309,19 @@
 
 
 def order_latent(me, own, own_rope, pieces):
-    shape = jax.ShapeDtypeStruct((2 * TOK, 512), jnp.bfloat16)
+    operands = (own, own_rope, *pieces)
+    shapes = [jax.ShapeDtypeStruct((2 * TOK, width), jnp.bfloat16) for width in (512, 512, QK_ROPE)]
     return pl.pallas_call(
         order_latent_kernel,
-        in_specs=[SMEM] + [VMEM] * 6,
-        out_specs=[VMEM] * 3,
-        out_shape=[shape, shape, jax.ShapeDtypeStruct((2 * TOK, QK_ROPE), jnp.bfloat16)],
+        grid=(1,),
+        in_specs=[SMEM] + [whole(a.shape) for a in operands],
+        out_specs=[whole(a.shape) for a in shapes],
+        out_shape=shapes,
         scratch_shapes=[pltpu.VMEM((TOK, 512 + QK_ROPE), jnp.bfloat16)],
-        compiler_params=pltpu.CompilerParams(vmem_limit_bytes=24 * MIB),
+        compiler_params=pltpu.CompilerParams(vmem_limit_bytes=16 * MIB),
         cost_estimate=pl.CostEstimate(flops=1_000_000_000, bytes_accessed=4_000_000, transcendentals=0),
         name="order_latent",
-    )(me.reshape(1), own, own_rope, *pieces)
+    )(me.reshape(1), *operands)
 
 
 def moved(block, axes, distance):
@@ -324,7 +352,7 @@
     mine = jnp.concatenate(
         [lax.dynamic_slice_in_dim(a, me_t * quarter, quarter, 0) for a in (latent, rope_own)], axis=1
     )
-    shard_a, mine, packed_b = barrier((shard_a, mine, packed_b))
+    shard_a, mine, packed_b, place, rope_own = barrier((shard_a, mine, packed_b, place, rope_own))
     gathered_a = lax.all_gather(shard_a, ("z", "core"), axis=0, tiled=True)
 
     up, down = moved(packed_b, "z", 1), moved(packed_b, "z", -1)
@@ -338,7 +366,8 @@
     prev = [theirs, moved(theirs, "tensor", 1), moved(theirs, "tensor", -1), moved(theirs, "tensor", 2)]
     x_a, x_b = order_query(query_latent[0])
     before, after, x_a, x_b = barrier((before, after, x_a, x_b))
-    far_low, far_high = moved(before[:32], X, 1), moved(after[32:], X, -1)
+    low, high = halves(before, after)
+    far_low, far_high = moved(low, X, 1), moved(high, X, -1)
     lat_a, lat_b, rope = order_latent(me_t, latent, rope_own, prev)
     far_low, far_high, lat_a, lat_b, rope = barrier((far_low, far_high, lat_a, lat_b, rope))
     mine = [own, before, after, far_low, far_high]

time: 149 us -> 134 us (0.90)
  local copies, waits for them, and re-layouts: 24 us -> 9.54 us
  Pallas kernels: 42.2 us -> 36.2 us
  starting transfers between devices: 38 us -> 41.7 us
  blocking collectives: 16.2 us -> 17.9 us
    unnamed x69 -> x21, local copies, waits for them, and re-layouts: 19.7 us -> 5.96 us
    ppermute x23, starting transfers between devices: 37.9 us -> 41.7 us  [moved(): lax.ppermute(block, axes, [(i, (i + distance) % count) for i in range(cou...]
    pallas_call x2, Pallas kernels: 3.99 us -> 0.9 us  [in_order(): pl.pallas_call(functools.partial(order_kernel, offsets), in_specs=[SMEM]...]
    all_to_all x1, blocking collectives: 16.2 us -> 17.9 us  [local(): lax.all_to_all(jnp.broadcast_to(peaks[None], (everyone, 1, heads)), GROUP...]
    pallas_call x1, Pallas kernels: 1.63 us -> 0.02 us  [pack(): pl.pallas_call(pack_kernel, in_specs=[VMEM] * 3, out_specs=[VMEM] * 2, ou...]
    slice x2 -> x0, local copies, waits for them, and re-layouts: 1.51 us -> none  [local(): far_low, far_high = (moved(before[:32], X, 1), moved(after[32:], X, -1))]
    pallas_call x4 -> x5, Pallas kernels: 36.5 us -> 35.3 us  [the longest x2 29.9 us: attend(): pl.pallas_call(kernel, grid=(pairs,), in_specs=[SMEM] + [whole(a.shape) f...]
  transfers between devices with their start and end apart: 24 -> 24, of which waited for: 4 -> 7; matrix products, arithmetic and copies ran while one was open for 3% -> 3% of each run, Pallas kernels for 14% -> 13%
where the time goes in v5:
time: 134 us; the launch traced here: 133 us
  starting transfers between devices  41.7 us (31%)
  Pallas kernels  36.2 us (27%)
  blocking collectives  17.9 us (13%)
  between operations  15.5 us (12%)
  waiting for transfers between devices  10.8 us (8%)
  local copies, waits for them, and re-layouts  9.54 us (7%)
  other arithmetic  1.53 us (1%)
    ppermute x23, starting transfers between devices, moved(): lax.ppermute(block, axes, [(i, (i + distance) % count) for i in range(cou...  41.7 us
    pallas_call x2, Pallas kernels, attend(): pl.pallas_call(kernel, grid=(pairs,), in_specs=[SMEM] + [whole(a.shape) f...  29.9 us
    all_to_all x1, blocking collectives, local(): lax.all_to_all(jnp.broadcast_to(peaks[None], (everyone, 1, heads)), GROUP...  17.9 us
    ppermute x23, waiting for transfers between devices, moved(): lax.ppermute(block, axes, [(i, (i + distance) % count) for i in range(cou...  10.7 us
    unnamed x21, local copies, waits for them, and re-layouts  5.96 us
    pallas_call x1, Pallas kernels, order_query(): pl.pallas_call(order_query_kernel, grid=(1,), in_specs=[whole(x.shape)],...  3.46 us
  transfers between devices with their start and end apart: 24, of which 7 were waited for; matrix products, arithmetic and copies ran while one was open for 3% of the time, Pallas kernels for 13%

profile of v5, /device:TPU:1, one launch (start us, length us, event | category | flops | bytes accessed | tf_op | source)
XLA Modules:
  0.0 133.2 jit_solution(5481940904848484518)
XLA Ops:
  9.7 2.1 %collective-permute-start = (bf16[8,8320]{1,0:T(8,128)(2,1)S(1)}, bf16[8,8320]{1,0:T(8,128)(2,1)S(1)}, u32[]{:S(2)}, u32[]{:S(2)}) collective-permute-start(bf16[8,8320]{1,0:T(8,128)(2,1)S(1)} %get-tuple-element.33.refs_0_), channel_id=1, source_target_pairs={{0,4},{4,128},{128,132},{132,0},{1,5},{5,129},{129,133},{133,1},{2... | collective-permute-start | bytes 399368 | tf_op jit(solution)/shard_map/ppermute | solution.py:329
  11.8 1.4 %collective-permute-start.1 = (bf16[8,8320]{1,0:T(8,128)(2,1)S(1)}, bf16[8,8320]{1,0:T(8,128)(2,1)S(1)}, u32[]{:S(2)}, u32[]{:S(2)}) collective-permute-start(bf16[8,8320]{1,0:T(8,128)(2,1)S(1)} %get-tuple-element.33.refs_0_), channel_id=1, source_target_pairs={{0,132},{4,0},{128,4},{132,128},{1,133},{5,1},{129,5},{133,129},{2... | collective-permute-start | bytes 399368 | tf_op jit(solution)/shard_map/ppermute | solution.py:329
  13.1 1.6 %collective-permute-start.2 = (bf16[8,8320]{1,0:T(8,128)(2,1)S(1)}, bf16[8,8320]{1,0:T(8,128)(2,1)S(1)}, u32[]{:S(2)}, u32[]{:S(2)}) collective-permute-start(bf16[8,8320]{1,0:T(8,128)(2,1)S(1)} %get-tuple-element.33.refs_0_), channel_id=1, source_target_pairs={{0,128},{4,132},{128,0},{132,4},{1,129},{5,133},{129,1},{133,5},{2... | collective-permute-start | bytes 399368 | tf_op jit(solution)/shard_map/ppermute | solution.py:329
  14.8 1.3 %fusion.1 = (s32[1,1]{1,0:T(1,128)}, s32[1,1]{1,0:T(1,128)}) fusion(s32[4,16]{1,0:T(4,128)} %param.10, s32[]{:T(128)S(6)} %select_n.28, s32[]{:T(128)S(6)} %select_n.33, s32[]{:T(128)S(6)} %select_n.31), kind=kLoop, calls=%fused_computation.11 | loop fusion | bytes 28 | tf_op jit(solution)/shard_map/dynamic_slice | solution.py:340
  21.1 1.8 %collective-permute-start.3 = (bf16[8,4992]{1,0:T(8,128)(2,1)S(1)}, bf16[8,4992]{1,0:T(8,128)(2,1)S(1)}, u32[]{:S(2)}, u32[]{:S(2)}) collective-permute-start(bf16[8,4992]{1,0:T(8,128)(2,1)S(1)} %get-tuple-element.36.refs_0_), channel_id=1, source_target_pairs={{0,8},{8,16},{16,24},{24,32},{32,40},{40,48},{48,56},{56,0},{1,9},... | collective-permute-start | bytes 239624 | tf_op jit(solution)/shard_map/ppermute | solution.py:329
  22.9 4.0 %collective-permute-start.4 = (bf16[8,4992]{1,0:T(8,128)(2,1)S(1)}, bf16[8,4992]{1,0:T(8,128)(2,1)S(1)}, u32[]{:S(2)}, u32[]{:S(2)}) collective-permute-start(bf16[8,4992]{1,0:T(8,128)(2,1)S(1)} %get-tuple-element.36.refs_0_), channel_id=1, source_target_pairs={{0,56},{8,0},{16,8},{24,16},{32,24},{40,32},{48,40},{56,48},{1,57}... | collective-permute-start | bytes 239624 | tf_op jit(solution)/shard_map/ppermute | solution.py:329
  27.1 3.6 %collective-permute-start.6 = (bf16[8,4992]{1,0:T(8,128)(2,1)S(1)}, bf16[8,4992]{1,0:T(8,128)(2,1)S(1)}, u32[]{:S(2)}, u32[]{:S(2)}) collective-permute-start(bf16[8,4992]{1,0:T(8,128)(2,1)S(1)} %get-tuple-element.36.refs_0_), channel_id=1, source_target_pairs={{0,48},{8,56},{16,0},{24,8},{32,16},{40,24},{48,32},{56,40},{1,49}... | collective-permute-start | bytes 239624 | tf_op jit(solution)/shard_map/ppermute | solution.py:329
  31.4 2.9 %collective-permute-start.8 = (bf16[8,4992]{1,0:T(8,128)(2,1)S(1)}, bf16[8,4992]{1,0:T(8,128)(2,1)S(1)}, u32[]{:S(2)}, u32[]{:S(2)}) collective-permute-start(bf16[8,4992]{1,0:T(8,128)(2,1)S(1)} %collective-permute-done.4.refs_2_), channel_id=1, source_target_pairs={{0,48},{8,56},{16,0},{24,8},{32,16},{40,24},{48,32},{56,40},{1,49}... | collective-permute-start | bytes 239624 | tf_op jit(solution)/shard_map/ppermute | solution.py:329
  35.0 2.4 %collective-permute-done.7.refs_5_ = bf16[8,4992]{1,0:T(8,128)(2,1)S(1)} collective-permute-done((bf16[8,4992]{1,0:T(8,128)(2,1)S(1)}, bf16[8,4992]{1,0:T(8,128)(2,1)S(1)}, u32[]{:S(2)}, u32[]{:S(2)}) %collective-permute-start.7) | collective-permute-done | bytes 79904 | tf_op jit(solution)/shard_map/ppermute | solution.py:329
  37.5 2.2 %collective-permute-done.8.refs_6_ = bf16[8,4992]{1,0:T(8,128)(2,1)S(1)} collective-permute-done((bf16[8,4992]{1,0:T(8,128)(2,1)S(1)}, bf16[8,4992]{1,0:T(8,128)(2,1)S(1)}, u32[]{:S(2)}, u32[]{:S(2)}) %collective-permute-start.8) | collective-permute-done | bytes 79904 | tf_op jit(solution)/shard_map/ppermute | solution.py:329
  39.7 3.6 %collective-permute-done.9.refs_7_ = bf16[8,4992]{1,0:T(8,128)(2,1)S(1)} collective-permute-done((bf16[8,4992]{1,0:T(8,128)(2,1)S(1)}, bf16[8,4992]{1,0:T(8,128)(2,1)S(1)}, u32[]{:S(2)}, u32[]{:S(2)}) %collective-permute-start.9) | collective-permute-done | bytes 79904 | tf_op jit(solution)/shard_map/ppermute | solution.py:329
  43.3 2.3 %collective-permute-start.11 = (bf16[64,4992]{1,0:T(8,128)(2,1)S(1)}, bf16[64,4992]{1,0:T(8,128)(2,1)S(1)}, u32[]{:S(2)}, u32[]{:S(2)}) collective-permute-start(bf16[64,4992]{1,0:T(8,128)(2,1)S(1)} %bitcast.16), channel_id=1, source_target_pairs={{0,4},{4,128},{128,132},{132,0},{1,5},{5,129},{129,133},{133,1},{2... | collective-permute-start | bytes 1916936 | tf_op jit(solution)/shard_map/ppermute | solution.py:329
  46.1 1.4 %collective-permute-start.15 = (bf16[128,576]{1,0:T(8,128)(2,1)S(1)}, bf16[128,576]{1,0:T(8,128)(2,1)S(1)}, u32[]{:S(2)}, u32[]{:S(2)}) collective-permute-start(bf16[128,576]{1,0:T(8,128)(2,1)S(1)} %collective-permute-done.10.refs_0_), channel_id=1, source_target_pairs={{0,1},{1,2},{2,3},{3,0},{4,5},{5,6},{6,7},{7,4},{8,9},{9,10},{10,1... | collective-permute-start | bytes 442376 | tf_op jit(solution)/shard_map/ppermute | solution.py:329
  47.5 1.7 %collective-permute-start.16 = (bf16[128,576]{1,0:T(8,128)(2,1)S(1)}, bf16[128,576]{1,0:T(8,128)(2,1)S(1)}, u32[]{:S(2)}, u32[]{:S(2)}) collective-permute-start(bf16[128,576]{1,0:T(8,128)(2,1)S(1)} %collective-permute-done.10.refs_0_), channel_id=1, source_target_pairs={{0,3},{1,0},{2,1},{3,2},{4,7},{5,4},{6,5},{7,6},{8,11},{9,8},{10,9... | collective-permute-start | bytes 442376 | tf_op jit(solution)/shard_map/ppermute | solution.py:329
  49.2 1.5 %collective-permute-start.17 = (bf16[128,576]{1,0:T(8,128)(2,1)S(1)}, bf16[128,576]{1,0:T(8,128)(2,1)S(1)}, u32[]{:S(2)}, u32[]{:S(2)}) collective-permute-start(bf16[128,576]{1,0:T(8,128)(2,1)S(1)} %collective-permute-done.10.refs_0_), channel_id=1, source_target_pairs={{0,2},{1,3},{2,0},{3,1},{4,6},{5,7},{6,4},{7,5},{8,10},{9,11},{10,... | collective-permute-start | bytes 442376 | tf_op jit(solution)/shard_map/ppermute | solution.py:329
  50.7 3.5 %order_query.1 = (bf16[3,512,512]{2,1,0:T(8,128)(2,1)S(1)}, bf16[3,512,512]{2,1,0:T(8,128)(2,1)S(1)}) custom-call(bf16[512,1536]{1,0:T(8,128)(2,1)S(1)} %bitcast.22), custom_call_target="tpu_custom_call" | custom-call | flops 2500000000 | bytes 6000000 | tf_op jit(solution)/shard_map/order_query/pallas_call | solution.py:282
  56.6 2.3 %collective-permute-start.14 = (bf16[32,4992]{1,0:T(8,128)(2,1)S(1)}, bf16[32,4992]{1,0:T(8,128)(2,1)S(1)}, u32[]{:S(2)}, u32[]{:S(2)}) collective-permute-start(bf16[32,4992]{1,0:T(8,128)(2,1)S(1)} %get-tuple-element.45), channel_id=1, source_target_pairs={{0,132},{4,0},{128,4},{132,128},{1,133},{5,1},{129,5},{133,129},{2... | collective-permute-start | bytes 958472 | tf_op jit(solution)/shard_map/ppermute | solution.py:329
  58.9 9.5 %collective-permute-start.18 = (bf16[64,4992]{1,0:T(8,128)(2,1)S(1)}, bf16[64,4992]{1,0:T(8,128)(2,1)S(1)}, u32[]{:S(2)}, u32[]{:S(2)}) collective-permute-start(bf16[64,4992]{1,0:T(8,128)(2,1)S(1)} %bitcast.18), channel_id=1, source_target_pairs={{0,64},{64,0},{1,65},{65,1},{2,66},{66,2},{3,67},{67,3},{4,68},{68... | collective-permute-start | bytes 1916936 | tf_op jit(solution)/shard_map/ppermute | solution.py:329
  68.9 1.9 %order_latent.1 = (bf16[1024,512]{1,0:T(8,128)(2,1)S(1)}, bf16[1024,512]{1,0:T(8,128)(2,1)S(1)}, bf16[1024,64]{1,0:T(8,128)(2,1)S(1)}) custom-call(s32[1]{0:T(128)} %bitcast.10.me_ref, bf16[512,512]{1,0:T(8,128)(2,1)S(1)} %bitcast.21, bf16[512,64]{1,0:T(8,128)(2,1)S(1)} %bitcast.20, bf16[128,576]{1,0:T(8,128)(2,1)S(1)} %collective-permute-done.10.refs_0_, ...), custom_call_target="tpu_custom_call" | custom-call | flops 1000000000 | bytes 4000000 | tf_op jit(solution)/shard_map/order_latent/pallas_call | solution.py:314
  70.8 2.5 %collective-permute-start.21 = (bf16[32,4992]{1,0:T(8,128)(2,1)S(1)}, bf16[32,4992]{1,0:T(8,128)(2,1)S(1)}, u32[]{:S(2)}, u32[]{:S(2)}) collective-permute-start(bf16[32,4992]{1,0:T(8,128)(2,1)S(1)} %collective-permute-done.13.rest_3_), channel_id=1, source_target_pairs={{0,64},{64,0},{1,65},{65,1},{2,66},{66,2},{3,67},{67,3},{4,68},{68... | collective-permute-start | bytes 958472 | tf_op jit(solution)/shard_map/ppermute | solution.py:329
  75.1 11.9 %early.1 = (bf16[512,2048]{1,0:T(8,128)(2,1)}, f32[8,8,128]{2,1,0:T(8,128)S(1)}) custom-call(s32[3]{0:T(128)S(1)} %pad_add_fusion.place_ref, bf16[3,512,512]{2,1,0:T(8,128)(2,1)S(1)} %get-tuple-element.54.x_ref, bf16[1024,512]{1,0:T(8,128)(2,1)S(1)} %get-tuple-element.55.lat_ref, bf16[1024,64]{1,0:T(8,128)(2,1)S(1)} %get-tuple-element.52.rope_ref, ...), custom_call_target="tpu_custom_call" | custom-call | flops 5400000000 | bytes 6000000 | tf_op jit(solution)/shard_map/early/pallas_call | solution.py:157
  87.0 1.4 %copy-done.8 = bf16[3,512,512]{2,1,0:T(8,128)(2,1)S(1)} copy-done((bf16[3,512,512]{2,1,0:T(8,128)(2,1)S(1)}, bf16[3,512,512]{2,1,0:T(8,128)(2,1)}, u32[]{:S(2)}) %copy-start.8) | copy-done | bytes 1572888
  88.4 18.0 %late.1 = (bf16[512,2048]{1,0:T(8,128)(2,1)}, f32[8,8,128]{2,1,0:T(8,128)S(1)}) custom-call(s32[3]{0:T(128)S(1)} %pad_add_fusion.place_ref, bf16[3,512,512]{2,1,0:T(8,128)(2,1)S(1)} %copy-done.8, bf16[1024,512]{1,0:T(8,128)(2,1)S(1)} %get-tuple-element.51.lat_ref, ...), custom_call_target="tpu_custom_call", output_to_operand_aliasing={{0}: (5, {}), {1}: (6, {})} | custom-call | flops 8999999488 | bytes 10000000 | tf_op jit(solution)/shard_map/late/pallas_call | solution.py:157
  106.6 17.9 %all_to_all.5 = f32[64,1,16]{2,1,0:T(1,128)S(1)} all-to-all(f32[64,1,16]{2,1,0:T(1,128)S(1)} %broadcast_in_dim.12), channel_id=1, replica_groups=mesh['xh'=2,'core'=2,'z'=8,'xl'=2,'tensor'=4] {'xh','core','z','xl'}, dimensions={0} | all-to-all | bytes 8192 | tf_op jit(solution)/shard_map/all_to_all | solution.py:381
  (73 shorter events, 14.9 us)
Async XLA Ops:
  7.2 79.8 %all-gather.2.cloned.1.call-start = ((), (), s32[]{:S(2)}) async-start(), calls=%async_computation.1 | async-start | bytes 9052160 | tf_op jit(solution)/shard_map/all_gather | solution.py:356
  9.7 10.5 %collective-permute-start = (bf16[8,8320]{1,0:T(8,128)(2,1)S(1)}, bf16[8,8320]{1,0:T(8,128)(2,1)S(1)}, u32[]{:S(2)}, u32[]{:S(2)}) collective-permute-start(bf16[8,8320]{1,0:T(8,128)(2,1)S(1)} %get-tuple-element.33.refs_0_), channel_id=1, source_target_pairs={{0,4},{4,128},{128,132},{132,0},{1,5},{5,129},{129,133},{133,1},{2... | collective-permute-start | bytes 399368 | tf_op jit(solution)/shard_map/ppermute | solution.py:329
  11.8 8.4 %collective-permute-start.1 = (bf16[8,8320]{1,0:T(8,128)(2,1)S(1)}, bf16[8,8320]{1,0:T(8,128)(2,1)S(1)}, u32[]{:S(2)}, u32[]{:S(2)}) collective-permute-start(bf16[8,8320]{1,0:T(8,128)(2,1)S(1)} %get-tuple-element.33.refs_0_), channel_id=1, source_target_pairs={{0,132},{4,0},{128,4},{132,128},{1,133},{5,1},{129,5},{133,129},{2... | collective-permute-start | bytes 399368 | tf_op jit(solution)/shard_map/ppermute | solution.py:329
  13.1 7.1 %collective-permute-start.2 = (bf16[8,8320]{1,0:T(8,128)(2,1)S(1)}, bf16[8,8320]{1,0:T(8,128)(2,1)S(1)}, u32[]{:S(2)}, u32[]{:S(2)}) collective-permute-start(bf16[8,8320]{1,0:T(8,128)(2,1)S(1)} %get-tuple-element.33.refs_0_), channel_id=1, source_target_pairs={{0,128},{4,132},{128,0},{132,4},{1,129},{5,133},{129,1},{133,5},{2... | collective-permute-start | bytes 399368 | tf_op jit(solution)/shard_map/ppermute | solution.py:329
  21.1 9.6 %collective-permute-start.3 = (bf16[8,4992]{1,0:T(8,128)(2,1)S(1)}, bf16[8,4992]{1,0:T(8,128)(2,1)S(1)}, u32[]{:S(2)}, u32[]{:S(2)}) collective-permute-start(bf16[8,4992]{1,0:T(8,128)(2,1)S(1)} %get-tuple-element.36.refs_0_), channel_id=1, source_target_pairs={{0,8},{8,16},{16,24},{24,32},{32,40},{40,48},{48,56},{56,0},{1,9},... | collective-permute-start | bytes 239624 | tf_op jit(solution)/shard_map/ppermute | solution.py:329
  22.9 8.5 %collective-permute-start.4 = (bf16[8,4992]{1,0:T(8,128)(2,1)S(1)}, bf16[8,4992]{1,0:T(8,128)(2,1)S(1)}, u32[]{:S(2)}, u32[]{:S(2)}) collective-permute-start(bf16[8,4992]{1,0:T(8,128)(2,1)S(1)} %get-tuple-element.36.refs_0_), channel_id=1, source_target_pairs={{0,56},{8,0},{16,8},{24,16},{32,24},{40,32},{48,40},{56,48},{1,57}... | collective-permute-start | bytes 239624 | tf_op jit(solution)/shard_map/ppermute | solution.py:329
  26.9 7.4 %collective-permute-start.5 = (bf16[8,4992]{1,0:T(8,128)(2,1)S(1)}, bf16[8,4992]{1,0:T(8,128)(2,1)S(1)}, u32[]{:S(2)}, u32[]{:S(2)}) collective-permute-start(bf16[8,4992]{1,0:T(8,128)(2,1)S(1)} %get-tuple-element.36.refs_0_), channel_id=1, source_target_pairs={{0,16},{8,24},{16,32},{24,40},{32,48},{40,56},{48,0},{56,8},{1,17}... | collective-permute-start | bytes 239624 | tf_op jit(solution)/shard_map/ppermute | solution.py:329
  26.9 16.4 %collective-permute-start.10 = (bf16[128,576]{1,0:T(8,128)(2,1)S(1)}, bf16[128,576]{1,0:T(8,128)(2,1)S(1)}, u32[]{:S(2)}, u32[]{:S(2)}) collective-permute-start(bf16[128,576]{1,0:T(8,128)(2,1)S(1)} %pad_maximum_fusion), channel_id=1, source_target_pairs={{0,4},{4,8},{8,12},{12,16},{16,20},{20,24},{24,28},{28,32},{32,36}... | collective-permute-start | bytes 442376 | tf_op jit(solution)/shard_map/ppermute | solution.py:329
  27.1 7.9 %collective-permute-start.6 = (bf16[8,4992]{1,0:T(8,128)(2,1)S(1)}, bf16[8,4992]{1,0:T(8,128)(2,1)S(1)}, u32[]{:S(2)}, u32[]{:S(2)}) collective-permute-start(bf16[8,4992]{1,0:T(8,128)(2,1)S(1)} %get-tuple-element.36.refs_0_), channel_id=1, source_target_pairs={{0,48},{8,56},{16,0},{24,8},{32,16},{40,24},{48,32},{56,40},{1,49}... | collective-permute-start | bytes 239624 | tf_op jit(solution)/shard_map/ppermute | solution.py:329
  30.7 6.7 %collective-permute-start.7 = (bf16[8,4992]{1,0:T(8,128)(2,1)S(1)}, bf16[8,4992]{1,0:T(8,128)(2,1)S(1)}, u32[]{:S(2)}, u32[]{:S(2)}) collective-permute-start(bf16[8,4992]{1,0:T(8,128)(2,1)S(1)} %collective-permute-done.3.refs_1_), channel_id=1, source_target_pairs={{0,16},{8,24},{16,32},{24,40},{32,48},{40,56},{48,0},{56,8},{1,17}... | collective-permute-start | bytes 239624 | tf_op jit(solution)/shard_map/ppermute | solution.py:329
  31.4 8.3 %collective-permute-start.8 = (bf16[8,4992]{1,0:T(8,128)(2,1)S(1)}, bf16[8,4992]{1,0:T(8,128)(2,1)S(1)}, u32[]{:S(2)}, u32[]{:S(2)}) collective-permute-start(bf16[8,4992]{1,0:T(8,128)(2,1)S(1)} %collective-permute-done.4.refs_2_), channel_id=1, source_target_pairs={{0,48},{8,56},{16,0},{24,8},{32,16},{40,24},{48,32},{56,40},{1,49}... | collective-permute-start | bytes 239624 | tf_op jit(solution)/shard_map/ppermute | solution.py:329
  34.3 8.9 %collective-permute-start.9 = (bf16[8,4992]{1,0:T(8,128)(2,1)S(1)}, bf16[8,4992]{1,0:T(8,128)(2,1)S(1)}, u32[]{:S(2)}, u32[]{:S(2)}) collective-permute-start(bf16[8,4992]{1,0:T(8,128)(2,1)S(1)} %collective-permute-done.5.refs_3_), channel_id=1, source_target_pairs={{0,16},{8,24},{16,32},{24,40},{32,48},{40,56},{48,0},{56,8},{1,17}... | collective-permute-start | bytes 239624 | tf_op jit(solution)/shard_map/ppermute | solution.py:329
  43.3 12.5 %collective-permute-start.11 = (bf16[64,4992]{1,0:T(8,128)(2,1)S(1)}, bf16[64,4992]{1,0:T(8,128)(2,1)S(1)}, u32[]{:S(2)}, u32[]{:S(2)}) collective-permute-start(bf16[64,4992]{1,0:T(8,128)(2,1)S(1)} %bitcast.16), channel_id=1, source_target_pairs={{0,4},{4,128},{128,132},{132,0},{1,5},{5,129},{129,133},{133,1},{2... | collective-permute-start | bytes 1916936 | tf_op jit(solution)/shard_map/ppermute | solution.py:329
  45.6 10.5 %collective-permute-start.12 = (bf16[64,4992]{1,0:T(8,128)(2,1)S(1)}, bf16[64,4992]{1,0:T(8,128)(2,1)S(1)}, u32[]{:S(2)}, u32[]{:S(2)}) collective-permute-start(bf16[64,4992]{1,0:T(8,128)(2,1)S(1)} %bitcast.17), channel_id=1, source_target_pairs={{0,132},{4,0},{128,4},{132,128},{1,133},{5,1},{129,5},{133,129},{2... | collective-permute-start | bytes 1916936 | tf_op jit(solution)/shard_map/ppermute | solution.py:329
  46.1 12.8 %collective-permute-start.15 = (bf16[128,576]{1,0:T(8,128)(2,1)S(1)}, bf16[128,576]{1,0:T(8,128)(2,1)S(1)}, u32[]{:S(2)}, u32[]{:S(2)}) collective-permute-start(bf16[128,576]{1,0:T(8,128)(2,1)S(1)} %collective-permute-done.10.refs_0_), channel_id=1, source_target_pairs={{0,1},{1,2},{2,3},{3,0},{4,5},{5,6},{6,7},{7,4},{8,9},{9,10},{10,1... | collective-permute-start | bytes 442376 | tf_op jit(solution)/shard_map/ppermute | solution.py:329
  47.5 20.9 %collective-permute-start.16 = (bf16[128,576]{1,0:T(8,128)(2,1)S(1)}, bf16[128,576]{1,0:T(8,128)(2,1)S(1)}, u32[]{:S(2)}, u32[]{:S(2)}) collective-permute-start(bf16[128,576]{1,0:T(8,128)(2,1)S(1)} %collective-permute-done.10.refs_0_), channel_id=1, source_target_pairs={{0,3},{1,0},{2,1},{3,2},{4,7},{5,4},{6,5},{7,6},{8,11},{9,8},{10,9... | collective-permute-start | bytes 442376 | tf_op jit(solution)/shard_map/ppermute | solution.py:329
  49.2 19.3 %collective-permute-start.17 = (bf16[128,576]{1,0:T(8,128)(2,1)S(1)}, bf16[128,576]{1,0:T(8,128)(2,1)S(1)}, u32[]{:S(2)}, u32[]{:S(2)}) collective-permute-start(bf16[128,576]{1,0:T(8,128)(2,1)S(1)} %collective-permute-done.10.refs_0_), channel_id=1, source_target_pairs={{0,2},{1,3},{2,0},{3,1},{4,6},{5,7},{6,4},{7,5},{8,10},{9,11},{10,... | collective-permute-start | bytes 442376 | tf_op jit(solution)/shard_map/ppermute | solution.py:329
  56.1 14.7 %collective-permute-start.13 = (bf16[32,4992]{1,0:T(8,128)(2,1)S(1)}, bf16[32,4992]{1,0:T(8,128)(2,1)S(1)}, u32[]{:S(2)}, u32[]{:S(2)}) collective-permute-start(bf16[32,4992]{1,0:T(8,128)(2,1)S(1)} %get-tuple-element.44), channel_id=1, source_target_pairs={{0,4},{4,128},{128,132},{132,0},{1,5},{5,129},{129,133},{133,1},{2... | collective-permute-start | bytes 958472 | tf_op jit(solution)/shard_map/ppermute | solution.py:329
  56.6 14.3 %collective-permute-start.14 = (bf16[32,4992]{1,0:T(8,128)(2,1)S(1)}, bf16[32,4992]{1,0:T(8,128)(2,1)S(1)}, u32[]{:S(2)}, u32[]{:S(2)}) collective-permute-start(bf16[32,4992]{1,0:T(8,128)(2,1)S(1)} %get-tuple-element.45), channel_id=1, source_target_pairs={{0,132},{4,0},{128,4},{132,128},{1,133},{5,1},{129,5},{133,129},{2... | collective-permute-start | bytes 958472 | tf_op jit(solution)/shard_map/ppermute | solution.py:329
  58.9 14.5 %collective-permute-start.18 = (bf16[64,4992]{1,0:T(8,128)(2,1)S(1)}, bf16[64,4992]{1,0:T(8,128)(2,1)S(1)}, u32[]{:S(2)}, u32[]{:S(2)}) collective-permute-start(bf16[64,4992]{1,0:T(8,128)(2,1)S(1)} %bitcast.18), channel_id=1, source_target_pairs={{0,64},{64,0},{1,65},{65,1},{2,66},{66,2},{3,67},{67,3},{4,68},{68... | collective-permute-start | bytes 1916936 | tf_op jit(solution)/shard_map/ppermute | solution.py:329
  68.4 5.0 %collective-permute-start.19 = (bf16[64,4992]{1,0:T(8,128)(2,1)S(1)}, bf16[64,4992]{1,0:T(8,128)(2,1)S(1)}, u32[]{:S(2)}, u32[]{:S(2)}) collective-permute-start(bf16[64,4992]{1,0:T(8,128)(2,1)S(1)} %collective-permute-done.11.before_ref.rest_1_), channel_id=1, source_target_pairs={{0,64},{64,0},{1,65},{65,1},{2,66},{66,2},{3,67},{67,3},{4,68},{68... | collective-permute-start | bytes 1916936 | tf_op jit(solution)/shard_map/ppermute | solution.py:329
  68.5 4.9 %collective-permute-start.20 = (bf16[64,4992]{1,0:T(8,128)(2,1)S(1)}, bf16[64,4992]{1,0:T(8,128)(2,1)S(1)}, u32[]{:S(2)}, u32[]{:S(2)}) collective-permute-start(bf16[64,4992]{1,0:T(8,128)(2,1)S(1)} %collective-permute-done.12.after_ref.rest_2_), channel_id=1, source_target_pairs={{0,64},{64,0},{1,65},{65,1},{2,66},{66,2},{3,67},{67,3},{4,68},{68... | collective-permute-start | bytes 1916936 | tf_op jit(solution)/shard_map/ppermute | solution.py:329
  70.8 3.7 %collective-permute-start.21 = (bf16[32,4992]{1,0:T(8,128)(2,1)S(1)}, bf16[32,4992]{1,0:T(8,128)(2,1)S(1)}, u32[]{:S(2)}, u32[]{:S(2)}) collective-permute-start(bf16[32,4992]{1,0:T(8,128)(2,1)S(1)} %collective-permute-done.13.rest_3_), channel_id=1, source_target_pairs={{0,64},{64,0},{1,65},{65,1},{2,66},{66,2},{3,67},{67,3},{4,68},{68... | collective-permute-start | bytes 958472 | tf_op jit(solution)/shard_map/ppermute | solution.py:329
  73.3 1.8 %collective-permute-start.22 = (bf16[32,4992]{1,0:T(8,128)(2,1)S(1)}, bf16[32,4992]{1,0:T(8,128)(2,1)S(1)}, u32[]{:S(2)}, u32[]{:S(2)}) collective-permute-start(bf16[32,4992]{1,0:T(8,128)(2,1)S(1)} %collective-permute-done.14.rest_4_), channel_id=1, source_target_pairs={{0,64},{64,0},{1,65},{65,1},{2,66},{66,2},{3,67},{67,3},{4,68},{68... | collective-permute-start | bytes 958472 | tf_op jit(solution)/shard_map/ppermute | solution.py:329
  (10 other events, 139.8 us)
Sparse Core Ops, SparseCore 0:
  21.2 62.9 all-gather.1
